TPU v7x, 32 devices: a whole 2x2x4 slice. The times are simulated.
32 devices in a mesh: lat: 8 (over z, y), lon: 4 (over x, core).
Axes of the slice: x: 2, y: 2, z: 4, core: 2. Of those that a mesh axis runs over, the one named last changes fastest.
Arguments:
- grid_in: float32 [8192, 512], P(('lat', 'lon')), may hold values from -6 to 6
- target: float32 [8192, 128], P(('lat', 'lon')), may hold values from -6 to 6
- w_enc: float32 [512, 512], replicated, may hold values from -0.25 to 0.25
- w_mix_self: float32 [2, 512, 512], replicated, may hold values from -0.25 to 0.25
- w_mix_nbr: float32 [2, 512, 512], replicated, may hold values from -0.25 to 0.25
- w_dec: float32 [512, 512], replicated, may hold values from -0.25 to 0.25
- w_out: float32 [512, 128], replicated, may hold values from -0.25 to 0.25
- var_weight: int32 [128], replicated, may hold values from 1 to 8
- g2m_idx: int32 [1024, 8], P(('lat', 'lon')), may hold values from 0 to 511, as said below
- g2m_w: float32 [1024, 8], P(('lat', 'lon')), may hold values from 0.1 to 1
- mesh_nbr: int32 [1024, 6], P(('lat', 'lon')), may hold values from 0 to 1023, as said below
- m2g_idx: int32 [8192, 4], P(('lat', 'lon')), may hold values from 0 to 1023, as said below
- m2g_w: float32 [8192, 4], P(('lat', 'lon')), may hold values from 0.1 to 1
Outputs:
- pred: float32 [8192, 128], P(('lat', 'lon'))
- loss: float32 [], replicated
- grad_out: float32 [512, 128], replicated
Inputs may be any that keep to these rules, and one draw needn't show every extreme that they name: `g2m_idx`: an entry of row r names a block held by a device whose lat index differs by at most one from that of the device holding row r, and whose lon index differs by at most one, counted cyclically over the 4 tiles; blocks of device d are rows d * 16 onward. `mesh_nbr`: an entry of row r names a mesh node held by a device whose lat index differs by at most one from that of the device holding row r, and whose lon index differs by at most one, counted cyclically over the 4 tiles. `m2g_idx`: an entry of row r names a mesh node held by a device whose lat index differs by at most one from that of the device holding row r, and whose lon index differs by at most one, counted cyclically over the 4 tiles.
All inputs are finite; a program needn't handle non-finite values.
Results may differ from a plain program's by a relative error of at most 0.00028.
Values sent between devices are 32-bit elements; how exact they have to be, the bound alone decides.
No kernel may reach another device: no remote copies, remote signals or barrier semaphores. Data moves between devices by JAX's collectives and lax.ppermute only.
A program may use at most 64 MiB of HBM per device.

v0:
```python
import jax
import jax.numpy as jnp
from jax import lax
from jax.sharding import PartitionSpec as P

BS = 16
L = 2


def padded(block, sides, width, periodic):
    for axis, dim in sides:
        count = lax.axis_size(axis)
        forward = [(i, i + 1) for i in range(count - 1)]
        if periodic:
            forward.append((count - 1, 0))
        backward = [(target, source) for source, target in forward]
        low = lax.ppermute(
            lax.slice_in_dim(block, block.shape[dim] - width, None, axis=dim), axis, forward
        )
        high = lax.ppermute(lax.slice_in_dim(block, 0, width, axis=dim), axis, backward)
        block = jnp.concatenate([low, block, high], axis=dim)
    return block


def silu(value):
    return value / (1.0 + jnp.exp(-value))


def matmul(left, right):
    return jnp.dot(left, right, precision=lax.Precision.HIGHEST, preferred_element_type=jnp.float32)


def band_window(table):
    shard_rows = table.shape[0]
    width = table.shape[1]
    n_tiles = lax.axis_size("lon")
    band = lax.axis_index("lat")
    tile = lax.axis_index("lon")
    stacked = table.reshape(1, 1, shard_rows, width)
    three_tiles = padded(stacked, (("lon", 1),), 1, True)
    square = padded(three_tiles, (("lat", 0),), 1, False)
    window = square.reshape(9 * shard_rows, width)

    def locate(index):
        owner = index // shard_rows
        within = index % shard_rows
        src_band = owner // n_tiles
        src_tile = owner % n_tiles
        band_slot = src_band - band + 1
        tile_slot = (src_tile - tile + 1 + n_tiles) % n_tiles
        return (band_slot * 3 + tile_slot) * shard_rows + within

    return (window, locate)


def interp(table, index, weights):
    window, locate = band_window(table)
    local = locate(index)
    rows = jnp.take(window, local.reshape(-1), axis=0).reshape(
        index.shape[0], index.shape[1], table.shape[1]
    )
    total = jnp.einsum("rk,rkd->rd", weights, rows, precision=lax.Precision.HIGHEST)
    return total / jnp.sum(weights, axis=1, keepdims=True)


def mixing(mesh, mesh_nbr, self_weight, nbr_weight):
    window, locate = band_window(mesh)
    local = locate(mesh_nbr)
    rows = jnp.take(window, local.reshape(-1), axis=0).reshape(
        mesh_nbr.shape[0], mesh_nbr.shape[1], mesh.shape[1]
    )
    agg = jnp.sum(rows, axis=1) / mesh_nbr.shape[1]
    center = mesh - jnp.mean(mesh, axis=1, keepdims=True)
    nrm = center / jnp.sqrt(jnp.mean(center * center, axis=1, keepdims=True) + 1e-05)
    return mesh + silu(matmul(nrm, self_weight) + matmul(agg, nbr_weight))


def shards(
    grid_in,
    target,
    w_enc,
    w_mix_self,
    w_mix_nbr,
    w_dec,
    w_out,
    var_weight,
    g2m_idx,
    g2m_w,
    mesh_nbr,
    m2g_idx,
    m2g_w,
):
    width = grid_in.shape[1]
    h_one = grid_in + silu(matmul(grid_in, w_enc))
    blocks = jnp.mean(h_one.reshape(-1, BS, width), axis=1)
    mesh = interp(blocks, g2m_idx, g2m_w)
    for layer in range(L):
        mesh = mixing(mesh, mesh_nbr, w_mix_self[layer], w_mix_nbr[layer])
    back = interp(mesh, m2g_idx, m2g_w)
    hidden = silu(matmul(h_one + back, w_dec))
    pred = matmul(hidden, w_out)
    resid = pred - target
    power_part = jnp.sum(target * target, axis=0)
    err_part = jnp.sum(resid * resid, axis=0)
    weights = var_weight.astype(jnp.float32)
    wsum = jnp.sum(weights)
    grid_total = grid_in.shape[0] * lax.axis_size("lat") * lax.axis_size("lon")
    power = lax.psum(power_part, ("lat", "lon"))
    scale = power / grid_total + 1e-06
    coef = 2.0 * weights / (scale * grid_total * wsum)
    grad_part = matmul(hidden.T, resid * coef[None, :])
    err, grad_out = lax.psum((err_part, grad_part), ("lat", "lon"))
    loss = jnp.sum(weights * err / (scale * grid_total * wsum))
    return (pred, loss, grad_out)


def solution(mesh):
    placed = (
        P(("lat", "lon"), None),
        P(("lat", "lon"), None),
        P(),
        P(),
        P(),
        P(),
        P(),
        P(),
        P(("lat", "lon"), None),
        P(("lat", "lon"), None),
        P(("lat", "lon"), None),
        P(("lat", "lon"), None),
        P(("lat", "lon"), None),
    )
    return jax.shard_map(
        shards,
        mesh=mesh,
        in_specs=placed,
        out_specs=(P(("lat", "lon"), None), P(), P()),
        check_vma=False,
    )
```

profile of v0, /device:TPU:0, one launch (start us, length us, event | category | flops | bytes accessed | tf_op | source)
XLA Modules:
  0.0 289.6 jit_solution(15733373557463484798)
XLA Ops:
  8.4 3.3 %bitcast_reduce_fusion = (f32[16,512]{1,0:T(8,128)S(1)}, f32[256,512]{1,0:T(8,128)}) fusion(f32[256,512]{1,0:T(8,128)} %param.15, f32[512,512]{1,0:T(8,128)S(1)} %copy-done), kind=kOutput, calls=%fused_computation.28 | convolution fusion | flops 805953536 | bytes 2129920 | tf_op jit(solution)/shard_map/dot_general | solution.py:30
  12.1 2.0 collective-permute-start.1
  16.6 4.2 %collective-permute-start.2 = (f32[1,3,16,512]{3,2,1,0:T(8,128)S(1)}, f32[1,3,16,512]{3,2,1,0:T(8,128)S(1)}, u32[]{:S(2)}, u32[]{:S(2)}) collective-permute-start(f32[1,3,16,512]{3,2,1,0:T(8,128)S(1)} %pad_maximum_fusion.7), channel_id=1, source_target_pairs={{0,4},{4,8},{8,12},{12,16},{16,20},{20,24},{24,28},{1,5},{5,9},{9,... | collective-permute-start | bytes 294920 | tf_op jit(solution)/shard_map/ppermute | solution.py:17
  23.7 4.1 %collective-permute-done.3 = f32[1,3,16,512]{3,2,1,0:T(8,128)S(1)} collective-permute-done((f32[1,3,16,512]{3,2,1,0:T(8,128)S(1)}, f32[1,3,16,512]{3,2,1,0:T(8,128)S(1)}, u32[]{:S(2)}, u32[]{:S(2)}) %collective-permute-start.3) | collective-permute-done | bytes 98336 | tf_op jit(solution)/shard_map/ppermute | solution.py:20
  29.9 1.7 collective-permute-start.5
  31.7 1.9 collective-permute-done.4
  33.6 4.3 %collective-permute-start.6 = (f32[1,3,32,512]{3,2,1,0:T(8,128)S(1)}, f32[1,3,32,512]{3,2,1,0:T(8,128)S(1)}, u32[]{:S(2)}, u32[]{:S(2)}) collective-permute-start(f32[1,3,32,512]{3,2,1,0:T(8,128)S(1)} %pad_maximum_fusion.4), channel_id=1, source_target_pairs={{0,4},{4,8},{8,12},{12,16},{16,20},{20,24},{24,28},{1,5},{5,9},{9,... | collective-permute-start | bytes 589832 | tf_op jit(solution)/shard_map/ppermute | solution.py:17
  39.3 2.0 fusion.6
  41.2 5.9 %collective-permute-done.6 = f32[1,3,32,512]{3,2,1,0:T(8,128)S(1)} collective-permute-done((f32[1,3,32,512]{3,2,1,0:T(8,128)S(1)}, f32[1,3,32,512]{3,2,1,0:T(8,128)S(1)}, u32[]{:S(2)}, u32[]{:S(2)}) %collective-permute-start.6) | collective-permute-done | bytes 196640 | tf_op jit(solution)/shard_map/ppermute | solution.py:17
  47.6 1.6 gather_fusion.2
  49.2 2.0 broadcast_select_fusion.1
  51.2 1.8 reshape.174
  55.2 1.7 collective-permute-start.9
  57.1 1.7 collective-permute-done.8
  58.8 4.1 %collective-permute-start.10 = (f32[1,3,32,512]{3,2,1,0:T(8,128)S(1)}, f32[1,3,32,512]{3,2,1,0:T(8,128)S(1)}, u32[]{:S(2)}, u32[]{:S(2)}) collective-permute-start(f32[1,3,32,512]{3,2,1,0:T(8,128)S(1)} %pad_maximum_fusion.5), channel_id=1, source_target_pairs={{0,4},{4,8},{8,12},{12,16},{16,20},{20,24},{24,28},{1,5},{5,9},{9,... | collective-permute-start | bytes 589832 | tf_op jit(solution)/shard_map/ppermute | solution.py:17
  64.3 2.0 fusion.3
  66.3 1.8 collective-permute-done.10
  68.1 4.5 %collective-permute-done.11 = f32[1,3,32,512]{3,2,1,0:T(8,128)S(1)} collective-permute-done((f32[1,3,32,512]{3,2,1,0:T(8,128)S(1)}, f32[1,3,32,512]{3,2,1,0:T(8,128)S(1)}, u32[]{:S(2)}, u32[]{:S(2)}) %collective-permute-start.11) | collective-permute-done | bytes 196640 | tf_op jit(solution)/shard_map/ppermute | solution.py:20
  72.6 1.6 gather_fusion.3
  74.2 2.0 broadcast_select_fusion
  76.2 1.8 reshape.177
  80.1 1.7 collective-permute-start.13
  83.8 4.5 %collective-permute-start.14 = (f32[1,3,32,512]{3,2,1,0:T(8,128)S(1)}, f32[1,3,32,512]{3,2,1,0:T(8,128)S(1)}, u32[]{:S(2)}, u32[]{:S(2)}) collective-permute-start(f32[1,3,32,512]{3,2,1,0:T(8,128)S(1)} %pad_maximum_fusion.6), channel_id=1, source_target_pairs={{0,4},{4,8},{8,12},{12,16},{16,20},{20,24},{24,28},{1,5},{5,9},{9,... | collective-permute-start | bytes 589832 | tf_op jit(solution)/shard_map/ppermute | solution.py:17
  89.8 3.6 %collective-permute-done.14 = f32[1,3,32,512]{3,2,1,0:T(8,128)S(1)} collective-permute-done((f32[1,3,32,512]{3,2,1,0:T(8,128)S(1)}, f32[1,3,32,512]{3,2,1,0:T(8,128)S(1)}, u32[]{:S(2)}, u32[]{:S(2)}) %collective-permute-start.14) | collective-permute-done | bytes 196640 | tf_op jit(solution)/shard_map/ppermute | solution.py:17
  93.4 4.8 %collective-permute-done.15 = f32[1,3,32,512]{3,2,1,0:T(8,128)S(1)} collective-permute-done((f32[1,3,32,512]{3,2,1,0:T(8,128)S(1)}, f32[1,3,32,512]{3,2,1,0:T(8,128)S(1)}, u32[]{:S(2)}, u32[]{:S(2)}) %collective-permute-start.15) | collective-permute-done | bytes 196640 | tf_op jit(solution)/shard_map/ppermute | solution.py:20
  98.2 4.9 %gather_fusion.1 = f32[1024,512]{1,0:T(8,128)} fusion(f32[288,512]{1,0:T(8,128)S(1)} %bitcast.66, s32[1024]{0:T(1024)S(1)} %broadcast_clamp_fusion), kind=kCustom, calls=%fused_computation.3 | custom fusion | bytes 4198400 | tf_op jit(solution)/shard_map/jit(_take)/gather | solution.py:59
  103.1 1.9 gather.18
  105.0 4.3 %fusion = f32[256,1,512]{2,1,0:T(1,128)S(1)} fusion(f32[256,4,1]{1,2,0:T(1,128)S(1)} %copy.25, f32[256,4,512]{2,1,0:T(4,128)S(1)} %gather.18, pred[256,4]{1,0:T(8,128)(4,1)S(1)} %copy-done.6), kind=kOutput, calls=%fused_computation.4 | convolution fusion | flops 6815744 | bytes 2626560 | tf_op jit(solution)/shard_map/rk,rkd->rd/dot_general | solution.py:62
  111.3 41.9 %all-reduce = (f32[128]{0:T(128)S(1)}, f32[128]{0:T(128)S(1)}) all-reduce(f32[128]{0:T(128)S(1)} %get-tuple-element.5, f32[128]{0:T(128)S(1)} %get-tuple-element.4), channel_id=1, replica_groups=mesh['lat'=8,'lon'=4] {'lat','lon'}, use_global_device_ids=true, to_apply=%region_10.12 | all-reduce | flops 256 | bytes 2048 | tf_op jit(solution)/shard_map/psum | solution.py:112
  153.8 1.7 fusion.24
  155.5 125.6 %all-reduce.3.cloned.1.call-done = f32[512,128]{1,0:T(8,128)} async-done(((f32[512,128]{1,0:T(8,128)}), f32[512,128]{1,0:T(8,128)}) %all-reduce.3.cloned.1.call-update) | async-done | bytes 262160 | tf_op jit(solution)/shard_map/psum | solution.py:112
  281.1 1.7 copy.46
  (100 shorter events, 21.9 us)
Async XLA Ops:
  7.2 6.9 %copy-start.9 = (s32[32,6]{0,1:T(8,128)S(1)}, s32[32,6]{0,1:T(8,128)}, u32[]{:S(2)}) copy-start(s32[32,6]{0,1:T(8,128)} %param.25) | copy-start | bytes 2308
  7.2 7.2 %copy-start.10 = (s32[32,8]{0,1:T(8,128)S(1)}, s32[32,8]{0,1:T(8,128)}, u32[]{:S(2)}) copy-start(s32[32,8]{0,1:T(8,128)} %param.23) | copy-start | bytes 3076
  7.2 7.4 %copy-start.11 = (s32[256,4]{0,1:T(4,128)S(1)}, s32[256,4]{0,1:T(4,128)}, u32[]{:S(2)}) copy-start(s32[256,4]{0,1:T(4,128)} %param.26) | copy-start | bytes 12292
  7.2 7.8 %copy-start.7 = (f32[32,8]{0,1:T(8,128)S(1)}, f32[32,8]{0,1:T(8,128)}, u32[]{:S(2)}) copy-start(f32[32,8]{0,1:T(8,128)} %param.24) | copy-start | bytes 3076
  7.2 8.7 %copy-start.8 = (f32[256,4]{0,1:T(4,128)S(1)}, f32[256,4]{0,1:T(4,128)}, u32[]{:S(2)}) copy-start(f32[256,4]{0,1:T(4,128)} %param.27) | copy-start | bytes 12292
  7.2 273.9 %all-reduce.3.cloned.1.call-start = ((), (), s32[]{:S(2)}) async-start(), calls=%async_computation | async-start | bytes 524288 | tf_op jit(solution)/shard_map/psum | solution.py:112
  11.7 5.0 %collective-permute-start = (f32[1,1,16,512]{3,2,1,0:T(8,128)S(1)}, f32[1,1,16,512]{3,2,1,0:T(8,128)S(1)}, u32[]{:S(2)}, u32[]{:S(2)}) collective-permute-start(f32[1,1,16,512]{3,2,1,0:T(8,128)S(1)} %multiply_bitcast_fusion), channel_id=1, source_target_pairs={{0,1},{1,2},{2,3},{3,0},{4,5},{5,6},{6,7},{7,4},{8,9},{9,10},{10,1... | collective-permute-start | bytes 98312 | tf_op jit(solution)/shard_map/ppermute | solution.py:17
  12.1 4.5 %collective-permute-start.1 = (f32[1,1,16,512]{3,2,1,0:T(8,128)S(1)}, f32[1,1,16,512]{3,2,1,0:T(8,128)S(1)}, u32[]{:S(2)}, u32[]{:S(2)}) collective-permute-start(f32[1,1,16,512]{3,2,1,0:T(8,128)S(1)} %multiply_bitcast_fusion), channel_id=1, source_target_pairs={{1,0},{2,1},{3,2},{0,3},{5,4},{6,5},{7,6},{4,7},{9,8},{10,9},{11,1... | collective-permute-start | bytes 98312 | tf_op jit(solution)/shard_map/ppermute | solution.py:20
  16.6 7.1 %collective-permute-start.2 = (f32[1,3,16,512]{3,2,1,0:T(8,128)S(1)}, f32[1,3,16,512]{3,2,1,0:T(8,128)S(1)}, u32[]{:S(2)}, u32[]{:S(2)}) collective-permute-start(f32[1,3,16,512]{3,2,1,0:T(8,128)S(1)} %pad_maximum_fusion.7), channel_id=1, source_target_pairs={{0,4},{4,8},{8,12},{12,16},{16,20},{20,24},{24,28},{1,5},{5,9},{9,... | collective-permute-start | bytes 294920 | tf_op jit(solution)/shard_map/ppermute | solution.py:17
  20.8 7.0 %collective-permute-start.3 = (f32[1,3,16,512]{3,2,1,0:T(8,128)S(1)}, f32[1,3,16,512]{3,2,1,0:T(8,128)S(1)}, u32[]{:S(2)}, u32[]{:S(2)}) collective-permute-start(f32[1,3,16,512]{3,2,1,0:T(8,128)S(1)} %pad_maximum_fusion.7), channel_id=1, source_target_pairs={{4,0},{8,4},{12,8},{16,12},{20,16},{24,20},{28,24},{5,1},{9,5},{13... | collective-permute-start | bytes 294920 | tf_op jit(solution)/shard_map/ppermute | solution.py:20
  29.9 3.7 %collective-permute-start.4 = (f32[1,1,32,512]{3,2,1,0:T(8,128)S(1)}, f32[1,1,32,512]{3,2,1,0:T(8,128)S(1)}, u32[]{:S(2)}, u32[]{:S(2)}) collective-permute-start(f32[1,1,32,512]{3,2,1,0:T(8,128)S(1)} %get-tuple-element.12), channel_id=1, source_target_pairs={{0,1},{1,2},{2,3},{3,0},{4,5},{5,6},{6,7},{7,4},{8,9},{9,10},{10,1... | collective-permute-start | bytes 196616 | tf_op jit(solution)/shard_map/ppermute | solution.py:17
  29.9 3.7 %collective-permute-start.5 = (f32[1,1,32,512]{3,2,1,0:T(8,128)S(1)}, f32[1,1,32,512]{3,2,1,0:T(8,128)S(1)}, u32[]{:S(2)}, u32[]{:S(2)}) collective-permute-start(f32[1,1,32,512]{3,2,1,0:T(8,128)S(1)} %get-tuple-element.12), channel_id=1, source_target_pairs={{1,0},{2,1},{3,2},{0,3},{5,4},{6,5},{7,6},{4,7},{9,8},{10,9},{11,1... | collective-permute-start | bytes 196616 | tf_op jit(solution)/shard_map/ppermute | solution.py:20
  33.6 13.5 %collective-permute-start.6 = (f32[1,3,32,512]{3,2,1,0:T(8,128)S(1)}, f32[1,3,32,512]{3,2,1,0:T(8,128)S(1)}, u32[]{:S(2)}, u32[]{:S(2)}) collective-permute-start(f32[1,3,32,512]{3,2,1,0:T(8,128)S(1)} %pad_maximum_fusion.4), channel_id=1, source_target_pairs={{0,4},{4,8},{8,12},{12,16},{16,20},{20,24},{24,28},{1,5},{5,9},{9,... | collective-permute-start | bytes 589832 | tf_op jit(solution)/shard_map/ppermute | solution.py:17
  38.0 9.6 %collective-permute-start.7 = (f32[1,3,32,512]{3,2,1,0:T(8,128)S(1)}, f32[1,3,32,512]{3,2,1,0:T(8,128)S(1)}, u32[]{:S(2)}, u32[]{:S(2)}) collective-permute-start(f32[1,3,32,512]{3,2,1,0:T(8,128)S(1)} %pad_maximum_fusion.4), channel_id=1, source_target_pairs={{4,0},{8,4},{12,8},{16,12},{20,16},{24,20},{28,24},{5,1},{9,5},{13... | collective-permute-start | bytes 589832 | tf_op jit(solution)/shard_map/ppermute | solution.py:20
  49.2 5.0 %copy-start.1 = (f32[2,512,512]{2,1,0:T(8,128)S(1)}, f32[2,512,512]{2,1,0:T(8,128)}, u32[]{:S(2)}) copy-start(f32[2,512,512]{2,1,0:T(8,128)} %param.19) | copy-start | bytes 6291460
  55.1 3.7 %collective-permute-start.8 = (f32[1,1,32,512]{3,2,1,0:T(8,128)S(1)}, f32[1,1,32,512]{3,2,1,0:T(8,128)S(1)}, u32[]{:S(2)}, u32[]{:S(2)}) collective-permute-start(f32[1,1,32,512]{3,2,1,0:T(8,128)S(1)} %bitcast.70), channel_id=1, source_target_pairs={{0,1},{1,2},{2,3},{3,0},{4,5},{5,6},{6,7},{7,4},{8,9},{9,10},{10,1... | collective-permute-start | bytes 196616 | tf_op jit(solution)/shard_map/ppermute | solution.py:17
  55.2 3.6 %collective-permute-start.9 = (f32[1,1,32,512]{3,2,1,0:T(8,128)S(1)}, f32[1,1,32,512]{3,2,1,0:T(8,128)S(1)}, u32[]{:S(2)}, u32[]{:S(2)}) collective-permute-start(f32[1,1,32,512]{3,2,1,0:T(8,128)S(1)} %bitcast.71), channel_id=1, source_target_pairs={{1,0},{2,1},{3,2},{0,3},{5,4},{6,5},{7,6},{4,7},{9,8},{10,9},{11,1... | collective-permute-start | bytes 196616 | tf_op jit(solution)/shard_map/ppermute | solution.py:20
  58.8 9.2 %collective-permute-start.10 = (f32[1,3,32,512]{3,2,1,0:T(8,128)S(1)}, f32[1,3,32,512]{3,2,1,0:T(8,128)S(1)}, u32[]{:S(2)}, u32[]{:S(2)}) collective-permute-start(f32[1,3,32,512]{3,2,1,0:T(8,128)S(1)} %pad_maximum_fusion.5), channel_id=1, source_target_pairs={{0,4},{4,8},{8,12},{12,16},{16,20},{20,24},{24,28},{1,5},{5,9},{9,... | collective-permute-start | bytes 589832 | tf_op jit(solution)/shard_map/ppermute | solution.py:17
  63.0 9.6 %collective-permute-start.11 = (f32[1,3,32,512]{3,2,1,0:T(8,128)S(1)}, f32[1,3,32,512]{3,2,1,0:T(8,128)S(1)}, u32[]{:S(2)}, u32[]{:S(2)}) collective-permute-start(f32[1,3,32,512]{3,2,1,0:T(8,128)S(1)} %pad_maximum_fusion.5), channel_id=1, source_target_pairs={{4,0},{8,4},{12,8},{16,12},{20,16},{24,20},{28,24},{5,1},{9,5},{13... | collective-permute-start | bytes 589832 | tf_op jit(solution)/shard_map/ppermute | solution.py:20
  74.2 5.0 %copy-start.2 = (f32[2,512,512]{2,1,0:T(8,128)S(1)}, f32[2,512,512]{2,1,0:T(8,128)}, u32[]{:S(2)}) copy-start(f32[2,512,512]{2,1,0:T(8,128)} %param.19) | copy-start | bytes 6291460
  74.2 7.6 %copy-start.13 = (s32[128]{0:T(128)S(1)}, s32[128]{0:T(128)}, u32[]{:S(2)}) copy-start(s32[128]{0:T(128)} %param.22) | copy-start | bytes 1540
  80.0 3.7 %collective-permute-start.12 = (f32[1,1,32,512]{3,2,1,0:T(8,128)S(1)}, f32[1,1,32,512]{3,2,1,0:T(8,128)S(1)}, u32[]{:S(2)}, u32[]{:S(2)}) collective-permute-start(f32[1,1,32,512]{3,2,1,0:T(8,128)S(1)} %add_bitcast_fusion), channel_id=1, source_target_pairs={{0,1},{1,2},{2,3},{3,0},{4,5},{5,6},{6,7},{7,4},{8,9},{9,10},{10,1... | collective-permute-start | bytes 196616 | tf_op jit(solution)/shard_map/ppermute | solution.py:17
  80.1 3.7 %collective-permute-start.13 = (f32[1,1,32,512]{3,2,1,0:T(8,128)S(1)}, f32[1,1,32,512]{3,2,1,0:T(8,128)S(1)}, u32[]{:S(2)}, u32[]{:S(2)}) collective-permute-start(f32[1,1,32,512]{3,2,1,0:T(8,128)S(1)} %add_bitcast_fusion), channel_id=1, source_target_pairs={{1,0},{2,1},{3,2},{0,3},{5,4},{6,5},{7,6},{4,7},{9,8},{10,9},{11,1... | collective-permute-start | bytes 196616 | tf_op jit(solution)/shard_map/ppermute | solution.py:20
  83.8 9.6 %collective-permute-start.14 = (f32[1,3,32,512]{3,2,1,0:T(8,128)S(1)}, f32[1,3,32,512]{3,2,1,0:T(8,128)S(1)}, u32[]{:S(2)}, u32[]{:S(2)}) collective-permute-start(f32[1,3,32,512]{3,2,1,0:T(8,128)S(1)} %pad_maximum_fusion.6), channel_id=1, source_target_pairs={{0,4},{4,8},{8,12},{12,16},{16,20},{20,24},{24,28},{1,5},{5,9},{9,... | collective-permute-start | bytes 589832 | tf_op jit(solution)/shard_map/ppermute | solution.py:17
  88.3 9.9 %collective-permute-start.15 = (f32[1,3,32,512]{3,2,1,0:T(8,128)S(1)}, f32[1,3,32,512]{3,2,1,0:T(8,128)S(1)}, u32[]{:S(2)}, u32[]{:S(2)}) collective-permute-start(f32[1,3,32,512]{3,2,1,0:T(8,128)S(1)} %pad_maximum_fusion.6), channel_id=1, source_target_pairs={{4,0},{8,4},{12,8},{16,12},{20,16},{24,20},{28,24},{5,1},{9,5},{13... | collective-permute-start | bytes 589832 | tf_op jit(solution)/shard_map/ppermute | solution.py:20
  103.1 1.9 copy-start.6
  105.0 4.3 %copy-start.12 = (f32[256]{0:T(256)S(1)}, f32[256]{0:T(256)}, u32[]{:S(2)}) copy-start(f32[256]{0:T(256)} %reduce_sum.125) | copy-start | bytes 3076
  105.0 4.3 %copy-start.14 = (f32[512,512]{1,0:T(8,128)S(1)}, f32[512,512]{1,0:T(8,128)}, u32[]{:S(2)}) copy-start(f32[512,512]{1,0:T(8,128)} %param.20) | copy-start | bytes 3145732
  105.0 4.3 %copy-start.15 = (f32[256,512]{1,0:T(8,128)S(1)}, f32[256,512]{1,0:T(8,128)}, u32[]{:S(2)}) copy-start(f32[256,512]{1,0:T(8,128)} %param.15) | copy-start | bytes 1572868
  105.0 4.3 %copy-start.16 = (f32[256,512]{1,0:T(8,128)S(1)}, f32[256,512]{1,0:T(8,128)}, u32[]{:S(2)}) copy-start(f32[256,512]{1,0:T(8,128)} %get-tuple-element.17) | copy-start | bytes 1572868
  109.4 1.3 copy-start.3
  111.3 171.5 %copy-start.4 = (f32[256,128]{1,0:T(8,128)}, f32[256,128]{1,0:T(8,128)S(1)}, u32[]{:S(2)}) copy-start(f32[256,128]{1,0:T(8,128)S(1)} %get-tuple-element.21) | copy-start | bytes 393220
  (2 other events, 2.6 us)
Sparse Core Ops, SparseCore 0:
  155.7 125.4 all-reduce.2
where the time goes:
time: 290 us
  waiting for transfers between devices  157 us (54%)
  blocking collectives  41.9 us (14%)
  starting transfers between devices  30.3 us (10%)
  local copies, waits for them, and re-layouts  19.2 us (7%)
  matrix products  17.3 us (6%)
  between operations  15.2 us (5%)
  other arithmetic  9.14 us (3%)
    psum x1, waiting for transfers between devices, shards(): err, grad_out = lax.psum((err_part, grad_part), ('lat', 'lon'))  126 us
    psum x1, blocking collectives, shards(): err, grad_out = lax.psum((err_part, grad_part), ('lat', 'lon'))  41.9 us
    ppermute x8, starting transfers between devices, padded(): lax.ppermute(lax.slice_in_dim(block, block.shape[dim] - width, None, axis...  17.9 us
    ppermute x8, waiting for transfers between devices, padded(): lax.ppermute(lax.slice_in_dim(block, block.shape[dim] - width, None, axis...  17.2 us
    ppermute x8, waiting for transfers between devices, padded(): lax.ppermute(lax.slice_in_dim(block, 0, width, axis=dim), axis, backward)  13.8 us
    ppermute x8, starting transfers between devices, padded(): lax.ppermute(lax.slice_in_dim(block, 0, width, axis=dim), axis, backward)  12.4 us
    dot_general x8, matrix products, matmul(): jnp.dot(left, right, precision=lax.Precision.HIGHEST, preferred_element_t...  12.3 us
    gather x3, local copies, waits for them, and re-layouts, interp(): jnp.take(window, local.reshape(-1), axis=0)  7.73 us
  transfers between devices with their start and end apart: 17, of which 12 were waited for; matrix products, arithmetic and copies ran while one was open for 2% of the time, Pallas kernels for 0%

commit v1 on v0

v1 whole, which is shorter than its diff:
```python
import functools

import jax
import jax.numpy as jnp
from jax import lax
from jax.experimental import pallas as pl
from jax.experimental.pallas import tpu as pltpu
from jax.sharding import PartitionSpec as P

BS = 16
L = 2
AXES = ("lat", "lon")
F32 = jnp.float32
BF16 = jnp.bfloat16
LANES = 128
GROUP = 32
TILE = 128
VMEM_LIMIT = 56 * 1024 * 1024


def split(value):
    high = value.astype(BF16)
    return high, (value - high.astype(F32)).astype(BF16)


def dot(left, right):
    return jnp.dot(left, right, preferred_element_type=F32)


def dot3(left, right):
    (lh, ll), (rh, rl) = left, right
    return dot(lh, rh) + (dot(lh, rl) + dot(ll, rh))


def silu(value):
    return value / (1.0 + jnp.exp(-value))


def vmem():
    return pl.BlockSpec(memory_space=pltpu.VMEM)


def smem():
    return pl.BlockSpec(memory_space=pltpu.SMEM)


def shape(dims, dtype=F32):
    return jax.ShapeDtypeStruct(dims, dtype)


def encode_kernel(x_ref, w_ref, e_ref, h_ref, p_ref):
    x = x_ref[...]
    h = x + silu(dot3(split(x), split(w_ref[...])))
    h_ref[...] = h
    rows, width = x.shape
    n_blocks = rows // BS
    means = jnp.sum(h.reshape(n_blocks, BS, width), axis=1) * (1.0 / BS)
    for part in range(n_blocks // 8):
        p_ref[:, part * width:(part + 1) * width] = means[part * 8:(part + 1) * 8]
    p_ref[:, (n_blocks // 8) * width:] = e_ref[...]


def prepare_kernel(base_node, s_ref, ws_ref, wn_ref, wd_ref, wo_ref, i_ref, c_ref, wh_ref, wl_ref, oh_ref, ol_ref, ah_ref, al_ref):
    for layer in range(L):
        wh_ref[2 * layer], wl_ref[2 * layer] = split(ws_ref[layer])
        wh_ref[2 * layer + 1], wl_ref[2 * layer + 1] = split(wn_ref[layer])
    wh_ref[2 * L], wl_ref[2 * L] = split(wd_ref[...])
    oh_ref[...], ol_ref[...] = split(wo_ref[...])
    rows, nodes = ah_ref.shape
    spread = i_ref.shape[1]
    local = (i_ref[...] - s_ref[4] * base_node).astype(F32)
    coef = c_ref[...]
    coef = coef / jnp.sum(coef, axis=1, keepdims=True)
    step = 32
    column = lax.broadcasted_iota(jnp.int32, (step, nodes), 1).astype(F32)
    for at in range(0, rows, step):
        total = jnp.zeros((step, nodes), F32)
        for k in range(spread):
            total = total + jnp.where(column == local[at:at + step, k:k + 1], coef[at:at + step, k:k + 1], 0.0)
        ah_ref[at:at + step], al_ref[at:at + step] = split(total)


def mesh_kernel(plan, s_ref, *refs):
    n_tables = plan["tables"]
    tables, refs = refs[:n_tables], refs[n_tables:]
    (wh_ref, wl_ref, oh_ref, ol_ref, ah_ref, al_ref, h_ref, t_ref, pred_ref, keep_ref, send_ref,
     th, tl, info, m0f, m0h, m0l, m1f, m1h, m1l, m2h, m2l) = refs
    width = h_ref.shape[1]
    lon, n_blocks, nodes = plan["lon"], plan["blocks"], plan["nodes"]
    k_g2m, k_nbr = plan["k_g2m"], plan["k_nbr"]
    slots = tables[0].shape[0]
    me = s_ref[0]
    for c, table in enumerate(tables):
        for i in range(slots):
            if plan["xor"] is None:
                place = i
            else:
                place = me ^ plan["xor"][c * slots + i]
            tile = table[i]
            rows = jnp.concatenate([tile[:, p * width:(p + 1) * width] for p in range(n_blocks // 8)], axis=0)
            at = pl.multiple_of(place * n_blocks, n_blocks)
            th[pl.ds(at, n_blocks), :], tl[pl.ds(at, n_blocks), :] = split(rows)
            info[place] = tile[:, (n_blocks // 8) * width:]

    per_step = TILE // nodes
    groups = nodes // 8

    def node_rows(first, build):
        out = []
        for d in range(per_step):
            tile = info[first + d]
            for j in range(groups):
                out.append(build(tile, j * GROUP))
        return out

    first0 = (s_ref[2] - s_ref[1]) * lon
    base_block = (s_ref[1] * (lon * n_blocks)).astype(F32)
    column_b = lax.broadcasted_iota(jnp.int32, (8, th.shape[0]), 1).astype(F32)

    def to_mesh(step, carry):
        def build(tile, lane):
            local = tile - base_block
            total = jnp.zeros(column_b.shape, F32)
            norm = jnp.zeros((8, 1), F32)
            for k in range(k_g2m):
                coef = tile[:, lane + k_g2m + k:lane + k_g2m + k + 1]
                total = total + jnp.where(column_b == local[:, lane + k:lane + k + 1], coef, 0.0)
                norm = norm + coef
            return total, jnp.where(norm == 0.0, 1.0, norm)

        parts = node_rows(first0 + step * per_step, build)
        matrix = jnp.concatenate([p[0] for p in parts], axis=0)
        norm = jnp.concatenate([p[1] for p in parts], axis=0)
        value = dot3(split(matrix), (th[...], tl[...])) / norm
        at = pl.ds(pl.multiple_of(step * TILE, TILE), TILE)
        m0f[at, :] = value
        m0h[at, :], m0l[at, :] = split(value)
        return carry

    lax.fori_loop(0, m0f.shape[0] // TILE, to_mesh, 0)

    def mixing(layer, src, src_band, out, out_band):
        srcf, srch, srcl = src
        column = lax.broadcasted_iota(jnp.int32, (8, srch.shape[0]), 1).astype(F32)
        base = (src_band * (lon * nodes)).astype(F32)
        first = (out_band - s_ref[1]) * lon
        shift = (out_band - src_band) * (lon * nodes)
        self_weight = (wh_ref[2 * layer], wl_ref[2 * layer])
        nbr_weight = (wh_ref[2 * layer + 1], wl_ref[2 * layer + 1])

        def body(step, carry):
            def build(tile, lane):
                local = tile - base
                total = jnp.zeros(column.shape, F32)
                for k in range(k_nbr):
                    at = lane + 2 * k_g2m + k
                    total = total + jnp.where(column == local[:, at:at + 1], 1.0, 0.0)
                return total

            matrix = jnp.concatenate(node_rows(first + step * per_step, build), axis=0).astype(BF16)
            agg = (dot(matrix, srch[...]) + dot(matrix, srcl[...])) * (1.0 / k_nbr)
            own = srcf[pl.ds(pl.multiple_of(shift + step * TILE, nodes), TILE), :]
            center = own - jnp.mean(own, axis=1, keepdims=True)
            nrm = center / jnp.sqrt(jnp.mean(center * center, axis=1, keepdims=True) + 1e-05)
            value = own + silu(dot3(split(nrm), self_weight) + dot3(split(agg), nbr_weight))
            at = pl.ds(pl.multiple_of(step * TILE, TILE), TILE)
            if out[0] is not None:
                out[0][at, :] = value
            out[1][at, :], out[2][at, :] = split(value)
            return carry

        lax.fori_loop(0, out[1].shape[0] // TILE, body, 0)

    mixing(0, (m0f, m0h, m0l), s_ref[2], (m1f, m1h, m1l), s_ref[3])
    mixing(1, (m1f, m1h, m1l), s_ref[3], (None, m2h, m2l), s_ref[4])

    x = h_ref[...] + dot3((ah_ref[...], al_ref[...]), (m2h[...], m2l[...]))
    z = split(silu(dot3(split(x), (wh_ref[2 * L], wl_ref[2 * L]))))
    pred = dot3(z, (oh_ref[...], ol_ref[...]))
    pred_ref[...] = pred
    target = t_ref[...]
    resid = pred - target
    err = jnp.sum(resid * resid, axis=0, keepdims=True)
    power = jnp.sum(target * target, axis=0, keepdims=True)
    sums = jnp.concatenate([err, power, jnp.zeros((6, err.shape[1]), F32)], axis=0)
    (zh, zl), (rh, rl) = z, split(resid)

    def dot_t(left, right):
        return lax.dot_general(left, right, (((0,), (0,)), ((), ())), preferred_element_type=F32)

    grad = dot_t(zh, rh) + (dot_t(zh, rl) + dot_t(zl, rh))
    half = width // 2
    swap = (me & 1) == 1
    top, bottom = grad[:half], grad[half:]
    keep_ref[:half] = jnp.where(swap, bottom, top)
    send_ref[:half] = jnp.where(swap, top, bottom)
    keep_ref[half:] = sums
    send_ref[half:] = sums


def flip(value, mask, count):
    return lax.ppermute(value, AXES, [(i, i ^ mask) for i in range(count)])


def pick(value, at):
    return lax.dynamic_index_in_dim(value, at, 0, keepdims=False)


def gather_all(payload, count):
    bits = count.bit_length() - 1
    groups = []
    top = bits
    while top > 1:
        low = max(1, top - 2)
        groups.append([m << low for m in range(1 << (top - low))])
        top = low
    masks = [0]
    table = payload[None]
    for group in groups:
        table = jnp.concatenate([table] + [flip(table, m, count) for m in group[1:]], axis=0)
        masks = [a ^ m for m in group for a in masks]
    return [table, flip(table, 1, count)], masks + [m ^ 1 for m in masks], groups


def gather_window(payload, reach):
    tiles = lax.all_gather(payload, "lon")
    n_lat = lax.axis_size("lat")
    bands = []
    for off in range(-reach, reach + 1):
        if off == 0:
            bands.append(tiles)
        else:
            pairs = [(i + off, i) for i in range(n_lat) if 0 <= i + off < n_lat]
            bands.append(lax.ppermute(tiles, "lat", pairs))
    return jnp.concatenate(bands, axis=0)


def shards(
    grid_in,
    target,
    w_enc,
    w_mix_self,
    w_mix_nbr,
    w_dec,
    w_out,
    var_weight,
    g2m_idx,
    g2m_w,
    mesh_nbr,
    m2g_idx,
    m2g_w,
):
    n_lat, n_lon = lax.axis_size("lat"), lax.axis_size("lon")
    count = n_lat * n_lon
    rows, width = grid_in.shape
    n_blocks = rows // BS
    nodes = g2m_idx.shape[0]
    k_g2m, k_nbr = g2m_idx.shape[1], mesh_nbr.shape[1]
    n_var = target.shape[1]
    band, tile = lax.axis_index("lat"), lax.axis_index("lon")
    me = band * n_lon + tile
    butterfly = count & (count - 1) == 0 and n_lat <= 9 and count >= 8
    reaches = (4, 3, 2, 1)
    if butterfly:
        widths = [min(2 * r + 1, n_lat) for r in reaches]
        starts = [jnp.clip(band - r, 0, n_lat - w) for r, w in zip(reaches, widths)]
        widths[0], starts[0] = n_lat, jnp.zeros_like(band)
    else:
        widths = [2 * r + 1 for r in reaches]
        starts = [band - r for r in reaches]
    scalars = jnp.stack([me] + starts).astype(jnp.int32)

    info = jnp.concatenate(
        [g2m_idx.astype(F32), g2m_w, mesh_nbr.astype(F32), jnp.zeros((nodes, GROUP - 2 * k_g2m - k_nbr), F32)], axis=1
    )
    info = info.reshape(nodes // 8, 8, GROUP).transpose(1, 0, 2).reshape(8, LANES)
    wide = (n_blocks // 8) * width + LANES
    h_one, payload = pl.pallas_call(
        encode_kernel,
        out_shape=(shape((rows, width)), shape((8, wide))),
        in_specs=[vmem()] * 3,
        out_specs=(vmem(), vmem()),
        compiler_params=pltpu.CompilerParams(vmem_limit_bytes=VMEM_LIMIT),
        name="encode",
    )(grid_in, w_enc, info)

    n2 = widths[3] * n_lon * nodes
    wh, wl, oh, ol, ah, al = pl.pallas_call(
        functools.partial(prepare_kernel, n_lon * nodes),
        out_shape=(
            shape((2 * L + 1, width, width), BF16),
            shape((2 * L + 1, width, width), BF16),
            shape((width, n_var), BF16),
            shape((width, n_var), BF16),
            shape((rows, n2), BF16),
            shape((rows, n2), BF16),
        ),
        in_specs=[smem()] + [vmem()] * 6,
        out_specs=[vmem()] * 6,
        compiler_params=pltpu.CompilerParams(vmem_limit_bytes=VMEM_LIMIT),
        cost_estimate=pl.CostEstimate(flops=0, bytes_accessed=12 * 1024 * 1024, transcendentals=0),
        name="prepare",
    )(scalars, w_mix_self, w_mix_nbr, w_dec, w_out, m2g_idx, m2g_w)

    if butterfly:
        tables, masks, groups = gather_all(payload, count)
    else:
        tables, masks = [gather_window(payload, reaches[0])], None
    plan = dict(tables=len(tables), xor=masks, lon=n_lon, blocks=n_blocks, nodes=nodes, k_g2m=k_g2m, k_nbr=k_nbr)
    nb = widths[0] * n_lon * n_blocks
    n0, n1 = (w * n_lon * nodes for w in widths[1:3])
    half = width // 2
    pred, keep, send = pl.pallas_call(
        functools.partial(mesh_kernel, plan),
        out_shape=(shape((rows, n_var)), shape((half + 8, n_var)), shape((half + 8, n_var))),
        in_specs=[smem()] + [vmem()] * (len(tables) + 8),
        out_specs=[vmem()] * 3,
        scratch_shapes=[
            pltpu.VMEM((nb, width), BF16),
            pltpu.VMEM((nb, width), BF16),
            pltpu.VMEM((widths[0] * n_lon, 8, LANES), F32),
            pltpu.VMEM((n0, width), F32),
            pltpu.VMEM((n0, width), BF16),
            pltpu.VMEM((n0, width), BF16),
            pltpu.VMEM((n1, width), F32),
            pltpu.VMEM((n1, width), BF16),
            pltpu.VMEM((n1, width), BF16),
            pltpu.VMEM((n2, width), BF16),
            pltpu.VMEM((n2, width), BF16),
        ],
        compiler_params=pltpu.CompilerParams(vmem_limit_bytes=VMEM_LIMIT),
        name="mesh",
    )(scalars, *tables, wh, wl, oh, ol, ah, al, h_one, target)

    weights = var_weight.astype(F32)
    wsum = jnp.sum(weights)
    grid_total = rows * count

    def factors(sums):
        scale = sums[1] / grid_total + 1e-06
        return sums[0], weights / (scale * grid_total * wsum)

    if not butterfly:
        swap = (me & 1) == 1
        top = jnp.where(swap, send[:half], keep[:half])
        bottom = jnp.where(swap, keep[:half], send[:half])
        total = lax.psum(jnp.concatenate([top, bottom, keep[half:]], axis=0), AXES)
        err, factor = factors(total[width:])
        return (pred, jnp.sum(err * factor), total[:width] * (2.0 * factor)[None, :])

    total = keep + flip(send, 1, count)
    group = groups[-1]
    low = len(group)
    at = (me >> 1) & (low - 1)
    part = half // low
    pieces, sums = total[:half].reshape(low, part, n_var), total[half:]
    total = jnp.concatenate([pick(pieces, at), sums], axis=0)
    for i, received in enumerate(
        [flip(jnp.concatenate([pick(pieces, at ^ i), sums], axis=0), m, count) for i, m in enumerate(group) if m]
    ):
        total = total + received
    for other in groups[-2::-1]:
        received = [flip(total, m, count) for m in other if m]
        for value in received:
            total = total + value
    err, factor = factors(total[part:])
    piece = total[:part] * (2.0 * factor)[None, :]
    pieces = jnp.stack([piece] + [flip(piece, m, count) for m in group if m])
    own = jnp.concatenate([pick(pieces, at ^ i) for i in range(low)], axis=0)
    other = flip(own, 1, count)
    swap = (me & 1) == 1
    grad_out = jnp.concatenate([jnp.where(swap, other, own), jnp.where(swap, own, other)], axis=0)
    return (pred, jnp.sum(err * factor), grad_out)


def solution(mesh):
    placed = (
        P(AXES, None),
        P(AXES, None),
        P(),
        P(),
        P(),
        P(),
        P(),
        P(),
        P(AXES, None),
        P(AXES, None),
        P(AXES, None),
        P(AXES, None),
        P(AXES, None),
    )
    return jax.shard_map(
        shards,
        mesh=mesh,
        in_specs=placed,
        out_specs=(P(AXES, None), P(), P()),
        check_vma=False,
    )
```

time: 290 us -> 84.8 us (0.29)
  waiting for transfers between devices: 157 us -> 19.6 us
  blocking collectives: 41.9 us -> 0 us
  Pallas kernels: 0 us -> 30.9 us
  matrix products: 17.3 us -> 0 us
  between operations: 15.2 us -> 1.52 us
  local copies, waits for them, and re-layouts: 19.2 us -> 5.72 us
  starting transfers between devices: 30.3 us -> 21.3 us
  other arithmetic: 9.14 us -> 5.21 us
    psum x1 -> x0, waiting for transfers between devices: 126 us -> none  [shards(): err, grad_out = lax.psum((err_part, grad_part), ('lat', 'lon'))]
    psum x1 -> x0, blocking collectives: 41.9 us -> none  [shards(): err, grad_out = lax.psum((err_part, grad_part), ('lat', 'lon'))]
    pallas_call x0 -> x3, Pallas kernels: none -> 30.9 us  [the longest x1 21.5 us: shards(): pl.pallas_call(functools.partial(mesh_kernel, plan), out_shape=(shape((ro...]
    dot_general x10 -> x0, matrix products: 17.3 us -> none  [the longest x8 12.3 us: matmul(): jnp.dot(left, right, precision=lax.Precision.HIGHEST, preferred_element_t...]
    ppermute x16 -> x18, waiting for transfers between devices: 31.1 us -> 19.6 us  [flip(): return lax.ppermute(value, AXES, [(i, i ^ mask) for i in range(count)])]
    gather x5 -> x0, local copies, waits for them, and re-layouts: 11 us -> none  [the longest x3 7.73 us: interp(): jnp.take(window, local.reshape(-1), axis=0)]
    ppermute x16 -> x18, starting transfers between devices: 30.3 us -> 21.3 us  [flip(): return lax.ppermute(value, AXES, [(i, i ^ mask) for i in range(count)])]
    select_n x5 -> x1, other arithmetic: 4.01 us -> 0.03 us  [shards(): jnp.where(swap, other, own)]
  transfers between devices with their start and end apart: 17 -> 18, of which waited for: 12 -> 12; matrix products, arithmetic and copies ran while one was open for 2% -> 5% of each run, Pallas kernels for 0% -> 8%
where the time goes in v1:
time: 84.8 us; the launch traced here: 84.4 us
  Pallas kernels  30.9 us (36%)
  starting transfers between devices  21.3 us (25%)
  waiting for transfers between devices  19.6 us (23%)
  local copies, waits for them, and re-layouts  5.72 us (7%)
  other arithmetic  5.21 us (6%)
  between operations  1.52 us (2%)
    pallas_call x1, Pallas kernels, shards(): pl.pallas_call(functools.partial(mesh_kernel, plan), out_shape=(shape((ro...  21.5 us
    ppermute x18, starting transfers between devices, flip(): return lax.ppermute(value, AXES, [(i, i ^ mask) for i in range(count)])  21.3 us
    ppermute x18, waiting for transfers between devices, flip(): return lax.ppermute(value, AXES, [(i, i ^ mask) for i in range(count)])  19.6 us
    pallas_call x1, Pallas kernels, shards(): pl.pallas_call(functools.partial(prepare_kernel, n_lon * nodes), out_shap...  6.59 us
    unnamed x19, local copies, waits for them, and re-layouts  4.06 us
    pallas_call x1, Pallas kernels, shards(): pl.pallas_call(encode_kernel, out_shape=(shape((rows, width)), shape((8,...  2.89 us
  transfers between devices with their start and end apart: 18, of which 12 were waited for; matrix products, arithmetic and copies ran while one was open for 5% of the time, Pallas kernels for 8%

profile of v1, /device:TPU:0, one launch (start us, length us, event | category | flops | bytes accessed | tf_op | source)
XLA Modules:
  0.0 84.4 jit_solution(15188355625345135289)
XLA Ops:
  2.2 0.8 copy.28
  3.8 2.9 %encode.1 = (f32[256,512]{1,0:T(8,128)}, f32[8,1152]{1,0:T(8,128)}) custom-call(f32[256,512]{1,0:T(8,128)} %x_ref.1, f32[512,512]{1,0:T(8,128)} %w_ref.1, f32[8,128]{1,0:T(8,128)} %reshape.23.e_ref), custom_call_target="tpu_custom_call" | custom-call | tf_op jit(solution)/shard_map/encode/pallas_call | solution.py:278
  6.7 3.0 %collective-permute-start = (f32[1,8,1152]{2,1,0:T(8,128)}, f32[1,8,1152]{2,1,0:T(8,128)S(1)}, u32[]{:S(2)}, u32[]{:S(2)}) collective-permute-start(f32[1,8,1152]{2,1,0:T(8,128)} %bitcast.44), channel_id=1, source_target_pairs={{0,8},{1,9},{2,10},{3,11},{4,12},{5,13},{6,14},{7,15},{8,0},{9,1},... | collective-permute-start | bytes 110600 | tf_op jit(solution)/shard_map/ppermute | solution.py:202
  9.7 2.6 %collective-permute-start.1 = (f32[1,8,1152]{2,1,0:T(8,128)}, f32[1,8,1152]{2,1,0:T(8,128)S(1)}, u32[]{:S(2)}, u32[]{:S(2)}) collective-permute-start(f32[1,8,1152]{2,1,0:T(8,128)} %bitcast.45), channel_id=1, source_target_pairs={{0,16},{1,17},{2,18},{3,19},{4,20},{5,21},{6,22},{7,23},{8,24},{9,... | collective-permute-start | bytes 110600 | tf_op jit(solution)/shard_map/ppermute | solution.py:202
  12.3 0.8 constant_dynamic-update-slice_fusion.6
  13.2 2.3 %collective-permute-done.1 = f32[1,8,1152]{2,1,0:T(8,128)S(1)} collective-permute-done((f32[1,8,1152]{2,1,0:T(8,128)}, f32[1,8,1152]{2,1,0:T(8,128)S(1)}, u32[]{:S(2)}, u32[]{:S(2)}) %collective-permute-start.1) | collective-permute-done | bytes 36896 | tf_op jit(solution)/shard_map/ppermute | solution.py:202
  15.5 2.8 %collective-permute-done.2 = f32[1,8,1152]{2,1,0:T(8,128)S(1)} collective-permute-done((f32[1,8,1152]{2,1,0:T(8,128)}, f32[1,8,1152]{2,1,0:T(8,128)S(1)}, u32[]{:S(2)}, u32[]{:S(2)}) %collective-permute-start.2) | collective-permute-done | bytes 36896 | tf_op jit(solution)/shard_map/ppermute | solution.py:202
  18.3 0.8 pad_maximum_fusion.1
  19.1 1.6 %collective-permute-start.3 = (f32[4,8,1152]{2,1,0:T(8,128)S(1)}, f32[4,8,1152]{2,1,0:T(8,128)S(1)}, u32[]{:S(2)}, u32[]{:S(2)}) collective-permute-start(f32[4,8,1152]{2,1,0:T(8,128)S(1)} %pad_maximum_fusion.1), channel_id=1, source_target_pairs={{0,2},{1,3},{2,0},{3,1},{4,6},{5,7},{6,4},{7,5},{8,10},{9,11},{10,... | collective-permute-start | bytes 442376 | tf_op jit(solution)/shard_map/ppermute | solution.py:202
  20.6 1.5 %collective-permute-start.4 = (f32[4,8,1152]{2,1,0:T(8,128)S(1)}, f32[4,8,1152]{2,1,0:T(8,128)S(1)}, u32[]{:S(2)}, u32[]{:S(2)}) collective-permute-start(f32[4,8,1152]{2,1,0:T(8,128)S(1)} %pad_maximum_fusion.1), channel_id=1, source_target_pairs={{0,4},{1,5},{2,6},{3,7},{4,0},{5,1},{6,2},{7,3},{8,12},{9,13},{10,... | collective-permute-start | bytes 442376 | tf_op jit(solution)/shard_map/ppermute | solution.py:202
  22.6 2.9 %collective-permute-done.3 = f32[4,8,1152]{2,1,0:T(8,128)S(1)} collective-permute-done((f32[4,8,1152]{2,1,0:T(8,128)S(1)}, f32[4,8,1152]{2,1,0:T(8,128)S(1)}, u32[]{:S(2)}, u32[]{:S(2)}) %collective-permute-start.3) | collective-permute-done | bytes 147488 | tf_op jit(solution)/shard_map/ppermute | solution.py:202
  25.5 2.8 %collective-permute-done.4 = f32[4,8,1152]{2,1,0:T(8,128)S(1)} collective-permute-done((f32[4,8,1152]{2,1,0:T(8,128)S(1)}, f32[4,8,1152]{2,1,0:T(8,128)S(1)}, u32[]{:S(2)}, u32[]{:S(2)}) %collective-permute-start.4) | collective-permute-done | bytes 147488 | tf_op jit(solution)/shard_map/ppermute | solution.py:202
  28.5 0.8 copy.31.i_ref
  29.3 0.8 copy.32.c_ref
  30.7 6.6 %prepare.1 = (bf16[5,512,512]{2,1,0:T(8,128)(2,1)}, bf16[5,512,512]{2,1,0:T(8,128)(2,1)}, bf16[512,128]{1,0:T(8,128)(2,1)}, bf16[512,128]{1,0:T(8,128)(2,1)}, bf...) custom-call(s32[5]{0:T(128)} %stack.34.s_ref, f32[2,512,512]{2,1,0:T(8,128)} %ws_ref.1, f32[2,512,512]{2,1,0:T(8,128)} %wn_ref.1, ...), custom_call_target="tpu_custom_call" | custom-call | bytes 12582912 | tf_op jit(solution)/shard_map/prepare/pallas_call | solution.py:288
  37.4 0.8 copy-done.1
  38.2 21.5 %mesh.1 = (f32[256,128]{1,0:T(8,128)}, f32[264,128]{1,0:T(8,128)}, f32[264,128]{1,0:T(8,128)}) custom-call(s32[5]{0:T(128)} %stack.34.s_ref, f32[16,8,1152]{2,1,0:T(8,128)} %copy-done, f32[16,8,1152]{2,1,0:T(8,128)} %copy-done.1, bf16[5,512,512]{2,1,0:T(8,128)(2,1)} %get-tuple-element.15.refs_2_, bf16[5,512,512]{2,1,0:T(8,128)(2,1)} %get-tuple-element.16.refs_3_, ...), custom_call_target="tpu_custom_call" | custom-call | tf_op jit(solution)/shard_map/mesh/pallas_call | solution.py:313
  60.1 1.2 %collective-permute-done.7 = f32[264,128]{1,0:T(8,128)S(1)} collective-permute-done((f32[264,128]{1,0:T(8,128)}, f32[264,128]{1,0:T(8,128)S(1)}, u32[]{:S(2)}, u32[]{:S(2)}) %collective-permute-start.7) | collective-permute-done | bytes 135200 | tf_op jit(solution)/shard_map/ppermute | solution.py:202
  61.3 0.9 %add.52 = f32[264,128]{1,0:T(8,128)S(1)} add(f32[264,128]{1,0:T(8,128)} %get-tuple-element.23, f32[264,128]{1,0:T(8,128)S(1)} %collective-permute-done.7) | non-fusion elementwise | flops 33792 | bytes 405504 | tf_op jit(solution)/shard_map/add | solution.py:351
  62.3 0.7 collective-permute-start.10
  63.0 1.9 %collective-permute-start.8 = (f32[72,128]{1,0:T(8,128)S(1)}, f32[72,128]{1,0:T(8,128)S(1)}, u32[]{:S(2)}, u32[]{:S(2)}) collective-permute-start(f32[72,128]{1,0:T(8,128)S(1)} %get-tuple-element.37), channel_id=1, source_target_pairs={{0,2},{1,3},{2,0},{3,1},{4,6},{5,7},{6,4},{7,5},{8,10},{9,11},{10,... | collective-permute-start | bytes 110600 | tf_op jit(solution)/shard_map/ppermute | solution.py:202
  64.9 1.0 %collective-permute-start.9 = (f32[72,128]{1,0:T(8,128)S(1)}, f32[72,128]{1,0:T(8,128)S(1)}, u32[]{:S(2)}, u32[]{:S(2)}) collective-permute-start(f32[72,128]{1,0:T(8,128)S(1)} %get-tuple-element.38), channel_id=1, source_target_pairs={{0,4},{1,5},{2,6},{3,7},{4,0},{5,1},{6,2},{7,3},{8,12},{9,13},{10,... | collective-permute-start | bytes 110600 | tf_op jit(solution)/shard_map/ppermute | solution.py:202
  65.9 1.5 %collective-permute-done.10 = f32[72,128]{1,0:T(8,128)S(1)} collective-permute-done((f32[72,128]{1,0:T(8,128)S(1)}, f32[72,128]{1,0:T(8,128)S(1)}, u32[]{:S(2)}, u32[]{:S(2)}) %collective-permute-start.10) | collective-permute-done | bytes 36896 | tf_op jit(solution)/shard_map/ppermute | solution.py:202
  67.4 1.4 %collective-permute-done.9 = f32[72,128]{1,0:T(8,128)S(1)} collective-permute-done((f32[72,128]{1,0:T(8,128)S(1)}, f32[72,128]{1,0:T(8,128)S(1)}, u32[]{:S(2)}, u32[]{:S(2)}) %collective-permute-start.9) | collective-permute-done | bytes 36896 | tf_op jit(solution)/shard_map/ppermute | solution.py:202
  69.0 1.1 %collective-permute-start.12 = (f32[72,128]{1,0:T(8,128)S(1)}, f32[72,128]{1,0:T(8,128)S(1)}, u32[]{:S(2)}, u32[]{:S(2)}) collective-permute-start(f32[72,128]{1,0:T(8,128)S(1)} %fusion.2), channel_id=1, source_target_pairs={{0,16},{1,17},{2,18},{3,19},{4,20},{5,21},{6,22},{7,23},{8,24},{9,... | collective-permute-start | bytes 110600 | tf_op jit(solution)/shard_map/ppermute | solution.py:202
  70.1 3.3 %collective-permute-start.13 = (f32[72,128]{1,0:T(8,128)S(1)}, f32[72,128]{1,0:T(8,128)S(1)}, u32[]{:S(2)}, u32[]{:S(2)}) collective-permute-start(f32[72,128]{1,0:T(8,128)S(1)} %fusion.2), channel_id=1, source_target_pairs={{0,24},{1,25},{2,26},{3,27},{4,28},{5,29},{6,30},{7,31},{8,16},{9,... | collective-permute-start | bytes 110600 | tf_op jit(solution)/shard_map/ppermute | solution.py:202
  74.6 1.2 %collective-permute-done.13 = f32[72,128]{1,0:T(8,128)S(1)} collective-permute-done((f32[72,128]{1,0:T(8,128)S(1)}, f32[72,128]{1,0:T(8,128)S(1)}, u32[]{:S(2)}, u32[]{:S(2)}) %collective-permute-start.13) | collective-permute-done | bytes 36896 | tf_op jit(solution)/shard_map/ppermute | solution.py:202
  76.1 1.2 %collective-permute-start.15 = (f32[64,128]{1,0:T(8,128)S(1)}, f32[64,128]{1,0:T(8,128)S(1)}, u32[]{:S(2)}, u32[]{:S(2)}) collective-permute-start(f32[64,128]{1,0:T(8,128)S(1)} %slice_multiply_fusion), channel_id=1, source_target_pairs={{0,4},{1,5},{2,6},{3,7},{4,0},{5,1},{6,2},{7,3},{8,12},{9,13},{10,... | collective-permute-start | bytes 98312 | tf_op jit(solution)/shard_map/ppermute | solution.py:202
  77.3 2.1 %collective-permute-start.16 = (f32[64,128]{1,0:T(8,128)S(1)}, f32[64,128]{1,0:T(8,128)S(1)}, u32[]{:S(2)}, u32[]{:S(2)}) collective-permute-start(f32[64,128]{1,0:T(8,128)S(1)} %slice_multiply_fusion), channel_id=1, source_target_pairs={{0,6},{1,7},{2,4},{3,5},{4,2},{5,3},{6,0},{7,1},{8,14},{9,15},{10,... | collective-permute-start | bytes 98312 | tf_op jit(solution)/shard_map/ppermute | solution.py:202
  80.1 2.1 %collective-permute-done.16 = f32[64,128]{1,0:T(8,128)S(1)} collective-permute-done((f32[64,128]{1,0:T(8,128)S(1)}, f32[64,128]{1,0:T(8,128)S(1)}, u32[]{:S(2)}, u32[]{:S(2)}) %collective-permute-start.16) | collective-permute-done | bytes 32800 | tf_op jit(solution)/shard_map/ppermute | solution.py:202
  82.9 0.7 collective-permute-done.17
  83.6 0.7 pad_maximum_fusion
  (55 shorter events, 6.6 us)
Async XLA Ops:
  0.6 27.8 %copy-start.2 = (s32[256,4]{0,1:T(4,128)S(1)}, s32[256,4]{0,1:T(4,128)}, u32[]{:S(2)}) copy-start(s32[256,4]{0,1:T(4,128)} %param.24) | copy-start | bytes 12292
  0.6 28.6 %copy-start.3 = (f32[256,4]{0,1:T(4,128)S(1)}, f32[256,4]{0,1:T(4,128)}, u32[]{:S(2)}) copy-start(f32[256,4]{0,1:T(4,128)} %param.25) | copy-start | bytes 12292
  6.7 6.5 %collective-permute-start = (f32[1,8,1152]{2,1,0:T(8,128)}, f32[1,8,1152]{2,1,0:T(8,128)S(1)}, u32[]{:S(2)}, u32[]{:S(2)}) collective-permute-start(f32[1,8,1152]{2,1,0:T(8,128)} %bitcast.44), channel_id=1, source_target_pairs={{0,8},{1,9},{2,10},{3,11},{4,12},{5,13},{6,14},{7,15},{8,0},{9,1},... | collective-permute-start | bytes 110600 | tf_op jit(solution)/shard_map/ppermute | solution.py:202
  9.7 5.7 %collective-permute-start.1 = (f32[1,8,1152]{2,1,0:T(8,128)}, f32[1,8,1152]{2,1,0:T(8,128)S(1)}, u32[]{:S(2)}, u32[]{:S(2)}) collective-permute-start(f32[1,8,1152]{2,1,0:T(8,128)} %bitcast.45), channel_id=1, source_target_pairs={{0,16},{1,17},{2,18},{3,19},{4,20},{5,21},{6,22},{7,23},{8,24},{9,... | collective-permute-start | bytes 110600 | tf_op jit(solution)/shard_map/ppermute | solution.py:202
  12.3 6.0 %collective-permute-start.2 = (f32[1,8,1152]{2,1,0:T(8,128)}, f32[1,8,1152]{2,1,0:T(8,128)S(1)}, u32[]{:S(2)}, u32[]{:S(2)}) collective-permute-start(f32[1,8,1152]{2,1,0:T(8,128)} %bitcast.46), channel_id=1, source_target_pairs={{0,24},{1,25},{2,26},{3,27},{4,28},{5,29},{6,30},{7,31},{8,16},{9,... | collective-permute-start | bytes 110600 | tf_op jit(solution)/shard_map/ppermute | solution.py:202
  19.1 6.4 %collective-permute-start.3 = (f32[4,8,1152]{2,1,0:T(8,128)S(1)}, f32[4,8,1152]{2,1,0:T(8,128)S(1)}, u32[]{:S(2)}, u32[]{:S(2)}) collective-permute-start(f32[4,8,1152]{2,1,0:T(8,128)S(1)} %pad_maximum_fusion.1), channel_id=1, source_target_pairs={{0,2},{1,3},{2,0},{3,1},{4,6},{5,7},{6,4},{7,5},{8,10},{9,11},{10,... | collective-permute-start | bytes 442376 | tf_op jit(solution)/shard_map/ppermute | solution.py:202
  20.6 7.7 %collective-permute-start.4 = (f32[4,8,1152]{2,1,0:T(8,128)S(1)}, f32[4,8,1152]{2,1,0:T(8,128)S(1)}, u32[]{:S(2)}, u32[]{:S(2)}) collective-permute-start(f32[4,8,1152]{2,1,0:T(8,128)S(1)} %pad_maximum_fusion.1), channel_id=1, source_target_pairs={{0,4},{1,5},{2,6},{3,7},{4,0},{5,1},{6,2},{7,3},{8,12},{9,13},{10,... | collective-permute-start | bytes 442376 | tf_op jit(solution)/shard_map/ppermute | solution.py:202
  22.1 6.2 %collective-permute-start.5 = (f32[4,8,1152]{2,1,0:T(8,128)S(1)}, f32[4,8,1152]{2,1,0:T(8,128)S(1)}, u32[]{:S(2)}, u32[]{:S(2)}) collective-permute-start(f32[4,8,1152]{2,1,0:T(8,128)S(1)} %pad_maximum_fusion.1), channel_id=1, source_target_pairs={{0,6},{1,7},{2,4},{3,5},{4,2},{5,3},{6,0},{7,1},{8,14},{9,15},{10,... | collective-permute-start | bytes 442376 | tf_op jit(solution)/shard_map/ppermute | solution.py:202
  28.4 9.0 %copy-start = (f32[16,8,1152]{2,1,0:T(8,128)}, f32[16,8,1152]{2,1,0:T(8,128)S(1)}, u32[]{:S(2)}) copy-start(f32[16,8,1152]{2,1,0:T(8,128)S(1)} %constant_dynamic-update-slice_fusion.refs_0_) | copy-start | bytes 1769476
  28.4 9.0 %collective-permute-start.6 = (f32[16,8,1152]{2,1,0:T(8,128)S(1)}, f32[16,8,1152]{2,1,0:T(8,128)S(1)}, u32[]{:S(2)}, u32[]{:S(2)}) collective-permute-start(f32[16,8,1152]{2,1,0:T(8,128)S(1)} %constant_dynamic-update-slice_fusion.refs_0_), channel_id=1, source_target_pairs={{0,1},{1,0},{2,3},{3,2},{4,5},{5,4},{6,7},{7,6},{8,9},{9,8},{10,11... | collective-permute-start | bytes 1769480 | tf_op jit(solution)/shard_map/ppermute | solution.py:202
  37.4 0.8 copy-start.1
  38.2 35.2 %copy-start.4 = (s32[128]{0:T(128)S(1)}, s32[128]{0:T(128)}, u32[]{:S(2)}) copy-start(s32[128]{0:T(128)} %param.20) | copy-start | bytes 1540
  59.6 1.7 %collective-permute-start.7 = (f32[264,128]{1,0:T(8,128)}, f32[264,128]{1,0:T(8,128)S(1)}, u32[]{:S(2)}, u32[]{:S(2)}) collective-permute-start(f32[264,128]{1,0:T(8,128)} %get-tuple-element.24), channel_id=1, source_target_pairs={{0,1},{1,0},{2,3},{3,2},{4,5},{5,4},{6,7},{7,6},{8,9},{9,8},{10,11... | collective-permute-start | bytes 405512 | tf_op jit(solution)/shard_map/ppermute | solution.py:202
  62.3 5.1 %collective-permute-start.10 = (f32[72,128]{1,0:T(8,128)S(1)}, f32[72,128]{1,0:T(8,128)S(1)}, u32[]{:S(2)}, u32[]{:S(2)}) collective-permute-start(f32[72,128]{1,0:T(8,128)S(1)} %get-tuple-element.39), channel_id=1, source_target_pairs={{0,6},{1,7},{2,4},{3,5},{4,2},{5,3},{6,0},{7,1},{8,14},{9,15},{10,... | collective-permute-start | bytes 110600 | tf_op jit(solution)/shard_map/ppermute | solution.py:202
  63.0 4.4 %collective-permute-start.8 = (f32[72,128]{1,0:T(8,128)S(1)}, f32[72,128]{1,0:T(8,128)S(1)}, u32[]{:S(2)}, u32[]{:S(2)}) collective-permute-start(f32[72,128]{1,0:T(8,128)S(1)} %get-tuple-element.37), channel_id=1, source_target_pairs={{0,2},{1,3},{2,0},{3,1},{4,6},{5,7},{6,4},{7,5},{8,10},{9,11},{10,... | collective-permute-start | bytes 110600 | tf_op jit(solution)/shard_map/ppermute | solution.py:202
  64.9 4.0 %collective-permute-start.9 = (f32[72,128]{1,0:T(8,128)S(1)}, f32[72,128]{1,0:T(8,128)S(1)}, u32[]{:S(2)}, u32[]{:S(2)}) collective-permute-start(f32[72,128]{1,0:T(8,128)S(1)} %get-tuple-element.38), channel_id=1, source_target_pairs={{0,4},{1,5},{2,6},{3,7},{4,0},{5,1},{6,2},{7,3},{8,12},{9,13},{10,... | collective-permute-start | bytes 110600 | tf_op jit(solution)/shard_map/ppermute | solution.py:202
  68.9 5.7 %collective-permute-start.11 = (f32[72,128]{1,0:T(8,128)S(1)}, f32[72,128]{1,0:T(8,128)S(1)}, u32[]{:S(2)}, u32[]{:S(2)}) collective-permute-start(f32[72,128]{1,0:T(8,128)S(1)} %fusion.2), channel_id=1, source_target_pairs={{0,8},{1,9},{2,10},{3,11},{4,12},{5,13},{6,14},{7,15},{8,0},{9,1},... | collective-permute-start | bytes 110600 | tf_op jit(solution)/shard_map/ppermute | solution.py:202
  69.0 5.6 %collective-permute-start.12 = (f32[72,128]{1,0:T(8,128)S(1)}, f32[72,128]{1,0:T(8,128)S(1)}, u32[]{:S(2)}, u32[]{:S(2)}) collective-permute-start(f32[72,128]{1,0:T(8,128)S(1)} %fusion.2), channel_id=1, source_target_pairs={{0,16},{1,17},{2,18},{3,19},{4,20},{5,21},{6,22},{7,23},{8,24},{9,... | collective-permute-start | bytes 110600 | tf_op jit(solution)/shard_map/ppermute | solution.py:202
  70.1 5.8 %collective-permute-start.13 = (f32[72,128]{1,0:T(8,128)S(1)}, f32[72,128]{1,0:T(8,128)S(1)}, u32[]{:S(2)}, u32[]{:S(2)}) collective-permute-start(f32[72,128]{1,0:T(8,128)S(1)} %fusion.2), channel_id=1, source_target_pairs={{0,24},{1,25},{2,26},{3,27},{4,28},{5,29},{6,30},{7,31},{8,16},{9,... | collective-permute-start | bytes 110600 | tf_op jit(solution)/shard_map/ppermute | solution.py:202
  75.9 4.0 %collective-permute-start.14 = (f32[64,128]{1,0:T(8,128)S(1)}, f32[64,128]{1,0:T(8,128)S(1)}, u32[]{:S(2)}, u32[]{:S(2)}) collective-permute-start(f32[64,128]{1,0:T(8,128)S(1)} %slice_multiply_fusion), channel_id=1, source_target_pairs={{0,2},{1,3},{2,0},{3,1},{4,6},{5,7},{6,4},{7,5},{8,10},{9,11},{10,... | collective-permute-start | bytes 98312 | tf_op jit(solution)/shard_map/ppermute | solution.py:202
  76.1 3.9 %collective-permute-start.15 = (f32[64,128]{1,0:T(8,128)S(1)}, f32[64,128]{1,0:T(8,128)S(1)}, u32[]{:S(2)}, u32[]{:S(2)}) collective-permute-start(f32[64,128]{1,0:T(8,128)S(1)} %slice_multiply_fusion), channel_id=1, source_target_pairs={{0,4},{1,5},{2,6},{3,7},{4,0},{5,1},{6,2},{7,3},{8,12},{9,13},{10,... | collective-permute-start | bytes 98312 | tf_op jit(solution)/shard_map/ppermute | solution.py:202
  77.3 4.8 %collective-permute-start.16 = (f32[64,128]{1,0:T(8,128)S(1)}, f32[64,128]{1,0:T(8,128)S(1)}, u32[]{:S(2)}, u32[]{:S(2)}) collective-permute-start(f32[64,128]{1,0:T(8,128)S(1)} %slice_multiply_fusion), channel_id=1, source_target_pairs={{0,6},{1,7},{2,4},{3,5},{4,2},{5,3},{6,0},{7,1},{8,14},{9,15},{10,... | collective-permute-start | bytes 98312 | tf_op jit(solution)/shard_map/ppermute | solution.py:202
  82.2 1.4 %collective-permute-start.17 = (f32[256,128]{1,0:T(8,128)S(1)}, f32[256,128]{1,0:T(8,128)S(1)}, u32[]{:S(2)}, u32[]{:S(2)}) collective-permute-start(f32[256,128]{1,0:T(8,128)S(1)} %pad_maximum_fusion.3), channel_id=1, source_target_pairs={{0,1},{1,0},{2,3},{3,2},{4,5},{5,4},{6,7},{7,6},{8,9},{9,8},{10,11... | collective-permute-start | bytes 393224 | tf_op jit(solution)/shard_map/ppermute | solution.py:202

commit v2 on v1

v2 whole, which is shorter than its diff:
```python
import functools

import jax
import jax.numpy as jnp
from jax import lax
from jax.experimental import pallas as pl
from jax.experimental.pallas import tpu as pltpu
from jax.sharding import PartitionSpec as P

BS = 16
L = 2
REACHES = (4, 3, 2, 1)
AXES = ("lat", "lon")
F32 = jnp.float32
BF16 = jnp.bfloat16
LANES = 128
GROUP = 32
MIB = 1024 * 1024


def split(value):
    high = value.astype(BF16)
    return high, (value - high.astype(F32)).astype(BF16)


def dot(left, right):
    return jnp.dot(left, right, preferred_element_type=F32)


def dot3(left, right):
    (lh, ll), (rh, rl) = left, right
    return dot(lh, rh) + (dot(lh, rl) + dot(ll, rh))


def silu(value):
    return value / (1.0 + jnp.exp(-value))


def vmem():
    return pl.BlockSpec(memory_space=pltpu.VMEM)


def hbm():
    return pl.BlockSpec(memory_space=pltpu.MemorySpace.HBM)


def fetch(sources, places, sems):
    copies = [pltpu.make_async_copy(a, b, sems.at[i]) for i, (a, b) in enumerate(zip(sources, places))]
    for copy in copies:
        copy.start()
    return copies


def shape(dims, dtype=F32):
    return jax.ShapeDtypeStruct(dims, dtype)


def encode_kernel(x_hbm, w_hbm, info_ref, h_ref, p_ref, x_ref, w_ref, sems):
    copies = fetch((x_hbm, w_hbm), (x_ref, w_ref), sems)
    rows, width = x_ref.shape
    n_blocks = rows // BS
    p_ref[:, (n_blocks // 8) * width:] = info_ref[...]
    for copy in copies:
        copy.wait()
    x = x_ref[...]
    h = x + silu(dot3(split(x), split(w_ref[...])))
    h_ref[...] = h
    means = jnp.sum(h.reshape(n_blocks, BS, width), axis=1) * (1.0 / BS)
    for part in range(n_blocks // 8):
        p_ref[:, part * width:(part + 1) * width] = means[part * 8:(part + 1) * 8]


def band_starts(plan):
    band, tile = lax.axis_index("lat"), lax.axis_index("lon")
    starts = []
    for reach, bands in zip(REACHES, plan["bands"]):
        start = band - reach
        if plan["xor"] is not None:
            start = jnp.clip(start, 0, plan["lat"] - bands)
        starts.append(start)
    return band * plan["lon"] + tile, starts


def prepare_kernel(plan, ws_hbm, wn_hbm, wd_hbm, wo_hbm, near_ref, wh_ref, wl_ref, dh_ref, dl_ref, oh_ref, ol_ref, ah_ref, al_ref,
                   w_ref, wd_ref, wo_ref, params, sems):
    width = wd_hbm.shape[0]
    sources, places = [], []
    for layer in range(L):
        sources += [ws_hbm.at[layer], wn_hbm.at[layer]]
        places += [w_ref.at[2 * layer], w_ref.at[2 * layer + 1]]
    copies = fetch(sources + [wd_hbm, wo_hbm], places + [wd_ref, wo_ref], sems)
    rows, nodes = ah_ref.shape
    spread = near_ref.shape[0] // 2
    starts = band_starts(plan)[1]
    params[...] = jnp.zeros_like(params)
    params[:spread] = near_ref[:spread] - (starts[3] * (plan["lon"] * plan["nodes"])).astype(F32)
    params[spread:2 * spread] = near_ref[spread:] / jnp.sum(near_ref[spread:], axis=0, keepdims=True)
    turned = params[...].T
    local, coef = turned[:, :spread], turned[:, spread:2 * spread]
    step = 32
    column = lax.broadcasted_iota(jnp.int32, (step, nodes), 1).astype(F32)
    for at in range(0, rows, step):
        total = jnp.zeros((step, nodes), F32)
        for k in range(spread):
            total = total + jnp.where(column == local[at:at + step, k:k + 1], coef[at:at + step, k:k + 1], 0.0)
        ah_ref[at:at + step], al_ref[at:at + step] = split(total)
    for i in range(2 * L):
        copies[i].wait()
        at = slice((i % 2) * width, (i % 2 + 1) * width)
        wh_ref[i // 2, at], wl_ref[i // 2, at] = split(w_ref[i])
    copies[-2].wait()
    dh_ref[...], dl_ref[...] = split(wd_ref[...])
    copies[-1].wait()
    oh_ref[...], ol_ref[...] = split(wo_ref[...])


def mesh_kernel(plan, *refs):
    n_tables = plan["tables"]
    tables, refs = refs[:n_tables], refs[n_tables:]
    (wh_ref, wl_ref, dh_ref, dl_ref, oh_ref, ol_ref, ah_ref, al_ref, h_ref, t_ref, pred_ref, keep_ref, send_ref,
     th, tl, info, m0f, m0h, m0l, m1f, m1h, m1l, m2h, m2l, pred_buf, sem) = refs
    width = h_ref.shape[1]
    lon, n_blocks, nodes = plan["lon"], plan["blocks"], plan["nodes"]
    k_g2m, k_nbr = plan["k_g2m"], plan["k_nbr"]
    slots = tables[0].shape[0]
    me, (start_b, start0, start1, start2) = band_starts(plan)
    lane = lax.broadcasted_iota(jnp.int32, (8, LANES), 1)
    for c, table in enumerate(tables):
        for i in range(slots):
            if plan["xor"] is None:
                place = i
            else:
                place = me ^ plan["xor"][c * slots + i]
            tile = table[i]
            rows = jnp.concatenate([tile[:, p * width:(p + 1) * width] for p in range(n_blocks // 8)], axis=0)
            at = pl.multiple_of(place * n_blocks, n_blocks)
            th[pl.ds(at, n_blocks), :], tl[pl.ds(at, n_blocks), :] = split(rows)
            info[place] = tile[:, (n_blocks // 8) * width:]

    def band_rows(band, which):
        first = (band - start_b) * lon
        out = []
        for at in range(0, lon * nodes, LANES):
            total = None
            for d in range(LANES // nodes):
                tile = info[first + at // nodes + d]
                if d != which:
                    tile = pltpu.roll(tile, ((d - which) * nodes) % LANES, 1)
                if total is None:
                    total = tile
                else:
                    total = jnp.where(lane >= d * nodes, tile, total)
            out.append(total)
        return jnp.concatenate(out, axis=1)

    def near(band, start, bands, per_band):
        three = min(3, bands)
        low = jnp.clip(band - 1, start, start + bands - three)
        at = pl.multiple_of((low - start) * per_band, per_band)
        return pl.ds(at, three * per_band), (low * per_band).astype(F32)

    per_band, per_band_b = lon * nodes, lon * n_blocks
    row_b = lax.broadcasted_iota(jnp.int32, (min(3, plan["bands"][0]) * per_band_b, per_band), 0).astype(F32)
    for i in range(plan["bands"][1]):
        src, base = near(start0 + i, start_b, plan["bands"][0], per_band_b)
        local = band_rows(start0 + i, 0) - base
        coef = band_rows(start0 + i, 1)
        total = jnp.sum(coef, axis=0, keepdims=True)
        coef = coef / jnp.where(total == 0.0, 1.0, total)
        matrix = jnp.zeros(row_b.shape, F32)
        for k in range(k_g2m):
            matrix = matrix + jnp.where(row_b == local[k:k + 1], coef[k:k + 1], 0.0)
        matrix = matrix.T
        value = dot3(split(matrix), (th[src, :], tl[src, :]))
        at = slice(i * per_band, (i + 1) * per_band)
        m0f[at] = value
        m0h[at], m0l[at] = split(value)

    def mixing(layer, src, src_start, src_bands, out, out_start, out_bands):
        srcf, srch, srcl = src
        row = lax.broadcasted_iota(jnp.int32, (min(3, src_bands) * per_band, per_band), 0).astype(F32)
        for i in range(out_bands):
            band = out_start + i
            rows, base = near(band, src_start, src_bands, per_band)

            local = band_rows(band, 2) - base
            matrix = jnp.zeros(row.shape, F32)
            for k in range(k_nbr):
                matrix = matrix + jnp.where(row == local[k:k + 1], 1.0, 0.0)
            matrix = matrix.T.astype(BF16)
            agg = (dot(matrix, srch[rows, :]) + dot(matrix, srcl[rows, :])) * (1.0 / k_nbr)
            own = srcf[pl.ds(pl.multiple_of((band - src_start) * per_band, per_band), per_band), :]
            center = own - jnp.mean(own, axis=1, keepdims=True)
            nrm = center * (1.0 / jnp.sqrt(jnp.mean(center * center, axis=1, keepdims=True) + 1e-05))
            value = own + silu(dot3(split(jnp.concatenate([nrm, agg], axis=1)), (wh_ref[layer], wl_ref[layer])))
            at = slice(i * per_band, (i + 1) * per_band)
            if out[0] is not None:
                out[0][at] = value
            out[1][at], out[2][at] = split(value)

    _, bands0, bands1, bands2 = plan["bands"]
    mixing(0, (m0f, m0h, m0l), start0, bands0, (m1f, m1h, m1l), start1, bands1)
    mixing(1, (m1f, m1h, m1l), start1, bands1, (None, m2h, m2l), start2, bands2)

    x = h_ref[...] + dot3((ah_ref[...], al_ref[...]), (m2h[...], m2l[...]))
    z = split(silu(dot3(split(x), (dh_ref[...], dl_ref[...]))))
    pred = dot3(z, (oh_ref[...], ol_ref[...]))
    pred_buf[...] = pred
    out = pltpu.make_async_copy(pred_buf, pred_ref, sem)
    out.start()
    target = t_ref[...]
    resid = pred - target
    err = jnp.sum(resid * resid, axis=0, keepdims=True)
    power = jnp.sum(target * target, axis=0, keepdims=True)
    sums = jnp.concatenate([err, power, jnp.zeros((6, err.shape[1]), F32)], axis=0)
    (zh, zl), (rh, rl) = z, split(resid)

    def dot_t(left, right):
        return lax.dot_general(left, right, (((0,), (0,)), ((), ())), preferred_element_type=F32)

    grad = dot_t(zh, rh) + (dot_t(zh, rl) + dot_t(zl, rh))
    half = width // 2
    swap = (me & 1) == 1
    top, bottom = grad[:half], grad[half:]
    keep_ref[:half] = jnp.where(swap, bottom, top)
    send_ref[:half] = jnp.where(swap, top, bottom)
    keep_ref[half:] = sums
    send_ref[half:] = sums
    out.wait()


def flip(value, mask, count):
    return lax.ppermute(value, AXES, [(i, i ^ mask) for i in range(count)])


def pick(value, at):
    return lax.dynamic_index_in_dim(value, at, 0, keepdims=False)


def gather_all(payload, groups, count, beside):
    table = payload[None]
    for group in groups:
        parts = [table] + [flip(table, m, count) for m in group[1:]]
        if group is groups[-1]:
            parts, beside = lax.optimization_barrier((parts, beside))
        table = jnp.concatenate(parts, axis=0)
    return [table, flip(table, 1, count)], beside


def gather_window(payload, reach):
    tiles = lax.all_gather(payload, "lon")
    n_lat = lax.axis_size("lat")
    bands = []
    for off in range(-reach, reach + 1):
        if off == 0:
            bands.append(tiles)
        else:
            pairs = [(i + off, i) for i in range(n_lat) if 0 <= i + off < n_lat]
            bands.append(lax.ppermute(tiles, "lat", pairs))
    return jnp.concatenate(bands, axis=0)


def shards(
    grid_in,
    target,
    w_enc,
    w_mix_self,
    w_mix_nbr,
    w_dec,
    w_out,
    var_weight,
    g2m_idx,
    g2m_w,
    mesh_nbr,
    m2g_idx,
    m2g_w,
):
    n_lat, n_lon = lax.axis_size("lat"), lax.axis_size("lon")
    count = n_lat * n_lon
    rows, width = grid_in.shape
    n_blocks = rows // BS
    nodes = g2m_idx.shape[0]
    k_g2m, k_nbr = g2m_idx.shape[1], mesh_nbr.shape[1]
    n_var = target.shape[1]
    band, tile = lax.axis_index("lat"), lax.axis_index("lon")
    me = band * n_lon + tile
    butterfly = count & (count - 1) == 0 and n_lat <= 9 and count >= 8
    if butterfly:
        bands = [n_lat] + [min(2 * r + 1, n_lat) for r in REACHES[1:]]
        bits = count.bit_length() - 1
        groups = []
        while bits > 1:
            low = max(1, bits - 2)
            groups.append([m << low for m in range(1 << (bits - low))])
            bits = low
        masks = [0]
        for group in groups:
            masks = [a ^ m for m in group for a in masks]
        masks = masks + [m ^ 1 for m in masks]
    else:
        bands = [2 * r + 1 for r in REACHES]
        masks = None
    plan = dict(
        tables=2 if butterfly else 1, xor=masks, bands=bands, lat=n_lat, lon=n_lon,
        blocks=n_blocks, nodes=nodes, k_g2m=k_g2m, k_nbr=k_nbr,
    )
    def place(value, at):
        return jnp.pad(value.T, ((0, 8 - value.shape[1]), (at * nodes, LANES - (at + 1) * nodes)))

    info = (place(g2m_idx, 0) + place(mesh_nbr, 2)).astype(F32) + place(g2m_w, 1)
    wide = (n_blocks // 8) * width + LANES
    h_one, payload = pl.pallas_call(
        encode_kernel,
        out_shape=(shape((rows, width)), shape((8, wide))),
        in_specs=[hbm(), hbm(), vmem()],
        out_specs=(vmem(), vmem()),
        scratch_shapes=[
            pltpu.VMEM(grid_in.shape, F32),
            pltpu.VMEM(w_enc.shape, F32),
            pltpu.SemaphoreType.DMA((2,)),
        ],
        compiler_params=pltpu.CompilerParams(vmem_limit_bytes=53 * MIB),
        name="encode",
    )(grid_in, w_enc, info)

    k_m2g = m2g_idx.shape[1]
    near = jnp.pad(m2g_idx.T, ((0, k_m2g), (0, 0))).astype(F32) + jnp.pad(m2g_w.T, ((k_m2g, 0), (0, 0)))
    n2 = bands[3] * n_lon * nodes
    prepared = pl.pallas_call(
        functools.partial(prepare_kernel, plan),
        out_shape=(
            shape((L, 2 * width, width), BF16),
            shape((L, 2 * width, width), BF16),
            shape((width, width), BF16),
            shape((width, width), BF16),
            shape((width, n_var), BF16),
            shape((width, n_var), BF16),
            shape((rows, n2), BF16),
            shape((rows, n2), BF16),
        ),
        in_specs=[hbm()] * 4 + [vmem()],
        out_specs=[vmem()] * 8,
        scratch_shapes=[
            pltpu.VMEM((2 * L, width, width), F32),
            pltpu.VMEM(w_dec.shape, F32),
            pltpu.VMEM(w_out.shape, F32),
            pltpu.VMEM((LANES, rows), F32),
            pltpu.SemaphoreType.DMA((2 * L + 2,)),
        ],
        compiler_params=pltpu.CompilerParams(vmem_limit_bytes=47 * MIB),
        cost_estimate=pl.CostEstimate(flops=0, bytes_accessed=12 * 1024 * 1024, transcendentals=0),
        name="prepare",
    )(w_mix_self, w_mix_nbr, w_dec, w_out, near)

    if butterfly:
        tables, prepared = gather_all(payload, groups, count, prepared)
    else:
        tables = [gather_window(payload, REACHES[0])]
    nb = bands[0] * n_lon * n_blocks
    n0, n1 = (w * n_lon * nodes for w in bands[1:3])
    half = width // 2
    pred, keep, send = pl.pallas_call(
        functools.partial(mesh_kernel, plan),
        out_shape=(shape((rows, n_var)), shape((half + 8, n_var)), shape((half + 8, n_var))),
        in_specs=[vmem()] * (len(tables) + 10),
        out_specs=[hbm(), vmem(), vmem()],
        scratch_shapes=[
            pltpu.VMEM((nb, width), BF16),
            pltpu.VMEM((nb, width), BF16),
            pltpu.VMEM((bands[0] * n_lon, 8, LANES), F32),
            pltpu.VMEM((n0, width), F32),
            pltpu.VMEM((n0, width), BF16),
            pltpu.VMEM((n0, width), BF16),
            pltpu.VMEM((n1, width), F32),
            pltpu.VMEM((n1, width), BF16),
            pltpu.VMEM((n1, width), BF16),
            pltpu.VMEM((n2, width), BF16),
            pltpu.VMEM((n2, width), BF16),
            pltpu.VMEM((rows, n_var), F32),
            pltpu.SemaphoreType.DMA(()),
        ],
        compiler_params=pltpu.CompilerParams(vmem_limit_bytes=32 * MIB),
        name="mesh",
    )(*tables, *prepared, h_one, target)

    weights = var_weight.astype(F32)
    wsum = jnp.sum(weights)
    grid_total = rows * count

    def factors(sums):
        scale = sums[1] / grid_total + 1e-06
        return sums[0], weights / (scale * grid_total * wsum)

    if not butterfly:
        swap = (me & 1) == 1
        top = jnp.where(swap, send[:half], keep[:half])
        bottom = jnp.where(swap, keep[:half], send[:half])
        total = lax.psum(jnp.concatenate([top, bottom, keep[half:]], axis=0), AXES)
        err, factor = factors(total[width:])
        return (pred, jnp.sum(err * factor), total[:width] * (2.0 * factor)[None, :])

    total = keep + flip(send, 1, count)
    group = groups[-1]
    low = len(group)
    at = (me >> 1) & (low - 1)
    part = half // low
    pieces, sums = total[:half].reshape(low, part, n_var), total[half:]
    total = jnp.concatenate([pick(pieces, at), sums], axis=0)
    for i, received in enumerate(
        [flip(jnp.concatenate([pick(pieces, at ^ i), sums], axis=0), m, count) for i, m in enumerate(group) if m]
    ):
        total = total + received
    for other in groups[-2::-1]:
        received = [flip(total, m, count) for m in other if m]
        for value in received:
            total = total + value
    err, factor = factors(total[part:])
    piece = total[:part] * (2.0 * factor)[None, :]
    pieces = jnp.stack([piece] + [flip(piece, m, count) for m in group if m])
    own = jnp.concatenate([pick(pieces, at ^ i) for i in range(low)], axis=0)
    other = flip(own, 1, count)
    swap = (me & 1) == 1
    grad_out = jnp.concatenate([jnp.where(swap, other, own), jnp.where(swap, own, other)], axis=0)
    return (pred, jnp.sum(err * factor), grad_out)


def solution(mesh):
    placed = (
        P(AXES, None),
        P(AXES, None),
        P(),
        P(),
        P(),
        P(),
        P(),
        P(),
        P(AXES, None),
        P(AXES, None),
        P(AXES, None),
        P(AXES, None),
        P(AXES, None),
    )
    return jax.shard_map(
        shards,
        mesh=mesh,
        in_specs=placed,
        out_specs=(P(AXES, None), P(), P()),
        check_vma=False,
    )
```

time: 84.8 us -> 60.1 us (0.71)
  Pallas kernels: 30.9 us -> 14.4 us
  local copies, waits for them, and re-layouts: 5.72 us -> 0.12 us
  other arithmetic: 5.21 us -> 3.68 us
    pallas_call x1, Pallas kernels: 21.5 us -> 9.65 us  [shards(): pl.pallas_call(functools.partial(mesh_kernel, plan), out_shape=(shape((ro...]
    pallas_call x1, Pallas kernels: 6.59 us -> 2.58 us  [shards(): pl.pallas_call(functools.partial(prepare_kernel, plan), out_shape=(shape(...]
    unnamed x19 -> x11, local copies, waits for them, and re-layouts: 4.06 us -> 0.05 us
    add x0 -> x2, other arithmetic: none -> 1.61 us  [the longest x1 0.9 us: shards(): (place(g2m_idx, 0) + place(mesh_nbr, 2)).astype(F32) + place(g2m_w, 1)]
    convert_element_type x2 -> x0, other arithmetic: 1.39 us -> none  [the longest x1 0.7 us: shards(): g2m_idx.astype(F32)]
    add x1, other arithmetic: 0.92 us -> 0.02 us  [shards(): total = keep + flip(send, 1, count)]
  transfers between devices with their start and end apart: 18 -> 18, of which waited for: 12 -> 12; matrix products, arithmetic and copies ran while one was open for 5% -> 3% of each run, Pallas kernels for 8% -> 4%
where the time goes in v2:
time: 60.1 us; the launch traced here: 59.8 us
  starting transfers between devices  21.1 us (35%)
  waiting for transfers between devices  19 us (32%)
  Pallas kernels  14.4 us (24%)
  other arithmetic  3.68 us (6%)
  between operations  1.5 us (2%)
    ppermute x18, starting transfers between devices, flip(): return lax.ppermute(value, AXES, [(i, i ^ mask) for i in range(count)])  21.1 us
    ppermute x18, waiting for transfers between devices, flip(): return lax.ppermute(value, AXES, [(i, i ^ mask) for i in range(count)])  19 us
    pallas_call x1, Pallas kernels, shards(): pl.pallas_call(functools.partial(mesh_kernel, plan), out_shape=(shape((ro...  9.65 us
    pallas_call x1, Pallas kernels, shards(): pl.pallas_call(functools.partial(prepare_kernel, plan), out_shape=(shape(...  2.58 us
    pallas_call x1, Pallas kernels, shards(): pl.pallas_call(encode_kernel, out_shape=(shape((rows, width)), shape((8,...  2.15 us
  transfers between devices with their start and end apart: 18, of which 12 were waited for; matrix products, arithmetic and copies ran while one was open for 3% of the time, Pallas kernels for 4%

profile of v2, /device:TPU:0, one launch (start us, length us, event | category | flops | bytes accessed | tf_op | source)
XLA Modules:
  0.0 59.8 jit_solution(9322947106580774994)
XLA Ops:
  0.7 0.9 %pad_add_fusion.1.info_ref = f32[8,128]{1,0:T(8,128)S(1)} fusion(f32[8,32]{1,0:T(8,128)} %bitcast.47, s32[6,32]{1,0:T(8,128)} %bitcast.48, s32[8,32]{1,0:T(8,128)} %bitcast.49), kind=kLoop, calls=%fused_computation.28 | loop fusion | flops 3072 | bytes 6912 | tf_op jit(solution)/shard_map/add | solution.py:310
  1.5 2.1 %encode.1 = (f32[256,512]{1,0:T(8,128)S(1)}, f32[8,1152]{1,0:T(8,128)S(1)}) custom-call(f32[256,512]{1,0:T(8,128)} %x_hbm.1, f32[512,512]{1,0:T(8,128)} %w_hbm.1, f32[8,128]{1,0:T(8,128)S(1)} %pad_add_fusion.1.info_ref), custom_call_target="tpu_custom_call" | custom-call | tf_op jit(solution)/shard_map/encode/pallas_call | solution.py:312
  3.7 3.1 %collective-permute-start = (f32[1,8,1152]{2,1,0:T(8,128)S(1)}, f32[1,8,1152]{2,1,0:T(8,128)S(1)}, u32[]{:S(2)}, u32[]{:S(2)}) collective-permute-start(f32[1,8,1152]{2,1,0:T(8,128)S(1)} %bitcast.39), channel_id=1, source_target_pairs={{0,8},{1,9},{2,10},{3,11},{4,12},{5,13},{6,14},{7,15},{8,0},{9,1},... | collective-permute-start | bytes 110600 | tf_op jit(solution)/shard_map/ppermute | solution.py:233
  6.8 2.6 %collective-permute-start.1 = (f32[1,8,1152]{2,1,0:T(8,128)S(1)}, f32[1,8,1152]{2,1,0:T(8,128)S(1)}, u32[]{:S(2)}, u32[]{:S(2)}) collective-permute-start(f32[1,8,1152]{2,1,0:T(8,128)S(1)} %bitcast.40), channel_id=1, source_target_pairs={{0,16},{1,17},{2,18},{3,19},{4,20},{5,21},{6,22},{7,23},{8,24},{9,... | collective-permute-start | bytes 110600 | tf_op jit(solution)/shard_map/ppermute | solution.py:233
  9.4 2.9 %collective-permute-done.1 = f32[1,8,1152]{2,1,0:T(8,128)S(1)} collective-permute-done((f32[1,8,1152]{2,1,0:T(8,128)S(1)}, f32[1,8,1152]{2,1,0:T(8,128)S(1)}, u32[]{:S(2)}, u32[]{:S(2)}) %collective-permute-start.1) | collective-permute-done | bytes 36896 | tf_op jit(solution)/shard_map/ppermute | solution.py:233
  12.3 2.8 %collective-permute-done.2 = f32[1,8,1152]{2,1,0:T(8,128)S(1)} collective-permute-done((f32[1,8,1152]{2,1,0:T(8,128)S(1)}, f32[1,8,1152]{2,1,0:T(8,128)S(1)}, u32[]{:S(2)}, u32[]{:S(2)}) %collective-permute-start.2) | collective-permute-done | bytes 36896 | tf_op jit(solution)/shard_map/ppermute | solution.py:233
  15.2 1.6 %collective-permute-start.3 = (f32[4,8,1152]{2,1,0:T(8,128)S(1)}, f32[4,8,1152]{2,1,0:T(8,128)S(1)}, u32[]{:S(2)}, u32[]{:S(2)}) collective-permute-start(f32[4,8,1152]{2,1,0:T(8,128)S(1)} %pad_maximum_fusion.1), channel_id=1, source_target_pairs={{0,2},{1,3},{2,0},{3,1},{4,6},{5,7},{6,4},{7,5},{8,10},{9,11},{10,... | collective-permute-start | bytes 442376 | tf_op jit(solution)/shard_map/ppermute | solution.py:233
  16.7 1.5 %collective-permute-start.4 = (f32[4,8,1152]{2,1,0:T(8,128)S(1)}, f32[4,8,1152]{2,1,0:T(8,128)S(1)}, u32[]{:S(2)}, u32[]{:S(2)}) collective-permute-start(f32[4,8,1152]{2,1,0:T(8,128)S(1)} %pad_maximum_fusion.1), channel_id=1, source_target_pairs={{0,4},{1,5},{2,6},{3,7},{4,0},{5,1},{6,2},{7,3},{8,12},{9,13},{10,... | collective-permute-start | bytes 442376 | tf_op jit(solution)/shard_map/ppermute | solution.py:233
  18.2 0.5 collective-permute-start.5
  18.7 0.7 %pad_add_fusion.near_ref = f32[8,256]{1,0:T(8,128)S(1)} fusion(f32[4,256]{1,0:T(4,128)} %bitcast.50, s32[4,256]{1,0:T(4,128)} %bitcast.51), kind=kLoop, calls=%fused_computation.27 | loop fusion | flops 4096 | bytes 16384 | tf_op jit(solution)/shard_map/add | solution.py:327
  19.4 2.6 %prepare.1 = (bf16[2,1024,512]{2,1,0:T(8,128)(2,1)S(1)}, bf16[2,1024,512]{2,1,0:T(8,128)(2,1)S(1)}, bf16[512,512]{1,0:T(8,128)(2,1)S(1)}, bf16[512,512]{1,0:T(8,...) custom-call(f32[2,512,512]{2,1,0:T(8,128)} %ws_hbm.1, ...), custom_call_target="tpu_custom_call" | custom-call | bytes 12582912 | tf_op jit(solution)/shard_map/prepare/pallas_call | solution.py:329
  22.0 2.4 %collective-permute-done.4 = f32[4,8,1152]{2,1,0:T(8,128)S(1)} collective-permute-done((f32[4,8,1152]{2,1,0:T(8,128)S(1)}, f32[4,8,1152]{2,1,0:T(8,128)S(1)}, u32[]{:S(2)}, u32[]{:S(2)}) %collective-permute-start.4) | collective-permute-done | bytes 147488 | tf_op jit(solution)/shard_map/ppermute | solution.py:233
  24.6 2.0 %collective-permute-done.6.refs_1_ = f32[16,8,1152]{2,1,0:T(8,128)S(1)} collective-permute-done((f32[16,8,1152]{2,1,0:T(8,128)S(1)}, f32[16,8,1152]{2,1,0:T(8,128)S(1)}, u32[]{:S(2)}, u32[]{:S(2)}) %collective-permute-start.6) | collective-permute-done | bytes 589856 | tf_op jit(solution)/shard_map/ppermute | solution.py:233
  26.6 9.7 %mesh.1 = (f32[256,128]{1,0:T(8,128)}, f32[264,128]{1,0:T(8,128)S(1)}, f32[264,128]{1,0:T(8,128)S(1)}) custom-call(f32[16,8,1152]{2,1,0:T(8,128)S(1)} %constant_dynamic-update-slice_fusion.refs_0_, f32[16,8,1152]{2,1,0:T(8,128)S(1)} %collective-permute-done.6.refs_1_, bf16[2,1024,512]{2,1,0:T(8,128)(2,1)S(1)} %get-tuple-element.41.refs_2_, ...), custom_call_target="tpu_custom_call" | custom-call | tf_op jit(solution)/shard_map/mesh/pallas_call | solution.py:362
  36.4 1.2 %collective-permute-done.7 = f32[264,128]{1,0:T(8,128)S(1)} collective-permute-done((f32[264,128]{1,0:T(8,128)S(1)}, f32[264,128]{1,0:T(8,128)S(1)}, u32[]{:S(2)}, u32[]{:S(2)}) %collective-permute-start.7) | collective-permute-done | bytes 135200 | tf_op jit(solution)/shard_map/ppermute | solution.py:233
  37.7 0.7 %collective-permute-start.10 = (f32[72,128]{1,0:T(8,128)S(1)}, f32[72,128]{1,0:T(8,128)S(1)}, u32[]{:S(2)}, u32[]{:S(2)}) collective-permute-start(f32[72,128]{1,0:T(8,128)S(1)} %get-tuple-element.67), channel_id=1, source_target_pairs={{0,6},{1,7},{2,4},{3,5},{4,2},{5,3},{6,0},{7,1},{8,14},{9,15},{10,... | collective-permute-start | bytes 110600 | tf_op jit(solution)/shard_map/ppermute | solution.py:233
  38.5 1.8 %collective-permute-start.8 = (f32[72,128]{1,0:T(8,128)S(1)}, f32[72,128]{1,0:T(8,128)S(1)}, u32[]{:S(2)}, u32[]{:S(2)}) collective-permute-start(f32[72,128]{1,0:T(8,128)S(1)} %get-tuple-element.65), channel_id=1, source_target_pairs={{0,2},{1,3},{2,0},{3,1},{4,6},{5,7},{6,4},{7,5},{8,10},{9,11},{10,... | collective-permute-start | bytes 110600 | tf_op jit(solution)/shard_map/ppermute | solution.py:233
  40.3 1.0 %collective-permute-start.9 = (f32[72,128]{1,0:T(8,128)S(1)}, f32[72,128]{1,0:T(8,128)S(1)}, u32[]{:S(2)}, u32[]{:S(2)}) collective-permute-start(f32[72,128]{1,0:T(8,128)S(1)} %get-tuple-element.66), channel_id=1, source_target_pairs={{0,4},{1,5},{2,6},{3,7},{4,0},{5,1},{6,2},{7,3},{8,12},{9,13},{10,... | collective-permute-start | bytes 110600 | tf_op jit(solution)/shard_map/ppermute | solution.py:233
  41.3 1.4 %collective-permute-done.10 = f32[72,128]{1,0:T(8,128)S(1)} collective-permute-done((f32[72,128]{1,0:T(8,128)S(1)}, f32[72,128]{1,0:T(8,128)S(1)}, u32[]{:S(2)}, u32[]{:S(2)}) %collective-permute-start.10) | collective-permute-done | bytes 36896 | tf_op jit(solution)/shard_map/ppermute | solution.py:233
  42.7 1.6 %collective-permute-done.9 = f32[72,128]{1,0:T(8,128)S(1)} collective-permute-done((f32[72,128]{1,0:T(8,128)S(1)}, f32[72,128]{1,0:T(8,128)S(1)}, u32[]{:S(2)}, u32[]{:S(2)}) %collective-permute-start.9) | collective-permute-done | bytes 36896 | tf_op jit(solution)/shard_map/ppermute | solution.py:233
  44.3 1.2 %collective-permute-start.12 = (f32[72,128]{1,0:T(8,128)S(1)}, f32[72,128]{1,0:T(8,128)S(1)}, u32[]{:S(2)}, u32[]{:S(2)}) collective-permute-start(f32[72,128]{1,0:T(8,128)S(1)} %fusion.2), channel_id=1, source_target_pairs={{0,16},{1,17},{2,18},{3,19},{4,20},{5,21},{6,22},{7,23},{8,24},{9,... | collective-permute-start | bytes 110600 | tf_op jit(solution)/shard_map/ppermute | solution.py:233
  45.5 3.2 %collective-permute-start.13 = (f32[72,128]{1,0:T(8,128)S(1)}, f32[72,128]{1,0:T(8,128)S(1)}, u32[]{:S(2)}, u32[]{:S(2)}) collective-permute-start(f32[72,128]{1,0:T(8,128)S(1)} %fusion.2), channel_id=1, source_target_pairs={{0,24},{1,25},{2,26},{3,27},{4,28},{5,29},{6,30},{7,31},{8,16},{9,... | collective-permute-start | bytes 110600 | tf_op jit(solution)/shard_map/ppermute | solution.py:233
  48.7 0.6 %convert_reduce_fusion = f32[]{:T(128)} fusion(s32[128]{0:T(128)S(1)} %copy-done.3), kind=kLoop, calls=%fused_computation.37 | loop fusion | flops 255 | bytes 516 | tf_op jit(solution)/shard_map/reduce_sum | solution.py:387
  50.0 1.3 %collective-permute-done.13 = f32[72,128]{1,0:T(8,128)S(1)} collective-permute-done((f32[72,128]{1,0:T(8,128)S(1)}, f32[72,128]{1,0:T(8,128)S(1)}, u32[]{:S(2)}, u32[]{:S(2)}) %collective-permute-start.13) | collective-permute-done | bytes 36896 | tf_op jit(solution)/shard_map/ppermute | solution.py:233
  51.3 0.3 collective-permute-start.14
  51.6 1.2 %collective-permute-start.15 = (f32[64,128]{1,0:T(8,128)S(1)}, f32[64,128]{1,0:T(8,128)S(1)}, u32[]{:S(2)}, u32[]{:S(2)}) collective-permute-start(f32[64,128]{1,0:T(8,128)S(1)} %slice_multiply_fusion), channel_id=1, source_target_pairs={{0,4},{1,5},{2,6},{3,7},{4,0},{5,1},{6,2},{7,3},{8,12},{9,13},{10,... | collective-permute-start | bytes 98312 | tf_op jit(solution)/shard_map/ppermute | solution.py:233
  52.8 2.1 %collective-permute-start.16 = (f32[64,128]{1,0:T(8,128)S(1)}, f32[64,128]{1,0:T(8,128)S(1)}, u32[]{:S(2)}, u32[]{:S(2)}) collective-permute-start(f32[64,128]{1,0:T(8,128)S(1)} %slice_multiply_fusion), channel_id=1, source_target_pairs={{0,6},{1,7},{2,4},{3,5},{4,2},{5,3},{6,0},{7,1},{8,14},{9,15},{10,... | collective-permute-start | bytes 98312 | tf_op jit(solution)/shard_map/ppermute | solution.py:233
  54.8 0.4 collective-permute-done.14
  55.5 2.1 %collective-permute-done.16 = f32[64,128]{1,0:T(8,128)S(1)} collective-permute-done((f32[64,128]{1,0:T(8,128)S(1)}, f32[64,128]{1,0:T(8,128)S(1)}, u32[]{:S(2)}, u32[]{:S(2)}) %collective-permute-start.16) | collective-permute-done | bytes 32800 | tf_op jit(solution)/shard_map/ppermute | solution.py:233
  57.7 0.6 %fusion.8 = f32[]{:T(128)} fusion(f32[128]{0:T(128)S(1)} %get-tuple-element.54, f32[72,128]{1,0:T(8,128)S(1)} %add_add_fusion), kind=kLoop, calls=%fused_computation.36 | loop fusion | flops 255 | bytes 1028 | tf_op jit(solution)/shard_map/reduce_sum | solution.py:424
  58.3 0.7 %collective-permute-done.17 = f32[256,128]{1,0:T(8,128)S(1)} collective-permute-done((f32[256,128]{1,0:T(8,128)S(1)}, f32[256,128]{1,0:T(8,128)S(1)}, u32[]{:S(2)}, u32[]{:S(2)}) %collective-permute-start.17) | collective-permute-done | bytes 131104 | tf_op jit(solution)/shard_map/ppermute | solution.py:233
  59.1 0.7 %pad_maximum_fusion = f32[512,128]{1,0:T(8,128)} fusion(f32[256,128]{1,0:T(8,128)S(1)} %get-tuple-element.56, f32[256,128]{1,0:T(8,128)S(1)} %get-tuple-element.55), kind=kLoop, calls=%fused_computation | loop fusion | flops 65536 | bytes 524288 | tf_op jit(solution)/shard_map/concatenate | solution.py:423
  (39 shorter events, 0.9 us)
Async XLA Ops:
  0.6 18.8 %copy-start = (f32[512,512]{1,0:T(8,128)S(1)}, f32[512,512]{1,0:T(8,128)}, u32[]{:S(2)}) copy-start(f32[512,512]{1,0:T(8,128)} %wd_hbm.1) | copy-start | bytes 3145732
  0.6 18.8 %copy-start.1 = (f32[512,128]{1,0:T(8,128)S(1)}, f32[512,128]{1,0:T(8,128)}, u32[]{:S(2)}) copy-start(f32[512,128]{1,0:T(8,128)} %wo_hbm.1) | copy-start | bytes 786436
  3.7 5.7 %collective-permute-start = (f32[1,8,1152]{2,1,0:T(8,128)S(1)}, f32[1,8,1152]{2,1,0:T(8,128)S(1)}, u32[]{:S(2)}, u32[]{:S(2)}) collective-permute-start(f32[1,8,1152]{2,1,0:T(8,128)S(1)} %bitcast.39), channel_id=1, source_target_pairs={{0,8},{1,9},{2,10},{3,11},{4,12},{5,13},{6,14},{7,15},{8,0},{9,1},... | collective-permute-start | bytes 110600 | tf_op jit(solution)/shard_map/ppermute | solution.py:233
  6.8 5.5 %collective-permute-start.1 = (f32[1,8,1152]{2,1,0:T(8,128)S(1)}, f32[1,8,1152]{2,1,0:T(8,128)S(1)}, u32[]{:S(2)}, u32[]{:S(2)}) collective-permute-start(f32[1,8,1152]{2,1,0:T(8,128)S(1)} %bitcast.40), channel_id=1, source_target_pairs={{0,16},{1,17},{2,18},{3,19},{4,20},{5,21},{6,22},{7,23},{8,24},{9,... | collective-permute-start | bytes 110600 | tf_op jit(solution)/shard_map/ppermute | solution.py:233
  9.4 5.8 %collective-permute-start.2 = (f32[1,8,1152]{2,1,0:T(8,128)S(1)}, f32[1,8,1152]{2,1,0:T(8,128)S(1)}, u32[]{:S(2)}, u32[]{:S(2)}) collective-permute-start(f32[1,8,1152]{2,1,0:T(8,128)S(1)} %bitcast.41), channel_id=1, source_target_pairs={{0,24},{1,25},{2,26},{3,27},{4,28},{5,29},{6,30},{7,31},{8,16},{9,... | collective-permute-start | bytes 110600 | tf_op jit(solution)/shard_map/ppermute | solution.py:233
  15.2 6.9 %collective-permute-start.3 = (f32[4,8,1152]{2,1,0:T(8,128)S(1)}, f32[4,8,1152]{2,1,0:T(8,128)S(1)}, u32[]{:S(2)}, u32[]{:S(2)}) collective-permute-start(f32[4,8,1152]{2,1,0:T(8,128)S(1)} %pad_maximum_fusion.1), channel_id=1, source_target_pairs={{0,2},{1,3},{2,0},{3,1},{4,6},{5,7},{6,4},{7,5},{8,10},{9,11},{10,... | collective-permute-start | bytes 442376 | tf_op jit(solution)/shard_map/ppermute | solution.py:233
  16.7 7.7 %collective-permute-start.4 = (f32[4,8,1152]{2,1,0:T(8,128)S(1)}, f32[4,8,1152]{2,1,0:T(8,128)S(1)}, u32[]{:S(2)}, u32[]{:S(2)}) collective-permute-start(f32[4,8,1152]{2,1,0:T(8,128)S(1)} %pad_maximum_fusion.1), channel_id=1, source_target_pairs={{0,4},{1,5},{2,6},{3,7},{4,0},{5,1},{6,2},{7,3},{8,12},{9,13},{10,... | collective-permute-start | bytes 442376 | tf_op jit(solution)/shard_map/ppermute | solution.py:233
  18.2 6.2 %collective-permute-start.5 = (f32[4,8,1152]{2,1,0:T(8,128)S(1)}, f32[4,8,1152]{2,1,0:T(8,128)S(1)}, u32[]{:S(2)}, u32[]{:S(2)}) collective-permute-start(f32[4,8,1152]{2,1,0:T(8,128)S(1)} %pad_maximum_fusion.1), channel_id=1, source_target_pairs={{0,6},{1,7},{2,4},{3,5},{4,2},{5,3},{6,0},{7,1},{8,14},{9,15},{10,... | collective-permute-start | bytes 442376 | tf_op jit(solution)/shard_map/ppermute | solution.py:233
  19.4 7.1 %copy-start.2 = (f32[256,128]{1,0:T(8,128)S(1)}, f32[256,128]{1,0:T(8,128)}, u32[]{:S(2)}) copy-start(f32[256,128]{1,0:T(8,128)} %refs_11_.1) | copy-start | bytes 393220
  24.5 2.1 %collective-permute-start.6 = (f32[16,8,1152]{2,1,0:T(8,128)S(1)}, f32[16,8,1152]{2,1,0:T(8,128)S(1)}, u32[]{:S(2)}, u32[]{:S(2)}) collective-permute-start(f32[16,8,1152]{2,1,0:T(8,128)S(1)} %constant_dynamic-update-slice_fusion.refs_0_), channel_id=1, source_target_pairs={{0,1},{1,0},{2,3},{3,2},{4,5},{5,4},{6,7},{7,6},{8,9},{9,8},{10,11... | collective-permute-start | bytes 1769480 | tf_op jit(solution)/shard_map/ppermute | solution.py:233
  26.6 22.1 %copy-start.3 = (s32[128]{0:T(128)S(1)}, s32[128]{0:T(128)}, u32[]{:S(2)}) copy-start(s32[128]{0:T(128)} %param.20) | copy-start | bytes 1540
  36.2 1.4 %collective-permute-start.7 = (f32[264,128]{1,0:T(8,128)S(1)}, f32[264,128]{1,0:T(8,128)S(1)}, u32[]{:S(2)}, u32[]{:S(2)}) collective-permute-start(f32[264,128]{1,0:T(8,128)S(1)} %get-tuple-element.52), channel_id=1, source_target_pairs={{0,1},{1,0},{2,3},{3,2},{4,5},{5,4},{6,7},{7,6},{8,9},{9,8},{10,11... | collective-permute-start | bytes 405512 | tf_op jit(solution)/shard_map/ppermute | solution.py:233
  37.7 4.9 %collective-permute-start.10 = (f32[72,128]{1,0:T(8,128)S(1)}, f32[72,128]{1,0:T(8,128)S(1)}, u32[]{:S(2)}, u32[]{:S(2)}) collective-permute-start(f32[72,128]{1,0:T(8,128)S(1)} %get-tuple-element.67), channel_id=1, source_target_pairs={{0,6},{1,7},{2,4},{3,5},{4,2},{5,3},{6,0},{7,1},{8,14},{9,15},{10,... | collective-permute-start | bytes 110600 | tf_op jit(solution)/shard_map/ppermute | solution.py:233
  38.5 4.2 %collective-permute-start.8 = (f32[72,128]{1,0:T(8,128)S(1)}, f32[72,128]{1,0:T(8,128)S(1)}, u32[]{:S(2)}, u32[]{:S(2)}) collective-permute-start(f32[72,128]{1,0:T(8,128)S(1)} %get-tuple-element.65), channel_id=1, source_target_pairs={{0,2},{1,3},{2,0},{3,1},{4,6},{5,7},{6,4},{7,5},{8,10},{9,11},{10,... | collective-permute-start | bytes 110600 | tf_op jit(solution)/shard_map/ppermute | solution.py:233
  40.3 4.0 %collective-permute-start.9 = (f32[72,128]{1,0:T(8,128)S(1)}, f32[72,128]{1,0:T(8,128)S(1)}, u32[]{:S(2)}, u32[]{:S(2)}) collective-permute-start(f32[72,128]{1,0:T(8,128)S(1)} %get-tuple-element.66), channel_id=1, source_target_pairs={{0,4},{1,5},{2,6},{3,7},{4,0},{5,1},{6,2},{7,3},{8,12},{9,13},{10,... | collective-permute-start | bytes 110600 | tf_op jit(solution)/shard_map/ppermute | solution.py:233
  44.2 5.7 %collective-permute-start.11 = (f32[72,128]{1,0:T(8,128)S(1)}, f32[72,128]{1,0:T(8,128)S(1)}, u32[]{:S(2)}, u32[]{:S(2)}) collective-permute-start(f32[72,128]{1,0:T(8,128)S(1)} %fusion.2), channel_id=1, source_target_pairs={{0,8},{1,9},{2,10},{3,11},{4,12},{5,13},{6,14},{7,15},{8,0},{9,1},... | collective-permute-start | bytes 110600 | tf_op jit(solution)/shard_map/ppermute | solution.py:233
  44.3 5.6 %collective-permute-start.12 = (f32[72,128]{1,0:T(8,128)S(1)}, f32[72,128]{1,0:T(8,128)S(1)}, u32[]{:S(2)}, u32[]{:S(2)}) collective-permute-start(f32[72,128]{1,0:T(8,128)S(1)} %fusion.2), channel_id=1, source_target_pairs={{0,16},{1,17},{2,18},{3,19},{4,20},{5,21},{6,22},{7,23},{8,24},{9,... | collective-permute-start | bytes 110600 | tf_op jit(solution)/shard_map/ppermute | solution.py:233
  45.5 5.8 %collective-permute-start.13 = (f32[72,128]{1,0:T(8,128)S(1)}, f32[72,128]{1,0:T(8,128)S(1)}, u32[]{:S(2)}, u32[]{:S(2)}) collective-permute-start(f32[72,128]{1,0:T(8,128)S(1)} %fusion.2), channel_id=1, source_target_pairs={{0,24},{1,25},{2,26},{3,27},{4,28},{5,29},{6,30},{7,31},{8,16},{9,... | collective-permute-start | bytes 110600 | tf_op jit(solution)/shard_map/ppermute | solution.py:233
  51.3 4.0 %collective-permute-start.14 = (f32[64,128]{1,0:T(8,128)S(1)}, f32[64,128]{1,0:T(8,128)S(1)}, u32[]{:S(2)}, u32[]{:S(2)}) collective-permute-start(f32[64,128]{1,0:T(8,128)S(1)} %slice_multiply_fusion), channel_id=1, source_target_pairs={{0,2},{1,3},{2,0},{3,1},{4,6},{5,7},{6,4},{7,5},{8,10},{9,11},{10,... | collective-permute-start | bytes 98312 | tf_op jit(solution)/shard_map/ppermute | solution.py:233
  51.6 3.9 %collective-permute-start.15 = (f32[64,128]{1,0:T(8,128)S(1)}, f32[64,128]{1,0:T(8,128)S(1)}, u32[]{:S(2)}, u32[]{:S(2)}) collective-permute-start(f32[64,128]{1,0:T(8,128)S(1)} %slice_multiply_fusion), channel_id=1, source_target_pairs={{0,4},{1,5},{2,6},{3,7},{4,0},{5,1},{6,2},{7,3},{8,12},{9,13},{10,... | collective-permute-start | bytes 98312 | tf_op jit(solution)/shard_map/ppermute | solution.py:233
  52.8 4.8 %collective-permute-start.16 = (f32[64,128]{1,0:T(8,128)S(1)}, f32[64,128]{1,0:T(8,128)S(1)}, u32[]{:S(2)}, u32[]{:S(2)}) collective-permute-start(f32[64,128]{1,0:T(8,128)S(1)} %slice_multiply_fusion), channel_id=1, source_target_pairs={{0,6},{1,7},{2,4},{3,5},{4,2},{5,3},{6,0},{7,1},{8,14},{9,15},{10,... | collective-permute-start | bytes 98312 | tf_op jit(solution)/shard_map/ppermute | solution.py:233
  57.6 1.4 %collective-permute-start.17 = (f32[256,128]{1,0:T(8,128)S(1)}, f32[256,128]{1,0:T(8,128)S(1)}, u32[]{:S(2)}, u32[]{:S(2)}) collective-permute-start(f32[256,128]{1,0:T(8,128)S(1)} %pad_maximum_fusion.3), channel_id=1, source_target_pairs={{0,1},{1,0},{2,3},{3,2},{4,5},{5,4},{6,7},{7,6},{8,9},{9,8},{10,11... | collective-permute-start | bytes 393224 | tf_op jit(solution)/shard_map/ppermute | solution.py:233

commit v3 on v2

--- a/solution.py
+++ b/solution.py
@@ -16,6 +16,9 @@
 LANES = 128
 GROUP = 32
 MIB = 1024 * 1024
+AHEAD = 1
+DENSE = (1, 1)
+CHUNKS = 2
 
 
 def split(value):
@@ -55,19 +58,40 @@
     return jax.ShapeDtypeStruct(dims, dtype)
 
 
-def encode_kernel(x_hbm, w_hbm, info_ref, h_ref, p_ref, x_ref, w_ref, sems):
-    copies = fetch((x_hbm, w_hbm), (x_ref, w_ref), sems)
+def encode_kernel(x_hbm, w_hbm, h_ref, p_ref, x_ref, w_ref, sems):
     rows, width = x_ref.shape
     n_blocks = rows // BS
-    p_ref[:, (n_blocks // 8) * width:] = info_ref[...]
-    for copy in copies:
-        copy.wait()
+    part = width // CHUNKS
+    sources = [x_hbm] + [w_hbm.at[pl.ds(i * part, part), :] for i in range(CHUNKS)]
+    places = [x_ref] + [w_ref.at[pl.ds(i * part, part), :] for i in range(CHUNKS)]
+    copies = fetch(sources, places, sems)
+    copies[0].wait()
     x = x_ref[...]
-    h = x + silu(dot3(split(x), split(w_ref[...])))
+    high, low = split(x)
+    total = jnp.zeros(x.shape, F32)
+    for i in range(CHUNKS):
+        copies[1 + i].wait()
+        at = slice(i * part, (i + 1) * part)
+        total = total + dot3((high[:, at], low[:, at]), split(w_ref[at]))
+    h = x + silu(total)
     h_ref[...] = h
     means = jnp.sum(h.reshape(n_blocks, BS, width), axis=1) * (1.0 / BS)
-    for part in range(n_blocks // 8):
-        p_ref[:, part * width:(part + 1) * width] = means[part * 8:(part + 1) * 8]
+    for i in range(n_blocks // 8):
+        p_ref[:, i * width:(i + 1) * width] = means[i * 8:(i + 1) * 8]
+
+
+def pack_kernel(m_ref, gi_ref, gw_ref, ni_ref, p_ref, params):
+    spread, nodes = gi_ref.shape
+    params[...] = jnp.zeros_like(params)
+    params[:spread, :nodes] = gi_ref[...].astype(F32)
+    params[8:8 + spread, :nodes] = gw_ref[...]
+    params[16:16 + ni_ref.shape[0], :nodes] = ni_ref[...].astype(F32)
+    tile = params[:8]
+    for i in (1, 2):
+        tile = tile + pltpu.roll(params[8 * i:8 * i + 8], i * nodes, 1)
+    wide = m_ref.shape[1]
+    p_ref[:, :wide] = m_ref[...]
+    p_ref[:, wide:] = tile
 
 
 def band_starts(plan):
@@ -118,7 +142,7 @@
     n_tables = plan["tables"]
     tables, refs = refs[:n_tables], refs[n_tables:]
     (wh_ref, wl_ref, dh_ref, dl_ref, oh_ref, ol_ref, ah_ref, al_ref, h_ref, t_ref, pred_ref, keep_ref, send_ref,
-     th, tl, info, m0f, m0h, m0l, m1f, m1h, m1l, m2h, m2l, pred_buf, sem) = refs
+     th, tl, info, m0f, m0h, m0l, m1f, m1h, m1l, m2h, m2l, xh, xl, pred_buf, sem) = refs
     width = h_ref.shape[1]
     lon, n_blocks, nodes = plan["lon"], plan["blocks"], plan["nodes"]
     k_g2m, k_nbr = plan["k_g2m"], plan["k_nbr"]
@@ -160,47 +184,83 @@
         return pl.ds(at, three * per_band), (low * per_band).astype(F32)
 
     per_band, per_band_b = lon * nodes, lon * n_blocks
-    row_b = lax.broadcasted_iota(jnp.int32, (min(3, plan["bands"][0]) * per_band_b, per_band), 0).astype(F32)
-    for i in range(plan["bands"][1]):
+    steps = []
+
+    def to_mesh(i):
         src, base = near(start0 + i, start_b, plan["bands"][0], per_band_b)
-        local = band_rows(start0 + i, 0) - base
-        coef = band_rows(start0 + i, 1)
-        total = jnp.sum(coef, axis=0, keepdims=True)
-        coef = coef / jnp.where(total == 0.0, 1.0, total)
-        matrix = jnp.zeros(row_b.shape, F32)
-        for k in range(k_g2m):
-            matrix = matrix + jnp.where(row_b == local[k:k + 1], coef[k:k + 1], 0.0)
-        matrix = matrix.T
-        value = dot3(split(matrix), (th[src, :], tl[src, :]))
-        at = slice(i * per_band, (i + 1) * per_band)
-        m0f[at] = value
-        m0h[at], m0l[at] = split(value)
-
-    def mixing(layer, src, src_start, src_bands, out, out_start, out_bands):
+
+        def build():
+            row = lax.broadcasted_iota(jnp.int32, (min(3, plan["bands"][0]) * per_band_b, per_band), 0).astype(F32)
+            local = band_rows(start0 + i, 0) - base
+            coef = band_rows(start0 + i, 1)
+            total = jnp.sum(coef, axis=0, keepdims=True)
+            coef = coef / jnp.where(total == 0.0, 1.0, total)
+            matrix = jnp.zeros(row.shape, F32)
+            for k in range(k_g2m):
+                matrix = matrix + jnp.where(row == local[k:k + 1], coef[k:k + 1], 0.0)
+            return split(matrix.T)
+
+        def run(matrix):
+            value = dot3(matrix, (th[src, :], tl[src, :]))
+            at = slice(i * per_band, (i + 1) * per_band)
+            m0f[at] = value
+            m0h[at], m0l[at] = split(value)
+
+        return build, run
+
+    def mixing(layer, i, src, src_start, src_bands, out, out_start):
         srcf, srch, srcl = src
-        row = lax.broadcasted_iota(jnp.int32, (min(3, src_bands) * per_band, per_band), 0).astype(F32)
-        for i in range(out_bands):
-            band = out_start + i
-            rows, base = near(band, src_start, src_bands, per_band)
-
+        band = out_start + i
+        rows, base = near(band, src_start, src_bands, per_band)
+
+        def build():
+            row = lax.broadcasted_iota(jnp.int32, (LANES, per_band), 0).astype(F32).astype(BF16)
+            one, none = jnp.ones((), BF16), jnp.zeros((), BF16)
             local = band_rows(band, 2) - base
-            matrix = jnp.zeros(row.shape, F32)
-            for k in range(k_nbr):
-                matrix = matrix + jnp.where(row == local[k:k + 1], 1.0, 0.0)
-            matrix = matrix.T.astype(BF16)
+            pieces = []
+            for at in range(0, min(3, src_bands) * per_band, LANES):
+                piece = jnp.zeros(row.shape, BF16)
+                here = (local - float(at)).astype(BF16)
+                for k in range(k_nbr):
+                    piece = piece + jnp.where(row == here[k:k + 1], one, none)
+                pieces.append(piece.T)
+            return jnp.concatenate(pieces, axis=1)
+
+        def run(matrix):
             agg = (dot(matrix, srch[rows, :]) + dot(matrix, srcl[rows, :])) * (1.0 / k_nbr)
             own = srcf[pl.ds(pl.multiple_of((band - src_start) * per_band, per_band), per_band), :]
             center = own - jnp.mean(own, axis=1, keepdims=True)
             nrm = center * (1.0 / jnp.sqrt(jnp.mean(center * center, axis=1, keepdims=True) + 1e-05))
-            value = own + silu(dot3(split(jnp.concatenate([nrm, agg], axis=1)), (wh_ref[layer], wl_ref[layer])))
             at = slice(i * per_band, (i + 1) * per_band)
-            if out[0] is not None:
-                out[0][at] = value
-            out[1][at], out[2][at] = split(value)
+            xh[at, :width], xl[at, :width] = split(nrm)
+            xh[at, width:], xl[at, width:] = split(agg)
+
+        return build, run
+
+    def dense(layer, srcf, shift, rows, out):
+        def run(_):
+            for at in range(0, rows, DENSE[layer] * per_band):
+                part = min(DENSE[layer] * per_band, rows - at)
+                here = slice(at, at + part)
+                own = srcf[pl.ds(pl.multiple_of(shift * per_band + at, per_band), part), :]
+                value = own + silu(dot3((xh[here], xl[here]), (wh_ref[layer], wl_ref[layer])))
+                if out[0] is not None:
+                    out[0][here] = value
+                out[1][here], out[2][here] = split(value)
+
+        return (lambda: None), run
 
     _, bands0, bands1, bands2 = plan["bands"]
-    mixing(0, (m0f, m0h, m0l), start0, bands0, (m1f, m1h, m1l), start1, bands1)
-    mixing(1, (m1f, m1h, m1l), start1, bands1, (None, m2h, m2l), start2, bands2)
+    steps += [to_mesh(i) for i in range(bands0)]
+    steps += [mixing(0, i, (m0f, m0h, m0l), start0, bands0, (m1f, m1h, m1l), start1) for i in range(bands1)]
+    steps += [dense(0, m0f, start1 - start0, bands1 * per_band, (m1f, m1h, m1l))]
+    steps += [mixing(1, i, (m1f, m1h, m1l), start1, bands1, (None, m2h, m2l), start2) for i in range(bands2)]
+    steps += [dense(1, m1f, start2 - start1, bands2 * per_band, (None, m2h, m2l))]
+    ready = [build() for build, _ in steps[:AHEAD]]
+    for i, (_, run) in enumerate(steps):
+        if i + AHEAD < len(steps):
+            ready.append(steps[i + AHEAD][0]())
+        run(ready.pop(0))
 
     x = h_ref[...] + dot3((ah_ref[...], al_ref[...]), (m2h[...], m2l[...]))
     z = split(silu(dot3(split(x), (dh_ref[...], dl_ref[...]))))
@@ -304,24 +364,30 @@
         tables=2 if butterfly else 1, xor=masks, bands=bands, lat=n_lat, lon=n_lon,
         blocks=n_blocks, nodes=nodes, k_g2m=k_g2m, k_nbr=k_nbr,
     )
-    def place(value, at):
-        return jnp.pad(value.T, ((0, 8 - value.shape[1]), (at * nodes, LANES - (at + 1) * nodes)))
-
-    info = (place(g2m_idx, 0) + place(mesh_nbr, 2)).astype(F32) + place(g2m_w, 1)
-    wide = (n_blocks // 8) * width + LANES
-    h_one, payload = pl.pallas_call(
+    wide = (n_blocks // 8) * width
+    h_one, means = pl.pallas_call(
         encode_kernel,
         out_shape=(shape((rows, width)), shape((8, wide))),
-        in_specs=[hbm(), hbm(), vmem()],
+        in_specs=[hbm()] * 2,
         out_specs=(vmem(), vmem()),
         scratch_shapes=[
             pltpu.VMEM(grid_in.shape, F32),
             pltpu.VMEM(w_enc.shape, F32),
-            pltpu.SemaphoreType.DMA((2,)),
+            pltpu.SemaphoreType.DMA((1 + CHUNKS,)),
         ],
         compiler_params=pltpu.CompilerParams(vmem_limit_bytes=53 * MIB),
         name="encode",
-    )(grid_in, w_enc, info)
+        cost_estimate=pl.CostEstimate(flops=4 * 10**9, bytes_accessed=2 * MIB, transcendentals=0),
+    )(grid_in, w_enc)
+    payload = pl.pallas_call(
+        pack_kernel,
+        out_shape=shape((8, wide + LANES)),
+        in_specs=[vmem()] * 4,
+        out_specs=vmem(),
+        scratch_shapes=[pltpu.VMEM((24, LANES), F32)],
+        compiler_params=pltpu.CompilerParams(vmem_limit_bytes=4 * MIB),
+        name="pack",
+    )(means, g2m_idx.T, g2m_w.T, mesh_nbr.T)
 
     k_m2g = m2g_idx.shape[1]
     near = jnp.pad(m2g_idx.T, ((0, k_m2g), (0, 0))).astype(F32) + jnp.pad(m2g_w.T, ((k_m2g, 0), (0, 0)))
@@ -376,6 +442,8 @@
             pltpu.VMEM((n1, width), BF16),
             pltpu.VMEM((n2, width), BF16),
             pltpu.VMEM((n2, width), BF16),
+            pltpu.VMEM((n1, 2 * width), BF16),
+            pltpu.VMEM((n1, 2 * width), BF16),
             pltpu.VMEM((rows, n_var), F32),
             pltpu.SemaphoreType.DMA(()),
         ],

time: 60.1 us -> 58.6 us (0.975)
  other arithmetic: 3.68 us -> 2.08 us
  waiting for transfers between devices: 19 us -> 19.7 us
    add x1 -> x0, other arithmetic: 0.9 us -> none  [shards(): (place(g2m_idx, 0) + place(mesh_nbr, 2)).astype(F32) + place(g2m_w, 1)]
    add x1, other arithmetic: 0.71 us -> 0.01 us  [shards(): jnp.pad(m2g_idx.T, ((0, k_m2g), (0, 0))).astype(F32)]
    ppermute x18, waiting for transfers between devices: 19 us -> 19.7 us  [flip(): return lax.ppermute(value, AXES, [(i, i ^ mask) for i in range(count)])]
  transfers between devices with their start and end apart: 18 -> 18, of which waited for: 12 -> 13; matrix products, arithmetic and copies ran while one was open for 3% -> 2% of each run, Pallas kernels for 4% -> 4%
where the time goes in v3:
time: 58.6 us; the launch traced here: 58.4 us
  starting transfers between devices  21.1 us (36%)
  waiting for transfers between devices  19.7 us (34%)
  Pallas kernels  13.8 us (24%)
  other arithmetic  2.08 us (4%)
  between operations  1.57 us (3%)
    ppermute x18, starting transfers between devices, flip(): return lax.ppermute(value, AXES, [(i, i ^ mask) for i in range(count)])  21.1 us
    ppermute x18, waiting for transfers between devices, flip(): return lax.ppermute(value, AXES, [(i, i ^ mask) for i in range(count)])  19.7 us
    pallas_call x1, Pallas kernels, shards(): pl.pallas_call(functools.partial(mesh_kernel, plan), out_shape=(shape((ro...  9.06 us
    pallas_call x1, Pallas kernels, shards(): pl.pallas_call(functools.partial(prepare_kernel, plan), out_shape=(shape(...  2.58 us
    pallas_call x1, Pallas kernels, shards(): pl.pallas_call(encode_kernel, out_shape=(shape((rows, width)), shape((8,...  2.11 us
  transfers between devices with their start and end apart: 18, of which 13 were waited for; matrix products, arithmetic and copies ran while one was open for 2% of the time, Pallas kernels for 4%

profile of v3, /device:TPU:0, one launch (start us, length us, event | category | flops | bytes accessed | tf_op | source)
XLA Modules:
  0.0 58.4 jit_solution(14210933961990115669)
XLA Ops:
  0.7 2.1 %encode.1 = (f32[256,512]{1,0:T(8,128)S(1)}, f32[8,1024]{1,0:T(8,128)S(1)}) custom-call(f32[256,512]{1,0:T(8,128)} %x_hbm.1, f32[512,512]{1,0:T(8,128)} %w_hbm.1), custom_call_target="tpu_custom_call" | custom-call | flops 4000000000 | bytes 2097152 | tf_op jit(solution)/shard_map/encode/pallas_call | solution.py:368
  2.9 3.0 %collective-permute-start = (f32[1,8,1152]{2,1,0:T(8,128)S(1)}, f32[1,8,1152]{2,1,0:T(8,128)S(1)}, u32[]{:S(2)}, u32[]{:S(2)}) collective-permute-start(f32[1,8,1152]{2,1,0:T(8,128)S(1)} %bitcast.39), channel_id=1, source_target_pairs={{0,8},{1,9},{2,10},{3,11},{4,12},{5,13},{6,14},{7,15},{8,0},{9,1},... | collective-permute-start | bytes 110600 | tf_op jit(solution)/shard_map/ppermute | solution.py:293
  6.0 2.6 %collective-permute-start.1 = (f32[1,8,1152]{2,1,0:T(8,128)S(1)}, f32[1,8,1152]{2,1,0:T(8,128)S(1)}, u32[]{:S(2)}, u32[]{:S(2)}) collective-permute-start(f32[1,8,1152]{2,1,0:T(8,128)S(1)} %bitcast.40), channel_id=1, source_target_pairs={{0,16},{1,17},{2,18},{3,19},{4,20},{5,21},{6,22},{7,23},{8,24},{9,... | collective-permute-start | bytes 110600 | tf_op jit(solution)/shard_map/ppermute | solution.py:293
  8.6 2.9 %collective-permute-done.1 = f32[1,8,1152]{2,1,0:T(8,128)S(1)} collective-permute-done((f32[1,8,1152]{2,1,0:T(8,128)S(1)}, f32[1,8,1152]{2,1,0:T(8,128)S(1)}, u32[]{:S(2)}, u32[]{:S(2)}) %collective-permute-start.1) | collective-permute-done | bytes 36896 | tf_op jit(solution)/shard_map/ppermute | solution.py:293
  11.5 2.8 %collective-permute-done.2 = f32[1,8,1152]{2,1,0:T(8,128)S(1)} collective-permute-done((f32[1,8,1152]{2,1,0:T(8,128)S(1)}, f32[1,8,1152]{2,1,0:T(8,128)S(1)}, u32[]{:S(2)}, u32[]{:S(2)}) %collective-permute-start.2) | collective-permute-done | bytes 36896 | tf_op jit(solution)/shard_map/ppermute | solution.py:293
  14.3 1.6 %collective-permute-start.3 = (f32[4,8,1152]{2,1,0:T(8,128)S(1)}, f32[4,8,1152]{2,1,0:T(8,128)S(1)}, u32[]{:S(2)}, u32[]{:S(2)}) collective-permute-start(f32[4,8,1152]{2,1,0:T(8,128)S(1)} %pad_maximum_fusion.1), channel_id=1, source_target_pairs={{0,2},{1,3},{2,0},{3,1},{4,6},{5,7},{6,4},{7,5},{8,10},{9,11},{10,... | collective-permute-start | bytes 442376 | tf_op jit(solution)/shard_map/ppermute | solution.py:293
  15.9 1.5 %collective-permute-start.4 = (f32[4,8,1152]{2,1,0:T(8,128)S(1)}, f32[4,8,1152]{2,1,0:T(8,128)S(1)}, u32[]{:S(2)}, u32[]{:S(2)}) collective-permute-start(f32[4,8,1152]{2,1,0:T(8,128)S(1)} %pad_maximum_fusion.1), channel_id=1, source_target_pairs={{0,4},{1,5},{2,6},{3,7},{4,0},{5,1},{6,2},{7,3},{8,12},{9,13},{10,... | collective-permute-start | bytes 442376 | tf_op jit(solution)/shard_map/ppermute | solution.py:293
  17.4 0.5 collective-permute-start.5
  17.9 2.6 %prepare.1 = (bf16[2,1024,512]{2,1,0:T(8,128)(2,1)S(1)}, bf16[2,1024,512]{2,1,0:T(8,128)(2,1)S(1)}, bf16[512,512]{1,0:T(8,128)(2,1)S(1)}, bf16[512,512]{1,0:T(8,...) custom-call(f32[2,512,512]{2,1,0:T(8,128)} %ws_hbm.1, ...), custom_call_target="tpu_custom_call" | custom-call | bytes 12582912 | tf_op jit(solution)/shard_map/prepare/pallas_call | solution.py:395
  20.5 0.3 collective-permute-done.3
  20.8 2.8 %collective-permute-done.4 = f32[4,8,1152]{2,1,0:T(8,128)S(1)} collective-permute-done((f32[4,8,1152]{2,1,0:T(8,128)S(1)}, f32[4,8,1152]{2,1,0:T(8,128)S(1)}, u32[]{:S(2)}, u32[]{:S(2)}) %collective-permute-start.4) | collective-permute-done | bytes 147488 | tf_op jit(solution)/shard_map/ppermute | solution.py:293
  23.7 2.0 %collective-permute-done.6.refs_1_ = f32[16,8,1152]{2,1,0:T(8,128)S(1)} collective-permute-done((f32[16,8,1152]{2,1,0:T(8,128)S(1)}, f32[16,8,1152]{2,1,0:T(8,128)S(1)}, u32[]{:S(2)}, u32[]{:S(2)}) %collective-permute-start.6) | collective-permute-done | bytes 589856 | tf_op jit(solution)/shard_map/ppermute | solution.py:293
  25.7 9.1 %mesh.1 = (f32[256,128]{1,0:T(8,128)}, f32[264,128]{1,0:T(8,128)S(1)}, f32[264,128]{1,0:T(8,128)S(1)}) custom-call(f32[16,8,1152]{2,1,0:T(8,128)S(1)} %constant_dynamic-update-slice_fusion.refs_0_, f32[16,8,1152]{2,1,0:T(8,128)S(1)} %collective-permute-done.6.refs_1_, bf16[2,1024,512]{2,1,0:T(8,128)(2,1)S(1)} %get-tuple-element.41.refs_2_, ...), custom_call_target="tpu_custom_call" | custom-call | tf_op jit(solution)/shard_map/mesh/pallas_call | solution.py:428
  35.0 1.2 %collective-permute-done.7 = f32[264,128]{1,0:T(8,128)S(1)} collective-permute-done((f32[264,128]{1,0:T(8,128)S(1)}, f32[264,128]{1,0:T(8,128)S(1)}, u32[]{:S(2)}, u32[]{:S(2)}) %collective-permute-start.7) | collective-permute-done | bytes 135200 | tf_op jit(solution)/shard_map/ppermute | solution.py:293
  36.3 0.7 %collective-permute-start.10 = (f32[72,128]{1,0:T(8,128)S(1)}, f32[72,128]{1,0:T(8,128)S(1)}, u32[]{:S(2)}, u32[]{:S(2)}) collective-permute-start(f32[72,128]{1,0:T(8,128)S(1)} %get-tuple-element.67), channel_id=1, source_target_pairs={{0,6},{1,7},{2,4},{3,5},{4,2},{5,3},{6,0},{7,1},{8,14},{9,15},{10,... | collective-permute-start | bytes 110600 | tf_op jit(solution)/shard_map/ppermute | solution.py:293
  37.0 1.8 %collective-permute-start.8 = (f32[72,128]{1,0:T(8,128)S(1)}, f32[72,128]{1,0:T(8,128)S(1)}, u32[]{:S(2)}, u32[]{:S(2)}) collective-permute-start(f32[72,128]{1,0:T(8,128)S(1)} %get-tuple-element.65), channel_id=1, source_target_pairs={{0,2},{1,3},{2,0},{3,1},{4,6},{5,7},{6,4},{7,5},{8,10},{9,11},{10,... | collective-permute-start | bytes 110600 | tf_op jit(solution)/shard_map/ppermute | solution.py:293
  38.9 1.0 %collective-permute-start.9 = (f32[72,128]{1,0:T(8,128)S(1)}, f32[72,128]{1,0:T(8,128)S(1)}, u32[]{:S(2)}, u32[]{:S(2)}) collective-permute-start(f32[72,128]{1,0:T(8,128)S(1)} %get-tuple-element.66), channel_id=1, source_target_pairs={{0,4},{1,5},{2,6},{3,7},{4,0},{5,1},{6,2},{7,3},{8,12},{9,13},{10,... | collective-permute-start | bytes 110600 | tf_op jit(solution)/shard_map/ppermute | solution.py:293
  39.9 1.4 %collective-permute-done.10 = f32[72,128]{1,0:T(8,128)S(1)} collective-permute-done((f32[72,128]{1,0:T(8,128)S(1)}, f32[72,128]{1,0:T(8,128)S(1)}, u32[]{:S(2)}, u32[]{:S(2)}) %collective-permute-start.10) | collective-permute-done | bytes 36896 | tf_op jit(solution)/shard_map/ppermute | solution.py:293
  41.3 1.6 %collective-permute-done.9 = f32[72,128]{1,0:T(8,128)S(1)} collective-permute-done((f32[72,128]{1,0:T(8,128)S(1)}, f32[72,128]{1,0:T(8,128)S(1)}, u32[]{:S(2)}, u32[]{:S(2)}) %collective-permute-start.9) | collective-permute-done | bytes 36896 | tf_op jit(solution)/shard_map/ppermute | solution.py:293
  42.9 1.1 %collective-permute-start.12 = (f32[72,128]{1,0:T(8,128)S(1)}, f32[72,128]{1,0:T(8,128)S(1)}, u32[]{:S(2)}, u32[]{:S(2)}) collective-permute-start(f32[72,128]{1,0:T(8,128)S(1)} %fusion.2), channel_id=1, source_target_pairs={{0,16},{1,17},{2,18},{3,19},{4,20},{5,21},{6,22},{7,23},{8,24},{9,... | collective-permute-start | bytes 110600 | tf_op jit(solution)/shard_map/ppermute | solution.py:293
  44.0 3.2 %collective-permute-start.13 = (f32[72,128]{1,0:T(8,128)S(1)}, f32[72,128]{1,0:T(8,128)S(1)}, u32[]{:S(2)}, u32[]{:S(2)}) collective-permute-start(f32[72,128]{1,0:T(8,128)S(1)} %fusion.2), channel_id=1, source_target_pairs={{0,24},{1,25},{2,26},{3,27},{4,28},{5,29},{6,30},{7,31},{8,16},{9,... | collective-permute-start | bytes 110600 | tf_op jit(solution)/shard_map/ppermute | solution.py:293
  47.3 0.6 %convert_reduce_fusion = f32[]{:T(128)} fusion(s32[128]{0:T(128)S(1)} %copy-done.8), kind=kLoop, calls=%fused_computation.36 | loop fusion | flops 255 | bytes 516 | tf_op jit(solution)/shard_map/reduce_sum | solution.py:455
  48.6 1.2 %collective-permute-done.13 = f32[72,128]{1,0:T(8,128)S(1)} collective-permute-done((f32[72,128]{1,0:T(8,128)S(1)}, f32[72,128]{1,0:T(8,128)S(1)}, u32[]{:S(2)}, u32[]{:S(2)}) %collective-permute-start.13) | collective-permute-done | bytes 36896 | tf_op jit(solution)/shard_map/ppermute | solution.py:293
  49.9 0.3 collective-permute-start.14
  50.2 1.2 %collective-permute-start.15 = (f32[64,128]{1,0:T(8,128)S(1)}, f32[64,128]{1,0:T(8,128)S(1)}, u32[]{:S(2)}, u32[]{:S(2)}) collective-permute-start(f32[64,128]{1,0:T(8,128)S(1)} %slice_multiply_fusion), channel_id=1, source_target_pairs={{0,4},{1,5},{2,6},{3,7},{4,0},{5,1},{6,2},{7,3},{8,12},{9,13},{10,... | collective-permute-start | bytes 98312 | tf_op jit(solution)/shard_map/ppermute | solution.py:293
  51.4 2.0 %collective-permute-start.16 = (f32[64,128]{1,0:T(8,128)S(1)}, f32[64,128]{1,0:T(8,128)S(1)}, u32[]{:S(2)}, u32[]{:S(2)}) collective-permute-start(f32[64,128]{1,0:T(8,128)S(1)} %slice_multiply_fusion), channel_id=1, source_target_pairs={{0,6},{1,7},{2,4},{3,5},{4,2},{5,3},{6,0},{7,1},{8,14},{9,15},{10,... | collective-permute-start | bytes 98312 | tf_op jit(solution)/shard_map/ppermute | solution.py:293
  53.4 0.4 collective-permute-done.14
  53.8 0.2 collective-permute-done.15
  54.1 2.1 %collective-permute-done.16 = f32[64,128]{1,0:T(8,128)S(1)} collective-permute-done((f32[64,128]{1,0:T(8,128)S(1)}, f32[64,128]{1,0:T(8,128)S(1)}, u32[]{:S(2)}, u32[]{:S(2)}) %collective-permute-start.16) | collective-permute-done | bytes 32800 | tf_op jit(solution)/shard_map/ppermute | solution.py:293
  56.3 0.6 %fusion.8 = f32[]{:T(128)} fusion(f32[128]{0:T(128)S(1)} %get-tuple-element.54, f32[72,128]{1,0:T(8,128)S(1)} %add_add_fusion), kind=kLoop, calls=%fused_computation.35 | loop fusion | flops 255 | bytes 1028 | tf_op jit(solution)/shard_map/reduce_sum | solution.py:492
  56.9 0.7 %collective-permute-done.17 = f32[256,128]{1,0:T(8,128)S(1)} collective-permute-done((f32[256,128]{1,0:T(8,128)S(1)}, f32[256,128]{1,0:T(8,128)S(1)}, u32[]{:S(2)}, u32[]{:S(2)}) %collective-permute-start.17) | collective-permute-done | bytes 131104 | tf_op jit(solution)/shard_map/ppermute | solution.py:293
  57.7 0.7 %pad_maximum_fusion = f32[512,128]{1,0:T(8,128)} fusion(f32[256,128]{1,0:T(8,128)S(1)} %get-tuple-element.56, f32[256,128]{1,0:T(8,128)S(1)} %get-tuple-element.55), kind=kLoop, calls=%fused_computation | loop fusion | flops 65536 | bytes 524288 | tf_op jit(solution)/shard_map/concatenate | solution.py:491
  (49 shorter events, 0.8 us)
Async XLA Ops:
  0.6 2.2 %copy-start.3 = (s32[32,8]{0,1:T(8,128)S(1)}, s32[32,8]{0,1:T(8,128)}, u32[]{:S(2)}) copy-start(s32[32,8]{0,1:T(8,128)} %param.21) | copy-start | bytes 3076
  0.6 2.2 %copy-start.4 = (f32[32,8]{0,1:T(8,128)S(1)}, f32[32,8]{0,1:T(8,128)}, u32[]{:S(2)}) copy-start(f32[32,8]{0,1:T(8,128)} %param.22) | copy-start | bytes 3076
  0.7 2.2 %copy-start.5 = (s32[32,6]{0,1:T(8,128)S(1)}, s32[32,6]{0,1:T(8,128)}, u32[]{:S(2)}) copy-start(s32[32,6]{0,1:T(8,128)} %param.23) | copy-start | bytes 2308
  0.7 17.2 %copy-start.7 = (s32[256,4]{0,1:T(4,128)S(1)}, s32[256,4]{0,1:T(4,128)}, u32[]{:S(2)}) copy-start(s32[256,4]{0,1:T(4,128)} %param.24) | copy-start | bytes 12292
  0.7 17.2 %copy-start.6 = (f32[256,4]{0,1:T(4,128)S(1)}, f32[256,4]{0,1:T(4,128)}, u32[]{:S(2)}) copy-start(f32[256,4]{0,1:T(4,128)} %param.25) | copy-start | bytes 12292
  0.7 17.2 %copy-start = (f32[512,512]{1,0:T(8,128)S(1)}, f32[512,512]{1,0:T(8,128)}, u32[]{:S(2)}) copy-start(f32[512,512]{1,0:T(8,128)} %wd_hbm.1) | copy-start | bytes 3145732
  0.7 17.2 %copy-start.1 = (f32[512,128]{1,0:T(8,128)S(1)}, f32[512,128]{1,0:T(8,128)}, u32[]{:S(2)}) copy-start(f32[512,128]{1,0:T(8,128)} %wo_hbm.1) | copy-start | bytes 786436
  2.9 5.6 %collective-permute-start = (f32[1,8,1152]{2,1,0:T(8,128)S(1)}, f32[1,8,1152]{2,1,0:T(8,128)S(1)}, u32[]{:S(2)}, u32[]{:S(2)}) collective-permute-start(f32[1,8,1152]{2,1,0:T(8,128)S(1)} %bitcast.39), channel_id=1, source_target_pairs={{0,8},{1,9},{2,10},{3,11},{4,12},{5,13},{6,14},{7,15},{8,0},{9,1},... | collective-permute-start | bytes 110600 | tf_op jit(solution)/shard_map/ppermute | solution.py:293
  6.0 5.5 %collective-permute-start.1 = (f32[1,8,1152]{2,1,0:T(8,128)S(1)}, f32[1,8,1152]{2,1,0:T(8,128)S(1)}, u32[]{:S(2)}, u32[]{:S(2)}) collective-permute-start(f32[1,8,1152]{2,1,0:T(8,128)S(1)} %bitcast.40), channel_id=1, source_target_pairs={{0,16},{1,17},{2,18},{3,19},{4,20},{5,21},{6,22},{7,23},{8,24},{9,... | collective-permute-start | bytes 110600 | tf_op jit(solution)/shard_map/ppermute | solution.py:293
  8.6 5.8 %collective-permute-start.2 = (f32[1,8,1152]{2,1,0:T(8,128)S(1)}, f32[1,8,1152]{2,1,0:T(8,128)S(1)}, u32[]{:S(2)}, u32[]{:S(2)}) collective-permute-start(f32[1,8,1152]{2,1,0:T(8,128)S(1)} %bitcast.41), channel_id=1, source_target_pairs={{0,24},{1,25},{2,26},{3,27},{4,28},{5,29},{6,30},{7,31},{8,16},{9,... | collective-permute-start | bytes 110600 | tf_op jit(solution)/shard_map/ppermute | solution.py:293
  14.3 6.4 %collective-permute-start.3 = (f32[4,8,1152]{2,1,0:T(8,128)S(1)}, f32[4,8,1152]{2,1,0:T(8,128)S(1)}, u32[]{:S(2)}, u32[]{:S(2)}) collective-permute-start(f32[4,8,1152]{2,1,0:T(8,128)S(1)} %pad_maximum_fusion.1), channel_id=1, source_target_pairs={{0,2},{1,3},{2,0},{3,1},{4,6},{5,7},{6,4},{7,5},{8,10},{9,11},{10,... | collective-permute-start | bytes 442376 | tf_op jit(solution)/shard_map/ppermute | solution.py:293
  15.9 7.7 %collective-permute-start.4 = (f32[4,8,1152]{2,1,0:T(8,128)S(1)}, f32[4,8,1152]{2,1,0:T(8,128)S(1)}, u32[]{:S(2)}, u32[]{:S(2)}) collective-permute-start(f32[4,8,1152]{2,1,0:T(8,128)S(1)} %pad_maximum_fusion.1), channel_id=1, source_target_pairs={{0,4},{1,5},{2,6},{3,7},{4,0},{5,1},{6,2},{7,3},{8,12},{9,13},{10,... | collective-permute-start | bytes 442376 | tf_op jit(solution)/shard_map/ppermute | solution.py:293
  17.4 6.2 %collective-permute-start.5 = (f32[4,8,1152]{2,1,0:T(8,128)S(1)}, f32[4,8,1152]{2,1,0:T(8,128)S(1)}, u32[]{:S(2)}, u32[]{:S(2)}) collective-permute-start(f32[4,8,1152]{2,1,0:T(8,128)S(1)} %pad_maximum_fusion.1), channel_id=1, source_target_pairs={{0,6},{1,7},{2,4},{3,5},{4,2},{5,3},{6,0},{7,1},{8,14},{9,15},{10,... | collective-permute-start | bytes 442376 | tf_op jit(solution)/shard_map/ppermute | solution.py:293
  17.9 7.8 %copy-start.2 = (f32[256,128]{1,0:T(8,128)S(1)}, f32[256,128]{1,0:T(8,128)}, u32[]{:S(2)}) copy-start(f32[256,128]{1,0:T(8,128)} %refs_11_.1) | copy-start | bytes 393220
  23.7 2.1 %collective-permute-start.6 = (f32[16,8,1152]{2,1,0:T(8,128)S(1)}, f32[16,8,1152]{2,1,0:T(8,128)S(1)}, u32[]{:S(2)}, u32[]{:S(2)}) collective-permute-start(f32[16,8,1152]{2,1,0:T(8,128)S(1)} %constant_dynamic-update-slice_fusion.refs_0_), channel_id=1, source_target_pairs={{0,1},{1,0},{2,3},{3,2},{4,5},{5,4},{6,7},{7,6},{8,9},{9,8},{10,11... | collective-permute-start | bytes 1769480 | tf_op jit(solution)/shard_map/ppermute | solution.py:293
  25.7 21.6 %copy-start.8 = (s32[128]{0:T(128)S(1)}, s32[128]{0:T(128)}, u32[]{:S(2)}) copy-start(s32[128]{0:T(128)} %param.20) | copy-start | bytes 1540
  34.8 1.4 %collective-permute-start.7 = (f32[264,128]{1,0:T(8,128)S(1)}, f32[264,128]{1,0:T(8,128)S(1)}, u32[]{:S(2)}, u32[]{:S(2)}) collective-permute-start(f32[264,128]{1,0:T(8,128)S(1)} %get-tuple-element.52), channel_id=1, source_target_pairs={{0,1},{1,0},{2,3},{3,2},{4,5},{5,4},{6,7},{7,6},{8,9},{9,8},{10,11... | collective-permute-start | bytes 405512 | tf_op jit(solution)/shard_map/ppermute | solution.py:293
  36.3 4.9 %collective-permute-start.10 = (f32[72,128]{1,0:T(8,128)S(1)}, f32[72,128]{1,0:T(8,128)S(1)}, u32[]{:S(2)}, u32[]{:S(2)}) collective-permute-start(f32[72,128]{1,0:T(8,128)S(1)} %get-tuple-element.67), channel_id=1, source_target_pairs={{0,6},{1,7},{2,4},{3,5},{4,2},{5,3},{6,0},{7,1},{8,14},{9,15},{10,... | collective-permute-start | bytes 110600 | tf_op jit(solution)/shard_map/ppermute | solution.py:293
  37.0 4.2 %collective-permute-start.8 = (f32[72,128]{1,0:T(8,128)S(1)}, f32[72,128]{1,0:T(8,128)S(1)}, u32[]{:S(2)}, u32[]{:S(2)}) collective-permute-start(f32[72,128]{1,0:T(8,128)S(1)} %get-tuple-element.65), channel_id=1, source_target_pairs={{0,2},{1,3},{2,0},{3,1},{4,6},{5,7},{6,4},{7,5},{8,10},{9,11},{10,... | collective-permute-start | bytes 110600 | tf_op jit(solution)/shard_map/ppermute | solution.py:293
  38.9 4.0 %collective-permute-start.9 = (f32[72,128]{1,0:T(8,128)S(1)}, f32[72,128]{1,0:T(8,128)S(1)}, u32[]{:S(2)}, u32[]{:S(2)}) collective-permute-start(f32[72,128]{1,0:T(8,128)S(1)} %get-tuple-element.66), channel_id=1, source_target_pairs={{0,4},{1,5},{2,6},{3,7},{4,0},{5,1},{6,2},{7,3},{8,12},{9,13},{10,... | collective-permute-start | bytes 110600 | tf_op jit(solution)/shard_map/ppermute | solution.py:293
  42.8 5.7 %collective-permute-start.11 = (f32[72,128]{1,0:T(8,128)S(1)}, f32[72,128]{1,0:T(8,128)S(1)}, u32[]{:S(2)}, u32[]{:S(2)}) collective-permute-start(f32[72,128]{1,0:T(8,128)S(1)} %fusion.2), channel_id=1, source_target_pairs={{0,8},{1,9},{2,10},{3,11},{4,12},{5,13},{6,14},{7,15},{8,0},{9,1},... | collective-permute-start | bytes 110600 | tf_op jit(solution)/shard_map/ppermute | solution.py:293
  42.9 5.6 %collective-permute-start.12 = (f32[72,128]{1,0:T(8,128)S(1)}, f32[72,128]{1,0:T(8,128)S(1)}, u32[]{:S(2)}, u32[]{:S(2)}) collective-permute-start(f32[72,128]{1,0:T(8,128)S(1)} %fusion.2), channel_id=1, source_target_pairs={{0,16},{1,17},{2,18},{3,19},{4,20},{5,21},{6,22},{7,23},{8,24},{9,... | collective-permute-start | bytes 110600 | tf_op jit(solution)/shard_map/ppermute | solution.py:293
  44.0 5.8 %collective-permute-start.13 = (f32[72,128]{1,0:T(8,128)S(1)}, f32[72,128]{1,0:T(8,128)S(1)}, u32[]{:S(2)}, u32[]{:S(2)}) collective-permute-start(f32[72,128]{1,0:T(8,128)S(1)} %fusion.2), channel_id=1, source_target_pairs={{0,24},{1,25},{2,26},{3,27},{4,28},{5,29},{6,30},{7,31},{8,16},{9,... | collective-permute-start | bytes 110600 | tf_op jit(solution)/shard_map/ppermute | solution.py:293
  49.9 4.0 %collective-permute-start.14 = (f32[64,128]{1,0:T(8,128)S(1)}, f32[64,128]{1,0:T(8,128)S(1)}, u32[]{:S(2)}, u32[]{:S(2)}) collective-permute-start(f32[64,128]{1,0:T(8,128)S(1)} %slice_multiply_fusion), channel_id=1, source_target_pairs={{0,2},{1,3},{2,0},{3,1},{4,6},{5,7},{6,4},{7,5},{8,10},{9,11},{10,... | collective-permute-start | bytes 98312 | tf_op jit(solution)/shard_map/ppermute | solution.py:293
  50.2 3.9 %collective-permute-start.15 = (f32[64,128]{1,0:T(8,128)S(1)}, f32[64,128]{1,0:T(8,128)S(1)}, u32[]{:S(2)}, u32[]{:S(2)}) collective-permute-start(f32[64,128]{1,0:T(8,128)S(1)} %slice_multiply_fusion), channel_id=1, source_target_pairs={{0,4},{1,5},{2,6},{3,7},{4,0},{5,1},{6,2},{7,3},{8,12},{9,13},{10,... | collective-permute-start | bytes 98312 | tf_op jit(solution)/shard_map/ppermute | solution.py:293
  51.4 4.8 %collective-permute-start.16 = (f32[64,128]{1,0:T(8,128)S(1)}, f32[64,128]{1,0:T(8,128)S(1)}, u32[]{:S(2)}, u32[]{:S(2)}) collective-permute-start(f32[64,128]{1,0:T(8,128)S(1)} %slice_multiply_fusion), channel_id=1, source_target_pairs={{0,6},{1,7},{2,4},{3,5},{4,2},{5,3},{6,0},{7,1},{8,14},{9,15},{10,... | collective-permute-start | bytes 98312 | tf_op jit(solution)/shard_map/ppermute | solution.py:293
  56.2 1.4 %collective-permute-start.17 = (f32[256,128]{1,0:T(8,128)S(1)}, f32[256,128]{1,0:T(8,128)S(1)}, u32[]{:S(2)}, u32[]{:S(2)}) collective-permute-start(f32[256,128]{1,0:T(8,128)S(1)} %pad_maximum_fusion.3), channel_id=1, source_target_pairs={{0,1},{1,0},{2,3},{3,2},{4,5},{5,4},{6,7},{7,6},{8,9},{9,8},{10,11... | collective-permute-start | bytes 393224 | tf_op jit(solution)/shard_map/ppermute | solution.py:293

commit v4 on v3

--- a/solution.py
+++ b/solution.py
@@ -16,8 +16,6 @@
 LANES = 128
 GROUP = 32
 MIB = 1024 * 1024
-AHEAD = 1
-DENSE = (1, 1)
 CHUNKS = 2
 
 
@@ -37,6 +35,13 @@
 
 def silu(value):
     return value / (1.0 + jnp.exp(-value))
+
+
+def second_half(number, bits):
+    half = number >> bits[0]
+    for bit in bits[1:]:
+        half = half ^ (number >> bit)
+    return (half & 1) == 1
 
 
 def vmem():
@@ -84,7 +89,7 @@
     spread, nodes = gi_ref.shape
     params[...] = jnp.zeros_like(params)
     params[:spread, :nodes] = gi_ref[...].astype(F32)
-    params[8:8 + spread, :nodes] = gw_ref[...]
+    params[8:8 + spread, :nodes] = gw_ref[...] / jnp.sum(gw_ref[...], axis=0, keepdims=True)
     params[16:16 + ni_ref.shape[0], :nodes] = ni_ref[...].astype(F32)
     tile = params[:8]
     for i in (1, 2):
@@ -105,7 +110,7 @@
     return band * plan["lon"] + tile, starts
 
 
-def prepare_kernel(plan, ws_hbm, wn_hbm, wd_hbm, wo_hbm, near_ref, wh_ref, wl_ref, dh_ref, dl_ref, oh_ref, ol_ref, ah_ref, al_ref,
+def prepare_kernel(ws_hbm, wn_hbm, wd_hbm, wo_hbm, near_ref, wh_ref, wl_ref, dh_ref, dl_ref, oh_ref, ol_ref, ah_ref, al_ref,
                    w_ref, wd_ref, wo_ref, params, sems):
     width = wd_hbm.shape[0]
     sources, places = [], []
@@ -115,9 +120,8 @@
     copies = fetch(sources + [wd_hbm, wo_hbm], places + [wd_ref, wo_ref], sems)
     rows, nodes = ah_ref.shape
     spread = near_ref.shape[0] // 2
-    starts = band_starts(plan)[1]
     params[...] = jnp.zeros_like(params)
-    params[:spread] = near_ref[:spread] - (starts[3] * (plan["lon"] * plan["nodes"])).astype(F32)
+    params[:spread] = near_ref[:spread]
     params[spread:2 * spread] = near_ref[spread:] / jnp.sum(near_ref[spread:], axis=0, keepdims=True)
     turned = params[...].T
     local, coef = turned[:, :spread], turned[:, spread:2 * spread]
@@ -164,16 +168,16 @@
     def band_rows(band, which):
         first = (band - start_b) * lon
         out = []
-        for at in range(0, lon * nodes, LANES):
+        for at in range(0, lon, LANES // nodes):
             total = None
-            for d in range(LANES // nodes):
-                tile = info[first + at // nodes + d]
+            for d in range(min(LANES // nodes, lon - at)):
+                value = info[first + at + d]
                 if d != which:
-                    tile = pltpu.roll(tile, ((d - which) * nodes) % LANES, 1)
+                    value = pltpu.roll(value, ((d - which) * nodes) % LANES, 1)
                 if total is None:
-                    total = tile
+                    total = value
                 else:
-                    total = jnp.where(lane >= d * nodes, tile, total)
+                    total = jnp.where(lane >= d * nodes, value, total)
             out.append(total)
         return jnp.concatenate(out, axis=1)
 
@@ -184,38 +188,32 @@
         return pl.ds(at, three * per_band), (low * per_band).astype(F32)
 
     per_band, per_band_b = lon * nodes, lon * n_blocks
-    steps = []
-
-    def to_mesh(i):
+
+    _, bands0, bands1, bands2 = plan["bands"]
+    row_b = lax.broadcasted_iota(jnp.int32, (min(3, plan["bands"][0]) * per_band_b, per_band), 0).astype(F32)
+    for i in range(bands0):
         src, base = near(start0 + i, start_b, plan["bands"][0], per_band_b)
-
-        def build():
-            row = lax.broadcasted_iota(jnp.int32, (min(3, plan["bands"][0]) * per_band_b, per_band), 0).astype(F32)
-            local = band_rows(start0 + i, 0) - base
-            coef = band_rows(start0 + i, 1)
-            total = jnp.sum(coef, axis=0, keepdims=True)
-            coef = coef / jnp.where(total == 0.0, 1.0, total)
-            matrix = jnp.zeros(row.shape, F32)
-            for k in range(k_g2m):
-                matrix = matrix + jnp.where(row == local[k:k + 1], coef[k:k + 1], 0.0)
-            return split(matrix.T)
-
-        def run(matrix):
-            value = dot3(matrix, (th[src, :], tl[src, :]))
-            at = slice(i * per_band, (i + 1) * per_band)
-            m0f[at] = value
-            m0h[at], m0l[at] = split(value)
-
-        return build, run
-
-    def mixing(layer, i, src, src_start, src_bands, out, out_start):
+        local = band_rows(start0 + i, 0) - base
+        coef = band_rows(start0 + i, 1)
+        matrix = jnp.zeros(row_b.shape, F32)
+        for k in range(k_g2m):
+            matrix = matrix + jnp.where(row_b == local[k:k + 1], coef[k:k + 1], 0.0)
+        value = dot3(split(matrix.T), (th[src, :], tl[src, :]))
+        at = slice(i * per_band, (i + 1) * per_band)
+        m0f[at] = value
+        m0h[at], m0l[at] = split(value)
+
+    def mixing(layer, src, src_start, src_bands, out, out_start, out_bands):
         srcf, srch, srcl = src
-        band = out_start + i
-        rows, base = near(band, src_start, src_bands, per_band)
-
-        def build():
-            row = lax.broadcasted_iota(jnp.int32, (LANES, per_band), 0).astype(F32).astype(BF16)
-            one, none = jnp.ones((), BF16), jnp.zeros((), BF16)
+        row = lax.broadcasted_iota(jnp.int32, (LANES, per_band), 0).astype(F32).astype(BF16)
+        one, none = jnp.ones((), BF16), jnp.zeros((), BF16)
+
+        def own_rows(i):
+            return srcf[pl.ds(pl.multiple_of((out_start + i - src_start) * per_band, per_band), per_band), :]
+
+        for i in range(out_bands):
+            band = out_start + i
+            rows, base = near(band, src_start, src_bands, per_band)
             local = band_rows(band, 2) - base
             pieces = []
             for at in range(0, min(3, src_bands) * per_band, LANES):
@@ -224,43 +222,23 @@
                 for k in range(k_nbr):
                     piece = piece + jnp.where(row == here[k:k + 1], one, none)
                 pieces.append(piece.T)
-            return jnp.concatenate(pieces, axis=1)
-
-        def run(matrix):
+            matrix = jnp.concatenate(pieces, axis=1)
             agg = (dot(matrix, srch[rows, :]) + dot(matrix, srcl[rows, :])) * (1.0 / k_nbr)
-            own = srcf[pl.ds(pl.multiple_of((band - src_start) * per_band, per_band), per_band), :]
+            own = own_rows(i)
             center = own - jnp.mean(own, axis=1, keepdims=True)
             nrm = center * (1.0 / jnp.sqrt(jnp.mean(center * center, axis=1, keepdims=True) + 1e-05))
             at = slice(i * per_band, (i + 1) * per_band)
             xh[at, :width], xl[at, :width] = split(nrm)
             xh[at, width:], xl[at, width:] = split(agg)
-
-        return build, run
-
-    def dense(layer, srcf, shift, rows, out):
-        def run(_):
-            for at in range(0, rows, DENSE[layer] * per_band):
-                part = min(DENSE[layer] * per_band, rows - at)
-                here = slice(at, at + part)
-                own = srcf[pl.ds(pl.multiple_of(shift * per_band + at, per_band), part), :]
-                value = own + silu(dot3((xh[here], xl[here]), (wh_ref[layer], wl_ref[layer])))
-                if out[0] is not None:
-                    out[0][here] = value
-                out[1][here], out[2][here] = split(value)
-
-        return (lambda: None), run
-
-    _, bands0, bands1, bands2 = plan["bands"]
-    steps += [to_mesh(i) for i in range(bands0)]
-    steps += [mixing(0, i, (m0f, m0h, m0l), start0, bands0, (m1f, m1h, m1l), start1) for i in range(bands1)]
-    steps += [dense(0, m0f, start1 - start0, bands1 * per_band, (m1f, m1h, m1l))]
-    steps += [mixing(1, i, (m1f, m1h, m1l), start1, bands1, (None, m2h, m2l), start2) for i in range(bands2)]
-    steps += [dense(1, m1f, start2 - start1, bands2 * per_band, (None, m2h, m2l))]
-    ready = [build() for build, _ in steps[:AHEAD]]
-    for i, (_, run) in enumerate(steps):
-        if i + AHEAD < len(steps):
-            ready.append(steps[i + AHEAD][0]())
-        run(ready.pop(0))
+        for i in range(out_bands):
+            at = slice(i * per_band, (i + 1) * per_band)
+            value = own_rows(i) + silu(dot3((xh[at], xl[at]), (wh_ref[layer], wl_ref[layer])))
+            if out[0] is not None:
+                out[0][at] = value
+            out[1][at], out[2][at] = split(value)
+
+    mixing(0, (m0f, m0h, m0l), start0, bands0, (m1f, m1h, m1l), start1, bands1)
+    mixing(1, (m1f, m1h, m1l), start1, bands1, (None, m2h, m2l), start2, bands2)
 
     x = h_ref[...] + dot3((ah_ref[...], al_ref[...]), (m2h[...], m2l[...]))
     z = split(silu(dot3(split(x), (dh_ref[...], dl_ref[...]))))
@@ -280,7 +258,7 @@
 
     grad = dot_t(zh, rh) + (dot_t(zh, rl) + dot_t(zl, rh))
     half = width // 2
-    swap = (me & 1) == 1
+    swap = second_half(me, plan["half_bits"])
     top, bottom = grad[:half], grad[half:]
     keep_ref[:half] = jnp.where(swap, bottom, top)
     send_ref[:half] = jnp.where(swap, top, bottom)
@@ -348,10 +326,11 @@
     if butterfly:
         bands = [n_lat] + [min(2 * r + 1, n_lat) for r in REACHES[1:]]
         bits = count.bit_length() - 1
-        groups = []
+        groups, half_bits = [], [0]
         while bits > 1:
             low = max(1, bits - 2)
-            groups.append([m << low for m in range(1 << (bits - low))])
+            groups.append([(m << low) | (m >> 1) for m in range(1 << (bits - low))])
+            half_bits += [low + 1] * (bits - low == 2)
             bits = low
         masks = [0]
         for group in groups:
@@ -359,10 +338,10 @@
         masks = masks + [m ^ 1 for m in masks]
     else:
         bands = [2 * r + 1 for r in REACHES]
-        masks = None
+        masks, half_bits = None, [0]
     plan = dict(
         tables=2 if butterfly else 1, xor=masks, bands=bands, lat=n_lat, lon=n_lon,
-        blocks=n_blocks, nodes=nodes, k_g2m=k_g2m, k_nbr=k_nbr,
+        blocks=n_blocks, nodes=nodes, k_g2m=k_g2m, k_nbr=k_nbr, half_bits=half_bits,
     )
     wide = (n_blocks // 8) * width
     h_one, means = pl.pallas_call(
@@ -390,10 +369,11 @@
     )(means, g2m_idx.T, g2m_w.T, mesh_nbr.T)
 
     k_m2g = m2g_idx.shape[1]
-    near = jnp.pad(m2g_idx.T, ((0, k_m2g), (0, 0))).astype(F32) + jnp.pad(m2g_w.T, ((k_m2g, 0), (0, 0)))
+    local = m2g_idx - band_starts(plan)[1][3] * (n_lon * nodes)
+    near = jnp.pad(local.T, ((0, k_m2g), (0, 0))).astype(F32) + jnp.pad(m2g_w.T, ((k_m2g, 0), (0, 0)))
     n2 = bands[3] * n_lon * nodes
     prepared = pl.pallas_call(
-        functools.partial(prepare_kernel, plan),
+        prepare_kernel,
         out_shape=(
             shape((L, 2 * width, width), BF16),
             shape((L, 2 * width, width), BF16),
@@ -460,7 +440,7 @@
         return sums[0], weights / (scale * grid_total * wsum)
 
     if not butterfly:
-        swap = (me & 1) == 1
+        swap = second_half(me, half_bits)
         top = jnp.where(swap, send[:half], keep[:half])
         bottom = jnp.where(swap, keep[:half], send[:half])
         total = lax.psum(jnp.concatenate([top, bottom, keep[half:]], axis=0), AXES)
@@ -487,7 +467,7 @@
     pieces = jnp.stack([piece] + [flip(piece, m, count) for m in group if m])
     own = jnp.concatenate([pick(pieces, at ^ i) for i in range(low)], axis=0)
     other = flip(own, 1, count)
-    swap = (me & 1) == 1
+    swap = second_half(me, half_bits)
     grad_out = jnp.concatenate([jnp.where(swap, other, own), jnp.where(swap, own, other)], axis=0)
     return (pred, jnp.sum(err * factor), grad_out)
 

time: 58.6 us -> 58.1 us (level)
  starting transfers between devices: 21.1 us -> 20 us
  waiting for transfers between devices: 19.7 us -> 20.3 us
    ppermute x18, starting transfers between devices: 21.1 us -> 20 us  [flip(): return lax.ppermute(value, AXES, [(i, i ^ mask) for i in range(count)])]
    ppermute x18, waiting for transfers between devices: 19.7 us -> 20.3 us  [flip(): return lax.ppermute(value, AXES, [(i, i ^ mask) for i in range(count)])]
  transfers between devices with their start and end apart: 18 -> 18, of which waited for: 13 -> 14; matrix products, arithmetic and copies ran while one was open for 2% -> 2% of each run, Pallas kernels for 4% -> 4%
where the time goes in v4:
time: 58.1 us; the launch traced here: 57.9 us
  waiting for transfers between devices  20.3 us (35%)
  starting transfers between devices  20 us (34%)
  Pallas kernels  13.8 us (24%)
  other arithmetic  2.08 us (4%)
  between operations  1.57 us (3%)
    ppermute x18, waiting for transfers between devices, flip(): return lax.ppermute(value, AXES, [(i, i ^ mask) for i in range(count)])  20.3 us
    ppermute x18, starting transfers between devices, flip(): return lax.ppermute(value, AXES, [(i, i ^ mask) for i in range(count)])  20 us
    pallas_call x1, Pallas kernels, shards(): pl.pallas_call(functools.partial(mesh_kernel, plan), out_shape=(shape((ro...  8.98 us
    pallas_call x1, Pallas kernels, shards(): pl.pallas_call(prepare_kernel, out_shape=(shape((L, 2 * width, width), BF...  2.57 us
    pallas_call x1, Pallas kernels, shards(): pl.pallas_call(encode_kernel, out_shape=(shape((rows, width)), shape((8,...  2.11 us
  transfers between devices with their start and end apart: 18, of which 14 were waited for; matrix products, arithmetic and copies ran while one was open for 2% of the time, Pallas kernels for 4%

profile of v4, /device:TPU:0, one launch (start us, length us, event | category | flops | bytes accessed | tf_op | source)
XLA Modules:
  0.0 57.9 jit_solution(14607104095201785275)
XLA Ops:
  0.7 2.1 %encode.1 = (f32[256,512]{1,0:T(8,128)S(1)}, f32[8,1024]{1,0:T(8,128)S(1)}) custom-call(f32[256,512]{1,0:T(8,128)} %x_hbm.1, f32[512,512]{1,0:T(8,128)} %w_hbm.1), custom_call_target="tpu_custom_call" | custom-call | flops 4000000000 | bytes 2097152 | tf_op jit(solution)/shard_map/encode/pallas_call | solution.py:347
  2.9 3.0 %collective-permute-start = (f32[1,8,1152]{2,1,0:T(8,128)S(1)}, f32[1,8,1152]{2,1,0:T(8,128)S(1)}, u32[]{:S(2)}, u32[]{:S(2)}) collective-permute-start(f32[1,8,1152]{2,1,0:T(8,128)S(1)} %bitcast.40), channel_id=1, source_target_pairs={{0,8},{1,9},{2,10},{3,11},{4,12},{5,13},{6,14},{7,15},{8,0},{9,1},... | collective-permute-start | bytes 110600 | tf_op jit(solution)/shard_map/ppermute | solution.py:271
  6.0 1.7 %collective-permute-start.1 = (f32[1,8,1152]{2,1,0:T(8,128)S(1)}, f32[1,8,1152]{2,1,0:T(8,128)S(1)}, u32[]{:S(2)}, u32[]{:S(2)}) collective-permute-start(f32[1,8,1152]{2,1,0:T(8,128)S(1)} %bitcast.41), channel_id=1, source_target_pairs={{0,17},{1,16},{2,19},{3,18},{4,21},{5,20},{6,23},{7,22},{8,25},{9,... | collective-permute-start | bytes 110600 | tf_op jit(solution)/shard_map/ppermute | solution.py:271
  8.1 2.3 %collective-permute-done.1 = f32[1,8,1152]{2,1,0:T(8,128)S(1)} collective-permute-done((f32[1,8,1152]{2,1,0:T(8,128)S(1)}, f32[1,8,1152]{2,1,0:T(8,128)S(1)}, u32[]{:S(2)}, u32[]{:S(2)}) %collective-permute-start.1) | collective-permute-done | bytes 36896 | tf_op jit(solution)/shard_map/ppermute | solution.py:271
  10.4 2.5 %collective-permute-done.2 = f32[1,8,1152]{2,1,0:T(8,128)S(1)} collective-permute-done((f32[1,8,1152]{2,1,0:T(8,128)S(1)}, f32[1,8,1152]{2,1,0:T(8,128)S(1)}, u32[]{:S(2)}, u32[]{:S(2)}) %collective-permute-start.2) | collective-permute-done | bytes 36896 | tf_op jit(solution)/shard_map/ppermute | solution.py:271
  12.9 1.6 %collective-permute-start.3 = (f32[4,8,1152]{2,1,0:T(8,128)S(1)}, f32[4,8,1152]{2,1,0:T(8,128)S(1)}, u32[]{:S(2)}, u32[]{:S(2)}) collective-permute-start(f32[4,8,1152]{2,1,0:T(8,128)S(1)} %pad_maximum_fusion.1), channel_id=1, source_target_pairs={{0,2},{1,3},{2,0},{3,1},{4,6},{5,7},{6,4},{7,5},{8,10},{9,11},{10,... | collective-permute-start | bytes 442376 | tf_op jit(solution)/shard_map/ppermute | solution.py:271
  14.5 1.8 %collective-permute-start.4 = (f32[4,8,1152]{2,1,0:T(8,128)S(1)}, f32[4,8,1152]{2,1,0:T(8,128)S(1)}, u32[]{:S(2)}, u32[]{:S(2)}) collective-permute-start(f32[4,8,1152]{2,1,0:T(8,128)S(1)} %pad_maximum_fusion.1), channel_id=1, source_target_pairs={{0,5},{1,4},{2,7},{3,6},{4,1},{5,0},{6,3},{7,2},{8,13},{9,12},{10,... | collective-permute-start | bytes 442376 | tf_op jit(solution)/shard_map/ppermute | solution.py:271
  16.4 2.6 %prepare.1 = (bf16[2,1024,512]{2,1,0:T(8,128)(2,1)S(1)}, bf16[2,1024,512]{2,1,0:T(8,128)(2,1)S(1)}, bf16[512,512]{1,0:T(8,128)(2,1)S(1)}, bf16[512,512]{1,0:T(8,...) custom-call(f32[2,512,512]{2,1,0:T(8,128)} %ws_hbm.1, ...), custom_call_target="tpu_custom_call" | custom-call | bytes 12582912 | tf_op jit(solution)/shard_map/prepare/pallas_call | solution.py:375
  18.9 0.8 %collective-permute-done.3 = f32[4,8,1152]{2,1,0:T(8,128)S(1)} collective-permute-done((f32[4,8,1152]{2,1,0:T(8,128)S(1)}, f32[4,8,1152]{2,1,0:T(8,128)S(1)}, u32[]{:S(2)}, u32[]{:S(2)}) %collective-permute-start.3) | collective-permute-done | bytes 147488 | tf_op jit(solution)/shard_map/ppermute | solution.py:271
  19.7 3.1 %collective-permute-done.4 = f32[4,8,1152]{2,1,0:T(8,128)S(1)} collective-permute-done((f32[4,8,1152]{2,1,0:T(8,128)S(1)}, f32[4,8,1152]{2,1,0:T(8,128)S(1)}, u32[]{:S(2)}, u32[]{:S(2)}) %collective-permute-start.4) | collective-permute-done | bytes 147488 | tf_op jit(solution)/shard_map/ppermute | solution.py:271
  22.8 1.0 %collective-permute-done.5 = f32[4,8,1152]{2,1,0:T(8,128)S(1)} collective-permute-done((f32[4,8,1152]{2,1,0:T(8,128)S(1)}, f32[4,8,1152]{2,1,0:T(8,128)S(1)}, u32[]{:S(2)}, u32[]{:S(2)}) %collective-permute-start.5) | collective-permute-done | bytes 147488 | tf_op jit(solution)/shard_map/ppermute | solution.py:271
  24.1 1.9 %collective-permute-done.6.refs_1_ = f32[16,8,1152]{2,1,0:T(8,128)S(1)} collective-permute-done((f32[16,8,1152]{2,1,0:T(8,128)S(1)}, f32[16,8,1152]{2,1,0:T(8,128)S(1)}, u32[]{:S(2)}, u32[]{:S(2)}) %collective-permute-start.6) | collective-permute-done | bytes 589856 | tf_op jit(solution)/shard_map/ppermute | solution.py:271
  26.0 9.0 %mesh.1 = (f32[256,128]{1,0:T(8,128)}, f32[264,128]{1,0:T(8,128)S(1)}, f32[264,128]{1,0:T(8,128)S(1)}) custom-call(f32[16,8,1152]{2,1,0:T(8,128)S(1)} %constant_dynamic-update-slice_fusion.refs_0_, f32[16,8,1152]{2,1,0:T(8,128)S(1)} %collective-permute-done.6.refs_1_, bf16[2,1024,512]{2,1,0:T(8,128)(2,1)S(1)} %get-tuple-element.41.refs_2_, ...), custom_call_target="tpu_custom_call" | custom-call | tf_op jit(solution)/shard_map/mesh/pallas_call | solution.py:408
  35.2 1.2 %collective-permute-done.7 = f32[264,128]{1,0:T(8,128)S(1)} collective-permute-done((f32[264,128]{1,0:T(8,128)S(1)}, f32[264,128]{1,0:T(8,128)S(1)}, u32[]{:S(2)}, u32[]{:S(2)}) %collective-permute-start.7) | collective-permute-done | bytes 135200 | tf_op jit(solution)/shard_map/ppermute | solution.py:271
  36.5 1.3 %collective-permute-start.10 = (f32[72,128]{1,0:T(8,128)S(1)}, f32[72,128]{1,0:T(8,128)S(1)}, u32[]{:S(2)}, u32[]{:S(2)}) collective-permute-start(f32[72,128]{1,0:T(8,128)S(1)} %get-tuple-element.67), channel_id=1, source_target_pairs={{0,7},{1,6},{2,5},{3,4},{4,3},{5,2},{6,1},{7,0},{8,15},{9,14},{10,... | collective-permute-start | bytes 110600 | tf_op jit(solution)/shard_map/ppermute | solution.py:271
  37.7 1.2 %collective-permute-start.8 = (f32[72,128]{1,0:T(8,128)S(1)}, f32[72,128]{1,0:T(8,128)S(1)}, u32[]{:S(2)}, u32[]{:S(2)}) collective-permute-start(f32[72,128]{1,0:T(8,128)S(1)} %get-tuple-element.65), channel_id=1, source_target_pairs={{0,2},{1,3},{2,0},{3,1},{4,6},{5,7},{6,4},{7,5},{8,10},{9,11},{10,... | collective-permute-start | bytes 110600 | tf_op jit(solution)/shard_map/ppermute | solution.py:271
  38.9 0.5 collective-permute-start.9
  39.5 1.4 %collective-permute-done.10 = f32[72,128]{1,0:T(8,128)S(1)} collective-permute-done((f32[72,128]{1,0:T(8,128)S(1)}, f32[72,128]{1,0:T(8,128)S(1)}, u32[]{:S(2)}, u32[]{:S(2)}) %collective-permute-start.10) | collective-permute-done | bytes 36896 | tf_op jit(solution)/shard_map/ppermute | solution.py:271
  40.9 0.8 %collective-permute-done.8 = f32[72,128]{1,0:T(8,128)S(1)} collective-permute-done((f32[72,128]{1,0:T(8,128)S(1)}, f32[72,128]{1,0:T(8,128)S(1)}, u32[]{:S(2)}, u32[]{:S(2)}) %collective-permute-start.8) | collective-permute-done | bytes 36896 | tf_op jit(solution)/shard_map/ppermute | solution.py:271
  41.7 0.9 %collective-permute-done.9 = f32[72,128]{1,0:T(8,128)S(1)} collective-permute-done((f32[72,128]{1,0:T(8,128)S(1)}, f32[72,128]{1,0:T(8,128)S(1)}, u32[]{:S(2)}, u32[]{:S(2)}) %collective-permute-start.9) | collective-permute-done | bytes 36896 | tf_op jit(solution)/shard_map/ppermute | solution.py:271
  42.8 1.9 %collective-permute-start.12 = (f32[72,128]{1,0:T(8,128)S(1)}, f32[72,128]{1,0:T(8,128)S(1)}, u32[]{:S(2)}, u32[]{:S(2)}) collective-permute-start(f32[72,128]{1,0:T(8,128)S(1)} %fusion.2), channel_id=1, source_target_pairs={{0,17},{1,16},{2,19},{3,18},{4,21},{5,20},{6,23},{7,22},{8,25},{9,... | collective-permute-start | bytes 110600 | tf_op jit(solution)/shard_map/ppermute | solution.py:271
  44.6 2.2 %collective-permute-start.13 = (f32[72,128]{1,0:T(8,128)S(1)}, f32[72,128]{1,0:T(8,128)S(1)}, u32[]{:S(2)}, u32[]{:S(2)}) collective-permute-start(f32[72,128]{1,0:T(8,128)S(1)} %fusion.2), channel_id=1, source_target_pairs={{0,25},{1,24},{2,27},{3,26},{4,29},{5,28},{6,31},{7,30},{8,17},{9,... | collective-permute-start | bytes 110600 | tf_op jit(solution)/shard_map/ppermute | solution.py:271
  46.8 0.6 %convert_reduce_fusion = f32[]{:T(128)} fusion(s32[128]{0:T(128)S(1)} %copy-done.8), kind=kLoop, calls=%fused_computation.37 | loop fusion | flops 255 | bytes 516 | tf_op jit(solution)/shard_map/reduce_sum | solution.py:435
  48.1 1.7 %collective-permute-done.13 = f32[72,128]{1,0:T(8,128)S(1)} collective-permute-done((f32[72,128]{1,0:T(8,128)S(1)}, f32[72,128]{1,0:T(8,128)S(1)}, u32[]{:S(2)}, u32[]{:S(2)}) %collective-permute-start.13) | collective-permute-done | bytes 36896 | tf_op jit(solution)/shard_map/ppermute | solution.py:271
  49.9 0.6 %collective-permute-start.14 = (f32[64,128]{1,0:T(8,128)S(1)}, f32[64,128]{1,0:T(8,128)S(1)}, u32[]{:S(2)}, u32[]{:S(2)}) collective-permute-start(f32[64,128]{1,0:T(8,128)S(1)} %slice_multiply_fusion), channel_id=1, source_target_pairs={{0,2},{1,3},{2,0},{3,1},{4,6},{5,7},{6,4},{7,5},{8,10},{9,11},{10,... | collective-permute-start | bytes 98312 | tf_op jit(solution)/shard_map/ppermute | solution.py:271
  50.5 0.7 %collective-permute-start.15 = (f32[64,128]{1,0:T(8,128)S(1)}, f32[64,128]{1,0:T(8,128)S(1)}, u32[]{:S(2)}, u32[]{:S(2)}) collective-permute-start(f32[64,128]{1,0:T(8,128)S(1)} %slice_multiply_fusion), channel_id=1, source_target_pairs={{0,5},{1,4},{2,7},{3,6},{4,1},{5,0},{6,3},{7,2},{8,13},{9,12},{10,... | collective-permute-start | bytes 98312 | tf_op jit(solution)/shard_map/ppermute | solution.py:271
  51.2 2.0 %collective-permute-start.16 = (f32[64,128]{1,0:T(8,128)S(1)}, f32[64,128]{1,0:T(8,128)S(1)}, u32[]{:S(2)}, u32[]{:S(2)}) collective-permute-start(f32[64,128]{1,0:T(8,128)S(1)} %slice_multiply_fusion), channel_id=1, source_target_pairs={{0,7},{1,6},{2,5},{3,4},{4,3},{5,2},{6,1},{7,0},{8,15},{9,14},{10,... | collective-permute-start | bytes 98312 | tf_op jit(solution)/shard_map/ppermute | solution.py:271
  53.2 0.7 %collective-permute-done.14 = f32[64,128]{1,0:T(8,128)S(1)} collective-permute-done((f32[64,128]{1,0:T(8,128)S(1)}, f32[64,128]{1,0:T(8,128)S(1)}, u32[]{:S(2)}, u32[]{:S(2)}) %collective-permute-start.14) | collective-permute-done | bytes 32800 | tf_op jit(solution)/shard_map/ppermute | solution.py:271
  53.9 1.5 %collective-permute-done.16 = f32[64,128]{1,0:T(8,128)S(1)} collective-permute-done((f32[64,128]{1,0:T(8,128)S(1)}, f32[64,128]{1,0:T(8,128)S(1)}, u32[]{:S(2)}, u32[]{:S(2)}) %collective-permute-start.16) | collective-permute-done | bytes 32800 | tf_op jit(solution)/shard_map/ppermute | solution.py:271
  55.5 0.7 %collective-permute-start.17 = (f32[256,128]{1,0:T(8,128)S(1)}, f32[256,128]{1,0:T(8,128)S(1)}, u32[]{:S(2)}, u32[]{:S(2)}) collective-permute-start(f32[256,128]{1,0:T(8,128)S(1)} %pad_maximum_fusion.3), channel_id=1, source_target_pairs={{0,1},{1,0},{2,3},{3,2},{4,5},{5,4},{6,7},{7,6},{8,9},{9,8},{10,11... | collective-permute-start | bytes 393224 | tf_op jit(solution)/shard_map/ppermute | solution.py:271
  56.2 0.6 %fusion.8 = f32[]{:T(128)} fusion(f32[128]{0:T(128)S(1)} %get-tuple-element.54, f32[72,128]{1,0:T(8,128)S(1)} %add_add_fusion), kind=kLoop, calls=%fused_computation.36 | loop fusion | flops 255 | bytes 1028 | tf_op jit(solution)/shard_map/reduce_sum | solution.py:472
  57.2 0.7 %pad_maximum_fusion = f32[512,128]{1,0:T(8,128)} fusion(f32[256,128]{1,0:T(8,128)S(1)} %get-tuple-element.56, f32[256,128]{1,0:T(8,128)S(1)} %get-tuple-element.55), kind=kLoop, calls=%fused_computation | loop fusion | flops 65536 | bytes 524288 | tf_op jit(solution)/shard_map/concatenate | solution.py:471
  (50 shorter events, 1.6 us)
Async XLA Ops:
  0.6 2.2 %copy-start.3 = (s32[32,8]{0,1:T(8,128)S(1)}, s32[32,8]{0,1:T(8,128)}, u32[]{:S(2)}) copy-start(s32[32,8]{0,1:T(8,128)} %param.21) | copy-start | bytes 3076
  0.6 2.2 %copy-start.4 = (f32[32,8]{0,1:T(8,128)S(1)}, f32[32,8]{0,1:T(8,128)}, u32[]{:S(2)}) copy-start(f32[32,8]{0,1:T(8,128)} %param.22) | copy-start | bytes 3076
  0.7 2.2 %copy-start.5 = (s32[32,6]{0,1:T(8,128)S(1)}, s32[32,6]{0,1:T(8,128)}, u32[]{:S(2)}) copy-start(s32[32,6]{0,1:T(8,128)} %param.23) | copy-start | bytes 2308
  0.7 15.6 %copy-start.6 = (s32[256,4]{0,1:T(4,128)S(1)}, s32[256,4]{0,1:T(4,128)}, u32[]{:S(2)}) copy-start(s32[256,4]{0,1:T(4,128)} %param.24) | copy-start | bytes 12292
  0.7 15.6 %copy-start.7 = (f32[256,4]{0,1:T(4,128)S(1)}, f32[256,4]{0,1:T(4,128)}, u32[]{:S(2)}) copy-start(f32[256,4]{0,1:T(4,128)} %param.25) | copy-start | bytes 12292
  0.7 15.6 %copy-start = (f32[512,512]{1,0:T(8,128)S(1)}, f32[512,512]{1,0:T(8,128)}, u32[]{:S(2)}) copy-start(f32[512,512]{1,0:T(8,128)} %wd_hbm.1) | copy-start | bytes 3145732
  0.7 15.6 %copy-start.1 = (f32[512,128]{1,0:T(8,128)S(1)}, f32[512,128]{1,0:T(8,128)}, u32[]{:S(2)}) copy-start(f32[512,128]{1,0:T(8,128)} %wo_hbm.1) | copy-start | bytes 786436
  2.9 5.2 %collective-permute-start = (f32[1,8,1152]{2,1,0:T(8,128)S(1)}, f32[1,8,1152]{2,1,0:T(8,128)S(1)}, u32[]{:S(2)}, u32[]{:S(2)}) collective-permute-start(f32[1,8,1152]{2,1,0:T(8,128)S(1)} %bitcast.40), channel_id=1, source_target_pairs={{0,8},{1,9},{2,10},{3,11},{4,12},{5,13},{6,14},{7,15},{8,0},{9,1},... | collective-permute-start | bytes 110600 | tf_op jit(solution)/shard_map/ppermute | solution.py:271
  6.0 4.4 %collective-permute-start.1 = (f32[1,8,1152]{2,1,0:T(8,128)S(1)}, f32[1,8,1152]{2,1,0:T(8,128)S(1)}, u32[]{:S(2)}, u32[]{:S(2)}) collective-permute-start(f32[1,8,1152]{2,1,0:T(8,128)S(1)} %bitcast.41), channel_id=1, source_target_pairs={{0,17},{1,16},{2,19},{3,18},{4,21},{5,20},{6,23},{7,22},{8,25},{9,... | collective-permute-start | bytes 110600 | tf_op jit(solution)/shard_map/ppermute | solution.py:271
  7.7 5.2 %collective-permute-start.2 = (f32[1,8,1152]{2,1,0:T(8,128)S(1)}, f32[1,8,1152]{2,1,0:T(8,128)S(1)}, u32[]{:S(2)}, u32[]{:S(2)}) collective-permute-start(f32[1,8,1152]{2,1,0:T(8,128)S(1)} %bitcast.42), channel_id=1, source_target_pairs={{0,25},{1,24},{2,27},{3,26},{4,29},{5,28},{6,31},{7,30},{8,17},{9,... | collective-permute-start | bytes 110600 | tf_op jit(solution)/shard_map/ppermute | solution.py:271
  12.9 6.8 %collective-permute-start.3 = (f32[4,8,1152]{2,1,0:T(8,128)S(1)}, f32[4,8,1152]{2,1,0:T(8,128)S(1)}, u32[]{:S(2)}, u32[]{:S(2)}) collective-permute-start(f32[4,8,1152]{2,1,0:T(8,128)S(1)} %pad_maximum_fusion.1), channel_id=1, source_target_pairs={{0,2},{1,3},{2,0},{3,1},{4,6},{5,7},{6,4},{7,5},{8,10},{9,11},{10,... | collective-permute-start | bytes 442376 | tf_op jit(solution)/shard_map/ppermute | solution.py:271
  14.5 8.3 %collective-permute-start.4 = (f32[4,8,1152]{2,1,0:T(8,128)S(1)}, f32[4,8,1152]{2,1,0:T(8,128)S(1)}, u32[]{:S(2)}, u32[]{:S(2)}) collective-permute-start(f32[4,8,1152]{2,1,0:T(8,128)S(1)} %pad_maximum_fusion.1), channel_id=1, source_target_pairs={{0,5},{1,4},{2,7},{3,6},{4,1},{5,0},{6,3},{7,2},{8,13},{9,12},{10,... | collective-permute-start | bytes 442376 | tf_op jit(solution)/shard_map/ppermute | solution.py:271
  16.3 7.6 %collective-permute-start.5 = (f32[4,8,1152]{2,1,0:T(8,128)S(1)}, f32[4,8,1152]{2,1,0:T(8,128)S(1)}, u32[]{:S(2)}, u32[]{:S(2)}) collective-permute-start(f32[4,8,1152]{2,1,0:T(8,128)S(1)} %pad_maximum_fusion.1), channel_id=1, source_target_pairs={{0,7},{1,6},{2,5},{3,4},{4,3},{5,2},{6,1},{7,0},{8,15},{9,14},{10,... | collective-permute-start | bytes 442376 | tf_op jit(solution)/shard_map/ppermute | solution.py:271
  16.3 9.6 %copy-start.2 = (f32[256,128]{1,0:T(8,128)S(1)}, f32[256,128]{1,0:T(8,128)}, u32[]{:S(2)}) copy-start(f32[256,128]{1,0:T(8,128)} %refs_11_.1) | copy-start | bytes 393220
  23.9 2.1 %collective-permute-start.6 = (f32[16,8,1152]{2,1,0:T(8,128)S(1)}, f32[16,8,1152]{2,1,0:T(8,128)S(1)}, u32[]{:S(2)}, u32[]{:S(2)}) collective-permute-start(f32[16,8,1152]{2,1,0:T(8,128)S(1)} %constant_dynamic-update-slice_fusion.refs_0_), channel_id=1, source_target_pairs={{0,1},{1,0},{2,3},{3,2},{4,5},{5,4},{6,7},{7,6},{8,9},{9,8},{10,11... | collective-permute-start | bytes 1769480 | tf_op jit(solution)/shard_map/ppermute | solution.py:271
  26.0 20.9 %copy-start.8 = (s32[128]{0:T(128)S(1)}, s32[128]{0:T(128)}, u32[]{:S(2)}) copy-start(s32[128]{0:T(128)} %param.20) | copy-start | bytes 1540
  35.0 1.4 %collective-permute-start.7 = (f32[264,128]{1,0:T(8,128)S(1)}, f32[264,128]{1,0:T(8,128)S(1)}, u32[]{:S(2)}, u32[]{:S(2)}) collective-permute-start(f32[264,128]{1,0:T(8,128)S(1)} %get-tuple-element.52), channel_id=1, source_target_pairs={{0,1},{1,0},{2,3},{3,2},{4,5},{5,4},{6,7},{7,6},{8,9},{9,8},{10,11... | collective-permute-start | bytes 405512 | tf_op jit(solution)/shard_map/ppermute | solution.py:271
  36.5 4.4 %collective-permute-start.10 = (f32[72,128]{1,0:T(8,128)S(1)}, f32[72,128]{1,0:T(8,128)S(1)}, u32[]{:S(2)}, u32[]{:S(2)}) collective-permute-start(f32[72,128]{1,0:T(8,128)S(1)} %get-tuple-element.67), channel_id=1, source_target_pairs={{0,7},{1,6},{2,5},{3,4},{4,3},{5,2},{6,1},{7,0},{8,15},{9,14},{10,... | collective-permute-start | bytes 110600 | tf_op jit(solution)/shard_map/ppermute | solution.py:271
  37.7 4.0 %collective-permute-start.8 = (f32[72,128]{1,0:T(8,128)S(1)}, f32[72,128]{1,0:T(8,128)S(1)}, u32[]{:S(2)}, u32[]{:S(2)}) collective-permute-start(f32[72,128]{1,0:T(8,128)S(1)} %get-tuple-element.65), channel_id=1, source_target_pairs={{0,2},{1,3},{2,0},{3,1},{4,6},{5,7},{6,4},{7,5},{8,10},{9,11},{10,... | collective-permute-start | bytes 110600 | tf_op jit(solution)/shard_map/ppermute | solution.py:271
  38.9 3.7 %collective-permute-start.9 = (f32[72,128]{1,0:T(8,128)S(1)}, f32[72,128]{1,0:T(8,128)S(1)}, u32[]{:S(2)}, u32[]{:S(2)}) collective-permute-start(f32[72,128]{1,0:T(8,128)S(1)} %get-tuple-element.66), channel_id=1, source_target_pairs={{0,5},{1,4},{2,7},{3,6},{4,1},{5,0},{6,3},{7,2},{8,13},{9,12},{10,... | collective-permute-start | bytes 110600 | tf_op jit(solution)/shard_map/ppermute | solution.py:271
  42.7 5.4 %collective-permute-start.11 = (f32[72,128]{1,0:T(8,128)S(1)}, f32[72,128]{1,0:T(8,128)S(1)}, u32[]{:S(2)}, u32[]{:S(2)}) collective-permute-start(f32[72,128]{1,0:T(8,128)S(1)} %fusion.2), channel_id=1, source_target_pairs={{0,8},{1,9},{2,10},{3,11},{4,12},{5,13},{6,14},{7,15},{8,0},{9,1},... | collective-permute-start | bytes 110600 | tf_op jit(solution)/shard_map/ppermute | solution.py:271
  42.8 5.4 %collective-permute-start.12 = (f32[72,128]{1,0:T(8,128)S(1)}, f32[72,128]{1,0:T(8,128)S(1)}, u32[]{:S(2)}, u32[]{:S(2)}) collective-permute-start(f32[72,128]{1,0:T(8,128)S(1)} %fusion.2), channel_id=1, source_target_pairs={{0,17},{1,16},{2,19},{3,18},{4,21},{5,20},{6,23},{7,22},{8,25},{9,... | collective-permute-start | bytes 110600 | tf_op jit(solution)/shard_map/ppermute | solution.py:271
  44.6 5.2 %collective-permute-start.13 = (f32[72,128]{1,0:T(8,128)S(1)}, f32[72,128]{1,0:T(8,128)S(1)}, u32[]{:S(2)}, u32[]{:S(2)}) collective-permute-start(f32[72,128]{1,0:T(8,128)S(1)} %fusion.2), channel_id=1, source_target_pairs={{0,25},{1,24},{2,27},{3,26},{4,29},{5,28},{6,31},{7,30},{8,17},{9,... | collective-permute-start | bytes 110600 | tf_op jit(solution)/shard_map/ppermute | solution.py:271
  49.9 4.0 %collective-permute-start.14 = (f32[64,128]{1,0:T(8,128)S(1)}, f32[64,128]{1,0:T(8,128)S(1)}, u32[]{:S(2)}, u32[]{:S(2)}) collective-permute-start(f32[64,128]{1,0:T(8,128)S(1)} %slice_multiply_fusion), channel_id=1, source_target_pairs={{0,2},{1,3},{2,0},{3,1},{4,6},{5,7},{6,4},{7,5},{8,10},{9,11},{10,... | collective-permute-start | bytes 98312 | tf_op jit(solution)/shard_map/ppermute | solution.py:271
  50.5 3.4 %collective-permute-start.15 = (f32[64,128]{1,0:T(8,128)S(1)}, f32[64,128]{1,0:T(8,128)S(1)}, u32[]{:S(2)}, u32[]{:S(2)}) collective-permute-start(f32[64,128]{1,0:T(8,128)S(1)} %slice_multiply_fusion), channel_id=1, source_target_pairs={{0,5},{1,4},{2,7},{3,6},{4,1},{5,0},{6,3},{7,2},{8,13},{9,12},{10,... | collective-permute-start | bytes 98312 | tf_op jit(solution)/shard_map/ppermute | solution.py:271
  51.2 4.2 %collective-permute-start.16 = (f32[64,128]{1,0:T(8,128)S(1)}, f32[64,128]{1,0:T(8,128)S(1)}, u32[]{:S(2)}, u32[]{:S(2)}) collective-permute-start(f32[64,128]{1,0:T(8,128)S(1)} %slice_multiply_fusion), channel_id=1, source_target_pairs={{0,7},{1,6},{2,5},{3,4},{4,3},{5,2},{6,1},{7,0},{8,15},{9,14},{10,... | collective-permute-start | bytes 98312 | tf_op jit(solution)/shard_map/ppermute | solution.py:271
  55.5 1.7 %collective-permute-start.17 = (f32[256,128]{1,0:T(8,128)S(1)}, f32[256,128]{1,0:T(8,128)S(1)}, u32[]{:S(2)}, u32[]{:S(2)}) collective-permute-start(f32[256,128]{1,0:T(8,128)S(1)} %pad_maximum_fusion.3), channel_id=1, source_target_pairs={{0,1},{1,0},{2,3},{3,2},{4,5},{5,4},{6,7},{7,6},{8,9},{9,8},{10,11... | collective-permute-start | bytes 393224 | tf_op jit(solution)/shard_map/ppermute | solution.py:271
